TPU v7x, 32 devices: a whole 2x2x4 slice. The times are simulated.
32 devices in a mesh: dp: 4 (over z), ctx: 4 (over y, x), mp: 2 (over core).
Axes of the slice: x: 2, y: 2, z: 4, core: 2. Of those that a mesh axis runs over, the one named last changes fastest.
Arguments:
- llm_grad: bfloat16 [2048, 4096], P(('dp', 'ctx')), may hold values from -6 to 6
- merger_pre: bfloat16 [768, 5120], P(('dp', 'ctx', 'mp')), may hold values from -6 to 6
- out_weight: bfloat16 [5120, 4096], P(('ctx', 'mp')), may hold values from -0.078125 to 0.078125
- patch_counts: int32 [4, 8, 4], P('dp'), may hold values from 1 to 12, 24 in all within a row
- image_order: int32 [4, 32], P('dp'), may hold values from 0 to 31, each once within a row
- vision_rows: int32 [4, 4, 48], P('dp'), may hold values from 0 to 127, as said below
Outputs:
- merger_pre_grad: bfloat16 [768, 5120], P(('dp', 'ctx', 'mp'))
- weight_grad: float32 [5120, 4096], P(('ctx', 'mp'), 'dp')
- bias_grad: float32 [4096], P('dp')
Inputs may be any that keep to these rules, and one draw needn't show every extreme that they name: `patch_counts`: each row of 4 counts sums to 24. `image_order`: each row is a permutation of the group's images. `vision_rows`: each row holds 48 distinct increasing positions, the first and last row of the shard among them.
All inputs are finite; a program needn't handle non-finite values.
Results may differ from a plain program's by a relative error of at most 0.003.
Values may be sent and summed in bfloat16 or wider, within the bound.
No kernel may reach another device: no remote copies, remote signals or barrier semaphores. Data moves between devices by JAX's collectives and lax.ppermute only.
A program may use at most 64 MiB of HBM per device.

v0:
```python
import jax
import jax.numpy as jnp
from jax import lax
from jax.sharding import PartitionSpec as P


def gelu_parts(x):
    cdf = 0.5 * (1.0 + lax.erf(x * 0.7071067811865476))
    pdf = jnp.exp(-0.5 * x * x) * 0.3989422804014327
    return (x * cdf, cdf + x * pdf)


def stream_rows(counts, order, length):
    total = counts.shape[0]
    vit_end = jnp.cumsum(counts)
    vit_start = vit_end - counts
    onehot = (order[:, None] == jnp.arange(total, dtype=jnp.int32)[None, :]).astype(jnp.int32)
    ordered = jnp.sum(onehot * counts[None, :], axis=1)
    place_start = jnp.cumsum(ordered) - ordered
    llm_start = jnp.sum(onehot * place_start[:, None], axis=0)
    shift = llm_start - vit_start
    rows = jnp.arange(length, dtype=jnp.int32)
    member = (rows[:, None] >= vit_start[None, :]) & (rows[:, None] < vit_end[None, :])
    return rows + jnp.sum(jnp.where(member, shift[None, :], 0), axis=1)


def per_device(llm_grad, merger_pre, out_weight, patch_counts, image_order, vision_rows):
    group_rows = merger_pre.shape[0] * lax.axis_size(("ctx", "mp"))
    stream = stream_rows(patch_counts.reshape(-1), image_order.reshape(-1), group_rows)
    own_places = vision_rows[0][lax.axis_index("ctx")]
    own_rows = llm_grad[own_places]
    stream_grad = lax.all_gather(own_rows, "ctx", axis=0, tiled=True)
    pre_cols = lax.all_to_all(merger_pre, ("ctx", "mp"), split_axis=1, concat_axis=0, tiled=True)
    row_grad = stream_grad[stream]
    value, slope = gelu_parts(pre_cols.astype(jnp.float32))
    act = value.astype(jnp.bfloat16)
    act_grad = lax.dot_general(
        row_grad, out_weight, (((1,), (1,)), ((), ())), preferred_element_type=jnp.float32
    )
    pre_grad = (act_grad * slope).astype(jnp.bfloat16)
    returned = lax.all_to_all(pre_grad, ("ctx", "mp"), split_axis=0, concat_axis=1, tiled=True)
    term = lax.dot_general(
        act, row_grad, (((0,), (0,)), ((), ())), preferred_element_type=jnp.float32
    )
    ones_row = jnp.ones((row_grad.shape[0],), jnp.bfloat16)
    bias_term = jnp.dot(ones_row, row_grad, preferred_element_type=jnp.float32)
    weight_grad, bias_grad = (
        lax.psum_scatter(term, "dp", scatter_dimension=1, tiled=True),
        lax.psum_scatter(bias_term, "dp", scatter_dimension=0, tiled=True),
    )
    return (returned, weight_grad, bias_grad)


def solution(mesh):
    placed = (
        P(("dp", "ctx"), None),
        P(("dp", "ctx", "mp"), None),
        P(("ctx", "mp"), None),
        P("dp", None, None),
        P("dp", None),
        P("dp", None, None),
    )
    return jax.shard_map(
        per_device,
        mesh=mesh,
        in_specs=placed,
        out_specs=(P(("dp", "ctx", "mp"), None), P(("ctx", "mp"), "dp"), P("dp")),
        check_vma=False,
    )
```

profile of v0, /device:TPU:0, one launch (start us, length us, event | category | flops | bytes accessed | tf_op | source)
XLA Modules:
  0.0 239.9 jit_solution(6637029986367791760)
XLA Ops:
  7.2 0.0 copy-start
  7.2 0.0 all-gather.3.cloned.1.call-start
  7.2 0.8 fusion.10
  8.0 0.4 copy-done
  8.4 0.0 copy-start.2
  8.4 0.0 copy-start.3
  8.4 0.0 copy-start.4
  8.4 1.5 gather_fusion
  10.0 0.0 all-gather.3.cloned.1.call-update
  10.0 0.0 copy-done.2
  10.0 0.7 copy.36
  10.7 5.2 %all-to-all-start = ((bf16[24,8,640]{2,0,1:T(8,128)(2,1)}), bf16[24,8,640]{2,0,1:T(8,128)(2,1)S(1)}, u32[]{:S(2)}, u32[]{:S(2)}) async-start(bf16[24,8,640]{2,0,1:T(8,128)(2,1)} %bitcast.36), calls=%async_computation | async-start | bytes 491520 | tf_op jit(solution)/shard_map/all_to_all | solution.py:33
  15.9 0.0 reduce-scatter.2.cloned.1.call-start
  15.9 0.0 copy-done.3
  15.9 0.1 copy.27
  16.0 0.1 reshape.134
  16.1 0.1 reshape.157
  16.2 0.1 reduce-window.15
  16.2 0.1 reduce
  16.3 0.0 copy-done.4
  16.3 0.2 select_reduce_fusion.2
  16.5 0.1 copy.30
  16.6 0.1 reduce-window.16
  16.7 0.1 reduce.1
  16.8 0.1 select_reduce_fusion.1
  16.9 0.1 select_reduce_fusion
  17.0 5.6 %all-to-all-done = bf16[24,8,640]{2,0,1:T(8,128)(2,1)S(1)} async-done(((bf16[24,8,640]{2,0,1:T(8,128)(2,1)}), bf16[24,8,640]{2,0,1:T(8,128)(2,1)S(1)}, u32[]{:S(2)}, u32[]{:S(2)}) %all-to-all-start) | async-done | bytes 245792 | tf_op jit(solution)/shard_map/all_to_all | solution.py:33
  22.6 0.9 fusion.8
  23.6 20.6 %all-gather.3.cloned.1.call-done = bf16[192,4096]{1,0:T(8,128)(2,1)} async-done(((bf16[48,4096]{1,0:T(8,128)(2,1)}), bf16[192,4096]{1,0:T(8,128)(2,1)}) %all-gather.3.cloned.1.call-update) | async-done | bytes 1572880 | tf_op jit(solution)/shard_map/all_gather | solution.py:32
  44.1 4.7 %gather_fusion.1 = bf16[192,4096]{1,0:T(8,128)(2,1)S(1)} fusion(bf16[192,4096]{1,0:T(8,128)(2,1)} %all-gather.3.cloned.1.call-done, s32[1024]{0:T(1024)S(1)} %pad_clamp_fusion), kind=kCustom, calls=%fused_computation.1 | custom fusion | bytes 3146496 | tf_op jit(solution)/shard_map/gather | solution.py:34
  48.8 5.6 %fusion.16 = f32[640,4096]{1,0:T(8,128)} fusion(bf16[192,640]{1,0:T(8,128)(2,1)S(1)} %get-tuple-element.3, bf16[192,4096]{1,0:T(8,128)(2,1)S(1)} %gather_fusion.1), kind=kOutput, calls=%fused_computation.32 | convolution fusion | flops 1006632960 | bytes 12304384 | tf_op jit(solution)/shard_map/dot_general | solution.py:42
  54.4 0.0 copy-start.5
  54.4 0.0 copy-start.1
  54.4 0.0 reduce-scatter.2.cloned.1.call-update
  54.4 0.6 copy-done.5
  55.0 0.6 dynamic-slice.1
  56.3 0.0 copy-done.1
  56.3 5.1 %fusion = bf16[192,640]{1,0:T(8,128)(2,1)} fusion(bf16[192,4096]{1,0:T(8,128)(2,1)S(1)} %gather_fusion.1, bf16[640,4096]{1,0:T(8,128)(2,1)} %param.8, f32[192,640]{1,0:T(8,128)S(1)} %copy-done.1, f32[192,640]{1,0:T(8,128)S(1)} %bitcast.38), kind=kOutput, calls=%fused_computation.3 | convolution fusion | flops 1007493120 | bytes 8044544 | tf_op jit(solution)/shard_map/dot_general | solution.py:37
  61.4 3.4 %all-to-all-start.1 = ((bf16[8,24,640]{2,1,0:T(8,128)(2,1)}), bf16[8,24,640]{2,1,0:T(8,128)(2,1)S(1)}, u32[]{:S(2)}, u32[]{:S(2)}) async-start(bf16[8,24,640]{2,1,0:T(8,128)(2,1)} %bitcast.40), calls=%async_computation.1 | async-start | bytes 491520 | tf_op jit(solution)/shard_map/all_to_all | solution.py:41
  64.8 0.3 fusion.11
  65.1 19.4 %all-reduce = f32[4096]{0:T(1024)S(1)} all-reduce(f32[4096]{0:T(1024)S(1)} %bitcast.42), channel_id=4, replica_groups=mesh['dp'=4,'ctx'=4,'mp'=2] {'dp'}, use_global_device_ids=true, to_apply=%region_6.7.clone | all-reduce | flops 4096 | bytes 32768
  84.5 0.6 dynamic-slice.2
  85.1 0.0 all-to-all-done.1
  85.1 0.7 copy.34
  85.8 147.3 %reduce-scatter.2.cloned.1.call-done = f32[640,1024]{1,0:T(8,128)} async-done(((f32[640,4096]{1,0:T(8,128)}), f32[640,1024]{1,0:T(8,128)}) %reduce-scatter.2.cloned.1.call-update) | async-done | bytes 2621456 | tf_op jit(solution)/shard_map/reduce_scatter | solution.py:48
  (6 shorter events, 0.1 us)
Async XLA Ops:
  7.2 1.2 copy-start
  7.2 37.0 %all-gather.3.cloned.1.call-start = ((), (), s32[]{:S(2)}) async-start(), calls=%async_computation.4 | async-start | bytes 1966080 | tf_op jit(solution)/shard_map/all_gather | solution.py:32
  8.4 1.6 copy-start.2
  8.4 7.5 %copy-start.3 = (s32[1,8,4]{1,2,0:T(4,128)S(1)}, s32[1,8,4]{1,2,0:T(4,128)}, u32[]{:S(2)}) copy-start(s32[1,8,4]{1,2,0:T(4,128)} %param.9) | copy-start | bytes 388
  8.4 7.9 %copy-start.4 = (s32[1,32]{1,0:T(1,128)S(1)}, s32[1,32]{1,0:T(1,128)}, u32[]{:S(2)}) copy-start(s32[1,32]{1,0:T(1,128)} %param.10) | copy-start | bytes 388
  10.7 11.9 %all-to-all-start = ((bf16[24,8,640]{2,0,1:T(8,128)(2,1)}), bf16[24,8,640]{2,0,1:T(8,128)(2,1)S(1)}, u32[]{:S(2)}, u32[]{:S(2)}) async-start(bf16[24,8,640]{2,0,1:T(8,128)(2,1)} %bitcast.36), calls=%async_computation | async-start | bytes 491520 | tf_op jit(solution)/shard_map/all_to_all | solution.py:33
  15.9 217.2 %reduce-scatter.2.cloned.1.call-start = ((), (), s32[]{:S(2)}) async-start(), calls=%async_computation.3 | async-start | bytes 13107200 | tf_op jit(solution)/shard_map/reduce_scatter | solution.py:48
  54.4 0.7 copy-start.5
  54.4 1.9 copy-start.1
  61.4 23.7 %all-to-all-start.1 = ((bf16[8,24,640]{2,1,0:T(8,128)(2,1)}), bf16[8,24,640]{2,1,0:T(8,128)(2,1)S(1)}, u32[]{:S(2)}, u32[]{:S(2)}) async-start(bf16[8,24,640]{2,1,0:T(8,128)(2,1)} %bitcast.40), calls=%async_computation.1 | async-start | bytes 491520 | tf_op jit(solution)/shard_map/all_to_all | solution.py:41
Sparse Core Ops, SparseCore 0:
  10.4 33.6 all-gather.2
  54.5 178.5 reduce-scatter.1
where the time goes:
time: 240 us
  waiting for transfers between devices  173 us (72%)
  blocking collectives  19.4 us (8%)
  between operations  14.8 us (6%)
  matrix products  10.9 us (5%)
  local copies, waits for them, and re-layouts  10.2 us (4%)
  starting transfers between devices  8.65 us (4%)
  other arithmetic  2.48 us (1%)
    reduce_scatter x1, waiting for transfers between devices, per_device(): lax.psum_scatter(term, 'dp', scatter_dimension=1, tiled=True)  147 us
    all_gather x1, waiting for transfers between devices, per_device(): stream_grad = lax.all_gather(own_rows, 'ctx', axis=0, tiled=True)  20.6 us
    unnamed x1, blocking collectives  19.4 us
    all_to_all x1, waiting for transfers between devices, per_device(): lax.all_to_all(merger_pre, ('ctx', 'mp'), split_axis=1, concat_axis=0, ti...  5.6 us
    dot_general x1, matrix products, per_device(): lax.dot_general(act, row_grad, (((0,), (0,)), ((), ())), preferred_elemen...  5.56 us
    all_to_all x1, starting transfers between devices, per_device(): lax.all_to_all(merger_pre, ('ctx', 'mp'), split_axis=1, concat_axis=0, ti...  5.17 us
    dot_general x1, matrix products, per_device(): lax.dot_general(row_grad, out_weight, (((1,), (1,)), ((), ())), preferred...  5.07 us
  transfers between devices with their start and end apart: 4, of which 3 were waited for; matrix products, arithmetic and copies ran while one was open for 4% of the time, Pallas kernels for 0%

commit v1 on v0

v1 whole, which is shorter than its diff:
```python
import functools

import jax
import jax.numpy as jnp
from jax import lax
from jax.experimental import pallas as pl
from jax.experimental.pallas import tpu as pltpu
from jax.sharding import PartitionSpec as P

BF16 = jnp.bfloat16
F32 = jnp.float32
VMEM = pl.BlockSpec(memory_space=pltpu.VMEM)
ANY = pl.BlockSpec(memory_space=pl.ANY)


def gelu_parts(x):
    cdf = 0.5 * (1.0 + lax.erf(x * 0.7071067811865476))
    pdf = jnp.exp(-0.5 * x * x) * 0.3989422804014327
    return (x * cdf, cdf + x * pdf)


def stream_rows(counts, order, length):
    total = counts.shape[0]
    vit_end = jnp.cumsum(counts)
    vit_start = vit_end - counts
    onehot = (order[:, None] == jnp.arange(total, dtype=jnp.int32)[None, :]).astype(jnp.int32)
    ordered = jnp.sum(onehot * counts[None, :], axis=1)
    place_start = jnp.cumsum(ordered) - ordered
    llm_start = jnp.sum(onehot * place_start[:, None], axis=0)
    shift = llm_start - vit_start
    rows = jnp.arange(length, dtype=jnp.int32)
    member = (rows[:, None] >= vit_start[None, :]) & (rows[:, None] < vit_end[None, :])
    return rows + jnp.sum(jnp.where(member, shift[None, :], 0), axis=1)


def reduced(llm_grad, merger_pre, out_weight, patch_counts, image_order, vision_rows):
    group_rows = merger_pre.shape[0] * lax.axis_size(("ctx", "mp"))
    stream = stream_rows(patch_counts.reshape(-1), image_order.reshape(-1), group_rows)
    own_places = vision_rows[0][lax.axis_index("ctx")]
    own_rows = llm_grad[own_places]
    stream_grad = lax.all_gather(own_rows, "ctx", axis=0, tiled=True)
    pre_cols = lax.all_to_all(merger_pre, ("ctx", "mp"), split_axis=1, concat_axis=0, tiled=True)
    row_grad = stream_grad[stream]
    value, slope = gelu_parts(pre_cols.astype(F32))
    act = value.astype(BF16)
    act_grad = lax.dot_general(row_grad, out_weight, (((1,), (1,)), ((), ())), preferred_element_type=F32)
    pre_grad = (act_grad * slope).astype(BF16)
    returned = lax.all_to_all(pre_grad, ("ctx", "mp"), split_axis=0, concat_axis=1, tiled=True)
    term = lax.dot_general(act, row_grad, (((0,), (0,)), ((), ())), preferred_element_type=F32)
    ones_row = jnp.ones((row_grad.shape[0],), BF16)
    bias_term = jnp.dot(ones_row, row_grad, preferred_element_type=F32)
    return (
        returned,
        lax.psum_scatter(term, "dp", scatter_dimension=1, tiled=True),
        lax.psum_scatter(bias_term, "dp", scatter_dimension=0, tiled=True),
    )


def pick_kernel(n_dp, ids, llm, places, pre, blocks, mine, other, parts, chosen):
    ctx, core = ids[1], ids[2]
    wide = blocks.shape[2]
    for i in range(blocks.shape[0]):
        blocks[i] = pre[:, i * wide : (i + 1) * wide]
    own = places[0, pl.ds(ctx, 1), :]
    hot = (lax.broadcasted_iota(jnp.int32, (llm.shape[0], own.shape[1]), 0) == own).astype(BF16)
    chosen[...] = lax.dot_general(hot, llm[...], (((0,), (0,)), ((), ())), preferred_element_type=F32).astype(BF16)
    half = mine.shape[1]
    mine[...] = chosen[:, pl.ds(pl.multiple_of(core * half, half), half)]
    other[...] = chosen[:, pl.ds(pl.multiple_of((1 - core) * half, half), half)]
    part = parts.shape[2]
    for i in range(n_dp):
        parts[i] = chosen[:, pl.ds(pl.multiple_of((2 * i + core) * part, part), part)]


def order_kernel(n_ctx, ids, counts, order, there, back):
    ctx = ids[1]
    images, rows = counts.shape[1], there.shape[0]
    block = rows // n_ctx
    up = lax.broadcasted_iota(jnp.int32, (images, images), 0)
    along = lax.broadcasted_iota(jnp.int32, (images, images), 1)
    count_row, order_row = counts[...], order[...]

    def total(mask, values, axis):
        return jnp.sum(jnp.where(mask, values, 0).astype(F32), axis=axis, keepdims=True).astype(jnp.int32)

    same = up == along
    count_col = total(same, count_row, 1)
    order_col = total(same, order_row, 1)
    vit_start_row = total(up < along, count_col, 0)
    vit_start_col = total(along < up, count_row, 1)
    placed_row = total(order_row == up, count_col, 0)
    placed_col = total(order_col == along, count_row, 1)
    place_start_col = total(along < up, placed_row, 1)
    place_start_row = total(up < along, placed_col, 0)
    llm_start_row = total(order_col == along, place_start_col, 0)
    llm_start_col = total(order_row == up, place_start_row, 1)

    def received(shape, dim):
        at = lax.broadcasted_iota(jnp.int32, shape, dim)
        out = jnp.zeros(shape, jnp.int32)
        for k in range(n_ctx):
            inside = (at >= k * block) & (at < (k + 1) * block)
            out = jnp.where(inside, at + ((ctx ^ k) - k) * block, out)
        return out

    image = lax.broadcasted_iota(jnp.int32, (rows, images), 0)
    member = (image >= vit_start_row) & (image < vit_start_row + count_row)
    stream_col = lax.broadcasted_iota(jnp.int32, (rows, 1), 0) + total(member, llm_start_row - vit_start_row, 1)
    back[...] = (stream_col == received((1, rows), 1)).astype(F32).astype(BF16)
    image = lax.broadcasted_iota(jnp.int32, (images, rows), 1)
    member = (image >= vit_start_col) & (image < vit_start_col + count_col)
    stream_row = lax.broadcasted_iota(jnp.int32, (1, rows), 1) + total(member, llm_start_col - vit_start_col, 0)
    there[...] = (stream_row == received((rows, 1), 0)).astype(F32).astype(BF16)


def act_kernel(there, pre, act, slope):
    x = jnp.dot(there[...], pre[...], preferred_element_type=F32)
    value, grade = gelu_parts(x)
    act[...] = value.astype(BF16)
    slope[...] = grade


def grad_kernel(n_ctx, ids, *refs):
    near, far = refs[:n_ctx], refs[n_ctx : 2 * n_ctx]
    weight, slope, back, out, rows, sems = refs[2 * n_ctx :]
    core = ids[2]
    block, half = near[0].shape

    @pl.when(pl.program_id(0) == 0)
    def _():
        copies = []
        for side, pieces in ((core, near), (1 - core, far)):
            at = pl.ds(pl.multiple_of(side * half, half), half)
            for k in range(n_ctx):
                copies.append(
                    pltpu.make_async_copy(pieces[k], rows.at[k * block : (k + 1) * block, at], sems.at[len(copies)])
                )
        for copy in copies:
            copy.start()
        for copy in copies:
            copy.wait()

    grad = lax.dot_general(rows[...], weight[...], (((1,), (1,)), ((), ())), preferred_element_type=F32)
    grad = (grad * slope[...]).astype(BF16)
    out[...] = jnp.dot(back[...], grad, preferred_element_type=F32).astype(BF16)


def weight_kernel(n_dp, n_ctx, ids, *refs):
    acts, near, far = refs[:n_dp], refs[n_dp : n_dp + n_ctx], refs[n_dp + n_ctx : n_dp + 2 * n_ctx]
    out, bias, left, right, sems = refs[n_dp + 2 * n_ctx :]
    group, core = ids[0], ids[2]
    rows, half = near[0].shape
    block = rows // n_dp

    @pl.when(pl.program_id(0) == 0)
    def _():
        copies = []
        for side, pieces in ((core, near), (1 - core, far)):
            at = pl.ds(pl.multiple_of(side * half, half), half)
            for k in range(n_ctx):
                copies.append(
                    pltpu.make_async_copy(pieces[k], right.at[k * rows : (k + 1) * rows, at], sems.at[len(copies)])
                )
        for j in range(n_dp):
            for k in range(n_ctx):
                to = pl.ds(pl.multiple_of((k * n_dp + (group ^ j)) * block, block), block)
                copies.append(
                    pltpu.make_async_copy(acts[j].at[k * block : (k + 1) * block], left.at[to], sems.at[len(copies)])
                )
        for copy in copies:
            copy.start()
        for copy in copies:
            copy.wait()

    wide = out.shape[1]
    piece = right[:, pl.ds(pl.multiple_of(pl.program_id(0) * wide, wide), wide)]
    out[...] = lax.dot_general(left[...], piece, (((0,), (0,)), ((), ())), preferred_element_type=F32)
    ones = jnp.ones((8, piece.shape[0]), BF16)
    bias[...] = jnp.dot(ones, piece, preferred_element_type=F32)[:1]


def struct(shape, dtype=BF16):
    return jax.ShapeDtypeStruct(shape, dtype)


def swap(x, axis, k):
    n = lax.axis_size(axis)
    return lax.ppermute(x, axis, [(i, i ^ k) for i in range(n)])


def gathered(llm_grad, merger_pre, out_weight, patch_counts, image_order, vision_rows):
    n_dp, n_ctx, n_mp = lax.axis_size("dp"), lax.axis_size("ctx"), lax.axis_size("mp")
    images = n_ctx * n_mp
    vit, hidden = merger_pre.shape
    hid, feat = out_weight.shape
    block = vision_rows.shape[-1]
    rows = n_ctx * block
    cols = feat // n_dp
    ids = jnp.stack([lax.axis_index(a) for a in ("dp", "ctx", "mp")]).astype(jnp.int32)
    smem = pl.BlockSpec(memory_space=pltpu.SMEM)

    blocks, mine, other, parts = pl.pallas_call(
        functools.partial(pick_kernel, n_dp),
        out_shape=(
            struct((images, vit, hid)),
            struct((block, feat // 2)),
            struct((block, feat // 2)),
            struct((n_dp, block, cols // 2)),
        ),
        in_specs=[smem, VMEM, VMEM, VMEM],
        out_specs=(VMEM,) * 4,
        scratch_shapes=[pltpu.VMEM((block, feat), BF16)],
        name="pick",
    )(ids, llm_grad, vision_rows, merger_pre)

    pre = lax.all_to_all(blocks, ("ctx", "mp"), 0, 0, tiled=True).reshape(rows, hid)
    split = lax.all_to_all(parts, "dp", 0, 0, tiled=True).reshape(n_dp * block, cols // 2)
    near = [mine] + [swap(mine, "ctx", k) for k in range(1, n_ctx)]
    far = [other] + [swap(x, "mp", 1) for x in near[1:]]

    there, back = pl.pallas_call(
        functools.partial(order_kernel, n_ctx),
        out_shape=(struct((rows, rows)),) * 2,
        in_specs=[smem, VMEM, VMEM],
        out_specs=(VMEM,) * 2,
        name="order",
    )(ids, patch_counts.reshape(1, -1), image_order)

    act, slope = pl.pallas_call(
        act_kernel,
        out_shape=(struct((rows, hid)), struct((rows, hid), F32)),
        in_specs=[VMEM] * 2,
        out_specs=(VMEM,) * 2,
        name="act",
    )(there, pre)
    acts = [act] + [swap(act, "dp", k) for k in range(1, n_dp)]
    near_part = [split] + [swap(split, "ctx", k) for k in range(1, n_ctx)]
    far_part = [swap(x, "mp", 1) for x in near_part]

    wide = 128
    grad = pl.pallas_call(
        functools.partial(grad_kernel, n_ctx),
        out_shape=struct((rows, hid)),
        grid=(hid // wide,),
        in_specs=[smem]
        + [ANY] * (2 * n_ctx)
        + [
            pl.BlockSpec((wide, feat), lambda i: (i, 0)),
            pl.BlockSpec((rows, wide), lambda i: (0, i)),
            pl.BlockSpec((rows, rows), lambda i: (0, 0)),
        ],
        out_specs=pl.BlockSpec((rows, wide), lambda i: (0, i)),
        scratch_shapes=[pltpu.VMEM((rows, feat), BF16), pltpu.SemaphoreType.DMA((2 * n_ctx,))],
        name="grad",
    )(ids, *near, *far, out_weight, slope, back)
    returned = lax.all_to_all(grad.reshape(images, vit, hid), ("ctx", "mp"), 0, 0, tiled=True)
    returned = jnp.swapaxes(returned, 0, 1).reshape(vit, hidden)

    wide = 256
    weight_grad, bias_grad = pl.pallas_call(
        functools.partial(weight_kernel, n_dp, n_ctx),
        out_shape=(struct((hid, cols), F32), struct((1, cols), F32)),
        grid=(cols // wide,),
        in_specs=[smem] + [ANY] * (n_dp + 2 * n_ctx),
        out_specs=(pl.BlockSpec((hid, wide), lambda i: (0, i)), pl.BlockSpec((1, wide), lambda i: (0, i))),
        scratch_shapes=[
            pltpu.VMEM((n_dp * rows, hid), BF16),
            pltpu.VMEM((n_dp * rows, cols), BF16),
            pltpu.SemaphoreType.DMA((2 * n_ctx + n_dp * n_ctx,)),
        ],
        name="weight",
    )(ids, *acts, *near_part, *far_part)
    return (returned, weight_grad, bias_grad.reshape(-1))


def solution(mesh):
    n_dp, n_ctx, n_mp = (mesh.shape[a] for a in ("dp", "ctx", "mp"))
    placed = (
        P(("dp", "ctx"), None),
        P(("dp", "ctx", "mp"), None),
        P(("ctx", "mp"), None),
        P("dp", None, None),
        P("dp", None),
        P("dp", None, None),
    )

    def per_device(*args):
        hid, feat = args[2].shape
        rows = args[1].shape[0] * n_ctx * n_mp
        gather = (n_dp - 1) * rows * (hid + feat // n_dp) * 2
        scatter = hid * feat * 4 * (n_dp - 1) // n_dp
        fits = n_mp == 2 and all(n & (n - 1) == 0 for n in (n_dp, n_ctx))
        return (gathered if fits and gather < scatter else reduced)(*args)

    return jax.shard_map(
        per_device,
        mesh=mesh,
        in_specs=placed,
        out_specs=(P(("dp", "ctx", "mp"), None), P(("ctx", "mp"), "dp"), P("dp")),
        check_vma=False,
    )
```

time: 240 us -> 78.1 us (0.33)
  waiting for transfers between devices: 173 us -> 15.7 us
  starting transfers between devices: 8.65 us -> 36 us
  Pallas kernels: 0 us -> 20.6 us
  blocking collectives: 19.4 us -> 0 us
  between operations: 14.8 us -> 0.85 us
  matrix products: 10.9 us -> 0 us
  local copies, waits for them, and re-layouts: 10.2 us -> 3.59 us
    reduce_scatter x1 -> x0, waiting for transfers between devices: 147 us -> none  [per_device(): lax.psum_scatter(term, 'dp', scatter_dimension=1, tiled=True)]
    ppermute x0 -> x16, starting transfers between devices: none -> 22.6 us  [swap(): return lax.ppermute(x, axis, [(i, i ^ k) for i in range(n)])]
    pallas_call x0 -> x5, Pallas kernels: none -> 20.6 us  [the longest x1 8.55 us: gathered(): pl.pallas_call(functools.partial(grad_kernel, n_ctx), out_shape=struct((r...]
    all_gather x1 -> x0, waiting for transfers between devices: 20.6 us -> none  [per_device(): stream_grad = lax.all_gather(own_rows, 'ctx', axis=0, tiled=True)]
    unnamed x1 -> x0, blocking collectives: 19.4 us -> none
    dot_general x3 -> x0, matrix products: 10.9 us -> none  [the longest x1 5.56 us: per_device(): lax.dot_general(act, row_grad, (((0,), (0,)), ((), ())), preferred_elemen...]
    ppermute x0 -> x16, waiting for transfers between devices: none -> 6.35 us  [swap(): return lax.ppermute(x, axis, [(i, i ^ k) for i in range(n)])]
    gather x2 -> x0, local copies, waits for them, and re-layouts: 6.19 us -> none  [the longest x1 4.66 us: per_device(): row_grad = stream_grad[stream]]
  transfers between devices with their start and end apart: 4 -> 19, of which waited for: 3 -> 4; matrix products, arithmetic and copies ran while one was open for 4% -> 3% of each run, Pallas kernels for 0% -> 16%
where the time goes in v1:
time: 78.1 us; the launch traced here: 77.4 us
  starting transfers between devices  36 us (46%)
  Pallas kernels  20.6 us (26%)
  waiting for transfers between devices  15.7 us (20%)
  local copies, waits for them, and re-layouts  3.59 us (5%)
  between operations  0.85 us (1%)
    ppermute x16, starting transfers between devices, swap(): return lax.ppermute(x, axis, [(i, i ^ k) for i in range(n)])  22.6 us
    pallas_call x1, Pallas kernels, gathered(): pl.pallas_call(functools.partial(grad_kernel, n_ctx), out_shape=struct((r...  8.55 us
    ppermute x16, waiting for transfers between devices, swap(): return lax.ppermute(x, axis, [(i, i ^ k) for i in range(n)])  6.35 us
    pallas_call x1, Pallas kernels, gathered(): pl.pallas_call(functools.partial(weight_kernel, n_dp, n_ctx), out_shape=(...  5.77 us
    all_to_all x1, waiting for transfers between devices, gathered(): lax.all_to_all(grad.reshape(images, vit, hid), ('ctx', 'mp'), 0, 0, tiled...  5.57 us
    all_to_all x1, starting transfers between devices, gathered(): lax.all_to_all(blocks, ('ctx', 'mp'), 0, 0, tiled=True).reshape(rows, hid)  5.17 us
    all_to_all x1, starting transfers between devices, gathered(): lax.all_to_all(parts, 'dp', 0, 0, tiled=True)  4.87 us
    all_to_all x1, waiting for transfers between devices, gathered(): lax.all_to_all(blocks, ('ctx', 'mp'), 0, 0, tiled=True).reshape(rows, hid)  3.75 us
  transfers between devices with their start and end apart: 19, of which 4 were waited for; matrix products, arithmetic and copies ran while one was open for 3% of the time, Pallas kernels for 16%

profile of v1, /device:TPU:0, one launch (start us, length us, event | category | flops | bytes accessed | tf_op | source)
XLA Modules:
  0.0 77.4 jit_solution(11417771876116582603)
XLA Ops:
  0.6 0.6 pad_add_fusion.ids
  1.2 2.5 %pick.1 = (bf16[8,24,640]{2,1,0:T(8,128)(2,1)}, bf16[48,2048]{1,0:T(8,128)(2,1)}, bf16[48,2048]{1,0:T(8,128)(2,1)}, bf16[4,48,512]{2,1,0:T(8,128)(2,1)}) custom-call(s32[3]{0:T(128)} %pad_add_fusion.ids, bf16[128,4096]{1,0:T(8,128)(2,1)} %llm.1, s32[1,4,48]{2,1,0:T(4,128)} %places.1, bf16[24,5120]{1,0:T(8,128)(2,1)} %pre.1), custom_call_target="tpu_custom_call" | custom-call | tf_op jit(solution)/shard_map/pick/pallas_call | solution.py:202
  3.7 5.2 %all-to-all-start = ((bf16[8,24,640]{2,1,0:T(8,128)(2,1)}), bf16[8,24,640]{2,1,0:T(8,128)(2,1)S(1)}, u32[]{:S(2)}, u32[]{:S(2)}) async-start(bf16[8,24,640]{2,1,0:T(8,128)(2,1)} %get-tuple-element.16), calls=%async_computation | async-start | bytes 491520 | tf_op jit(solution)/shard_map/all_to_all | solution.py:216
  8.9 2.9 %collective-permute-start.2 = (bf16[48,2048]{1,0:T(8,128)(2,1)}, bf16[48,2048]{1,0:T(8,128)(2,1)S(1)}, u32[]{:S(2)}, u32[]{:S(2)}) collective-permute-start(bf16[48,2048]{1,0:T(8,128)(2,1)} %get-tuple-element.13.refs_0_), channel_id=1, source_target_pairs={{0,6},{2,4},{4,2},{6,0},{1,7},{3,5},{5,3},{7,1},{8,14},{10,12},{12... | collective-permute-start | bytes 589832 | tf_op jit(solution)/shard_map/ppermute | solution.py:188
  11.8 0.6 collective-permute-start.1
  12.3 0.1 collective-permute-start
  12.4 3.8 %all-to-all-done = bf16[8,24,640]{2,1,0:T(8,128)(2,1)S(1)} async-done(((bf16[8,24,640]{2,1,0:T(8,128)(2,1)}), bf16[8,24,640]{2,1,0:T(8,128)(2,1)S(1)}, u32[]{:S(2)}, u32[]{:S(2)}) %all-to-all-start) | async-done | bytes 245792 | tf_op jit(solution)/shard_map/all_to_all | solution.py:216
  16.1 4.9 %all-to-all-start.2 = ((bf16[4,48,512]{2,1,0:T(8,128)(2,1)}), bf16[4,48,512]{2,1,0:T(8,128)(2,1)S(1)}, u32[]{:S(2)}, u32[]{:S(2)}) async-start(bf16[4,48,512]{2,1,0:T(8,128)(2,1)} %get-tuple-element.20), calls=%async_computation.2 | async-start | bytes 393216 | tf_op jit(solution)/shard_map/all_to_all | solution.py:217
  21.0 0.0 collective-permute-done.2.refs_3_
  21.0 0.1 collective-permute-start.5
  21.1 2.6 %collective-permute-done.1.refs_2_ = bf16[48,2048]{1,0:T(8,128)(2,1)S(1)} collective-permute-done((bf16[48,2048]{1,0:T(8,128)(2,1)}, bf16[48,2048]{1,0:T(8,128)(2,1)S(1)}, u32[]{:S(2)}, u32[]{:S(2)}) %collective-permute-start.1) | collective-permute-done | bytes 196640 | tf_op jit(solution)/shard_map/ppermute | solution.py:188
  23.7 0.0 collective-permute-start.4
  23.7 0.0 collective-permute-done.refs_1_
  23.7 0.5 collective-permute-start.3
  24.2 0.8 copy.11
  25.0 0.6 reshape.24.counts
  25.6 1.7 %order.2 = (bf16[192,192]{1,0:T(8,128)(2,1)}, bf16[192,192]{1,0:T(8,128)(2,1)}) custom-call(s32[3]{0:T(128)} %pad_add_fusion.ids, s32[1,32]{1,0:T(1,128)} %reshape.24.counts, s32[1,32]{1,0:T(1,128)} %order.3), custom_call_target="tpu_custom_call" | custom-call | tf_op jit(solution)/shard_map/order/pallas_call | solution.py:221
  27.2 2.2 %act.1 = (bf16[192,640]{1,0:T(8,128)(2,1)}, f32[192,640]{1,0:T(8,128)}) custom-call(bf16[192,192]{1,0:T(8,128)(2,1)} %get-tuple-element.15.there, bf16[192,640]{1,0:T(8,128)(2,1)} %bitcast.10), custom_call_target="tpu_custom_call" | custom-call | tf_op jit(solution)/shard_map/act/pallas_call | solution.py:229
  29.4 3.6 %collective-permute-start.8 = (bf16[192,640]{1,0:T(8,128)(2,1)}, bf16[192,640]{1,0:T(8,128)(2,1)S(1)}, u32[]{:S(2)}, u32[]{:S(2)}) collective-permute-start(bf16[192,640]{1,0:T(8,128)(2,1)} %get-tuple-element.19.refs_0_), channel_id=1, source_target_pairs={{0,24},{8,16},{16,8},{24,0},{1,25},{9,17},{17,9},{25,1},{2,26},{10... | collective-permute-start | bytes 737288 | tf_op jit(solution)/shard_map/ppermute | solution.py:188
  33.0 0.0 collective-permute-start.7
  33.0 0.0 all-to-all-done.2
  33.0 0.0 collective-permute-done.5.refs_7_
  33.1 1.5 %collective-permute-start.11 = (bf16[192,512]{1,0:T(8,128)(2,1)S(1)}, bf16[192,512]{1,0:T(8,128)(2,1)S(1)}, u32[]{:S(2)}, u32[]{:S(2)}) collective-permute-start(bf16[192,512]{1,0:T(8,128)(2,1)S(1)} %bitcast.13), channel_id=1, source_target_pairs={{0,6},{2,4},{4,2},{6,0},{1,7},{3,5},{5,3},{7,1},{8,14},{10,12},{12... | collective-permute-start | bytes 589832 | tf_op jit(solution)/shard_map/ppermute | solution.py:188
  34.5 0.0 collective-permute-done.4.refs_6_
  34.5 1.9 %collective-permute-start.10 = (bf16[192,512]{1,0:T(8,128)(2,1)S(1)}, bf16[192,512]{1,0:T(8,128)(2,1)S(1)}, u32[]{:S(2)}, u32[]{:S(2)}) collective-permute-start(bf16[192,512]{1,0:T(8,128)(2,1)S(1)} %bitcast.14), channel_id=1, source_target_pairs={{0,4},{2,6},{4,0},{6,2},{1,5},{3,7},{5,1},{7,3},{8,12},{10,14},{12... | collective-permute-start | bytes 589832 | tf_op jit(solution)/shard_map/ppermute | solution.py:188
  36.4 0.0 collective-permute-done.3.refs_5_
  36.4 0.2 collective-permute-start.9
  36.6 3.7 %collective-permute-done.8.refs_3_ = bf16[192,640]{1,0:T(8,128)(2,1)S(1)} collective-permute-done((bf16[192,640]{1,0:T(8,128)(2,1)}, bf16[192,640]{1,0:T(8,128)(2,1)S(1)}, u32[]{:S(2)}, u32[]{:S(2)}) %collective-permute-start.8) | collective-permute-done | bytes 245792 | tf_op jit(solution)/shard_map/ppermute | solution.py:188
  40.3 10.2 %collective-permute-start.6 = (bf16[192,640]{1,0:T(8,128)(2,1)}, bf16[192,640]{1,0:T(8,128)(2,1)S(1)}, u32[]{:S(2)}, u32[]{:S(2)}) collective-permute-start(bf16[192,640]{1,0:T(8,128)(2,1)} %get-tuple-element.19.refs_0_), channel_id=1, source_target_pairs={{0,8},{8,0},{16,24},{24,16},{1,9},{9,1},{17,25},{25,17},{2,10},{10... | collective-permute-start | bytes 737288 | tf_op jit(solution)/shard_map/ppermute | solution.py:188
  50.6 8.5 %grad.1 = bf16[192,640]{1,0:T(8,128)(2,1)} custom-call(s32[3]{0:T(128)} %pad_add_fusion.ids, bf16[48,2048]{1,0:T(8,128)(2,1)} %get-tuple-element.13.refs_0_, bf16[48,2048]{1,0:T(8,128)(2,1)} %copy-done.8, bf16[48,2048]{1,0:T(8,128)(2,1)} %copy-done.7, bf16[48,2048]{1,0:T(8,128)(2,1)} %copy-done.5, bf16[48,2048]{1,0:T(8,128)(2,1)} %get-tuple-element.14.refs_4_, ...), custom_call_target="tpu_custom_call" | custom-call | tf_op jit(solution)/shard_map/grad/pallas_call | solution.py:241
  59.1 3.4 %all-to-all-start.1 = ((bf16[8,24,640]{2,1,0:T(8,128)(2,1)}), bf16[8,24,640]{2,1,0:T(8,128)(2,1)S(1)}, u32[]{:S(2)}, u32[]{:S(2)}) async-start(bf16[8,24,640]{2,1,0:T(8,128)(2,1)} %bitcast.11), calls=%async_computation.1 | async-start | bytes 491520 | tf_op jit(solution)/shard_map/all_to_all | solution.py:256
  62.6 0.0 collective-permute-done.7.refs_2_
  62.6 0.5 collective-permute-start.12
  63.1 0.1 collective-permute-start.15
  63.2 0.4 collective-permute-start.14
  63.6 0.0 collective-permute-done.9.refs_5_
  63.6 0.1 collective-permute-start.13
  63.7 5.6 %all-to-all-done.1 = bf16[8,24,640]{2,1,0:T(8,128)(2,1)S(1)} async-done(((bf16[8,24,640]{2,1,0:T(8,128)(2,1)}), bf16[8,24,640]{2,1,0:T(8,128)(2,1)S(1)}, u32[]{:S(2)}, u32[]{:S(2)}) %all-to-all-start.1) | async-done | bytes 245792 | tf_op jit(solution)/shard_map/all_to_all | solution.py:256
  69.3 0.7 copy.13
  70.0 0.0 collective-permute-done.6.refs_1_
  70.0 0.0 collective-permute-done.15.refs_11_
  70.0 0.0 collective-permute-done.14.refs_10_
  70.1 0.6 copy-done.4
  70.7 0.1 copy-done.14
  70.8 0.1 copy-done.15
  70.8 0.1 copy-done.16
  70.9 0.7 copy-done.17
  71.6 5.8 %weight.1 = (f32[640,1024]{1,0:T(8,128)}, f32[1,1024]{1,0:T(1,128)}) custom-call(s32[3]{0:T(128)} %pad_add_fusion.ids, bf16[192,640]{1,0:T(8,128)(2,1)} %get-tuple-element.19.refs_0_, bf16[192,640]{1,0:T(8,128)(2,1)} %copy-done.4, bf16[192,640]{1,0:T(8,128)(2,1)} %copy-done.3, bf16[192,640]{1,0:T(8,128)(2,1)} %copy-done.2, bf16[192,512]{1,0:T(8,128)(2,1)} %bitcast.17, ...), custom_call_target="tpu_custom_call" | custom-call | tf_op jit(solution)/shard_map/weight/pallas_call | solution.py:260
  (35 shorter events, 0.1 us)
Async XLA Ops:
  3.7 12.5 %all-to-all-start = ((bf16[8,24,640]{2,1,0:T(8,128)(2,1)}), bf16[8,24,640]{2,1,0:T(8,128)(2,1)S(1)}, u32[]{:S(2)}, u32[]{:S(2)}) async-start(bf16[8,24,640]{2,1,0:T(8,128)(2,1)} %get-tuple-element.16), calls=%async_computation | async-start | bytes 491520 | tf_op jit(solution)/shard_map/all_to_all | solution.py:216
  8.9 12.2 %collective-permute-start.2 = (bf16[48,2048]{1,0:T(8,128)(2,1)}, bf16[48,2048]{1,0:T(8,128)(2,1)S(1)}, u32[]{:S(2)}, u32[]{:S(2)}) collective-permute-start(bf16[48,2048]{1,0:T(8,128)(2,1)} %get-tuple-element.13.refs_0_), channel_id=1, source_target_pairs={{0,6},{2,4},{4,2},{6,0},{1,7},{3,5},{5,3},{7,1},{8,14},{10,12},{12... | collective-permute-start | bytes 589832 | tf_op jit(solution)/shard_map/ppermute | solution.py:188
  11.8 11.9 %collective-permute-start.1 = (bf16[48,2048]{1,0:T(8,128)(2,1)}, bf16[48,2048]{1,0:T(8,128)(2,1)S(1)}, u32[]{:S(2)}, u32[]{:S(2)}) collective-permute-start(bf16[48,2048]{1,0:T(8,128)(2,1)} %get-tuple-element.13.refs_0_), channel_id=1, source_target_pairs={{0,4},{2,6},{4,0},{6,2},{1,5},{3,7},{5,1},{7,3},{8,12},{10,14},{12... | collective-permute-start | bytes 589832 | tf_op jit(solution)/shard_map/ppermute | solution.py:188
  12.3 11.4 %collective-permute-start = (bf16[48,2048]{1,0:T(8,128)(2,1)}, bf16[48,2048]{1,0:T(8,128)(2,1)S(1)}, u32[]{:S(2)}, u32[]{:S(2)}) collective-permute-start(bf16[48,2048]{1,0:T(8,128)(2,1)} %get-tuple-element.13.refs_0_), channel_id=1, source_target_pairs={{0,2},{2,0},{4,6},{6,4},{1,3},{3,1},{5,7},{7,5},{8,10},{10,8},{12,... | collective-permute-start | bytes 589832 | tf_op jit(solution)/shard_map/ppermute | solution.py:188
  16.1 11.1 %copy-start = (bf16[8,24,640]{2,1,0:T(8,128)(2,1)}, bf16[8,24,640]{2,1,0:T(8,128)(2,1)S(1)}, u32[]{:S(2)}) copy-start(bf16[8,24,640]{2,1,0:T(8,128)(2,1)S(1)} %all-to-all-done) | copy-start | bytes 737284
  16.1 16.9 %all-to-all-start.2 = ((bf16[4,48,512]{2,1,0:T(8,128)(2,1)}), bf16[4,48,512]{2,1,0:T(8,128)(2,1)S(1)}, u32[]{:S(2)}, u32[]{:S(2)}) async-start(bf16[4,48,512]{2,1,0:T(8,128)(2,1)} %get-tuple-element.20), calls=%async_computation.2 | async-start | bytes 393216 | tf_op jit(solution)/shard_map/all_to_all | solution.py:217
  21.0 29.5 %copy-start.5 = (bf16[48,2048]{1,0:T(8,128)(2,1)}, bf16[48,2048]{1,0:T(8,128)(2,1)S(1)}, u32[]{:S(2)}) copy-start(bf16[48,2048]{1,0:T(8,128)(2,1)S(1)} %collective-permute-done.2.refs_3_) | copy-start | bytes 589828
  21.0 12.0 %collective-permute-start.5 = (bf16[48,2048]{1,0:T(8,128)(2,1)S(1)}, bf16[48,2048]{1,0:T(8,128)(2,1)S(1)}, u32[]{:S(2)}, u32[]{:S(2)}) collective-permute-start(bf16[48,2048]{1,0:T(8,128)(2,1)S(1)} %collective-permute-done.2.refs_3_), channel_id=1, source_target_pairs={{0,1},{1,0},{2,3},{3,2},{4,5},{5,4},{6,7},{7,6},{8,9},{9,8},{10,11... | collective-permute-start | bytes 589832 | tf_op jit(solution)/shard_map/ppermute | solution.py:188
  23.7 26.9 %copy-start.7 = (bf16[48,2048]{1,0:T(8,128)(2,1)}, bf16[48,2048]{1,0:T(8,128)(2,1)S(1)}, u32[]{:S(2)}) copy-start(bf16[48,2048]{1,0:T(8,128)(2,1)S(1)} %collective-permute-done.1.refs_2_) | copy-start | bytes 589828
  23.7 10.8 %collective-permute-start.4 = (bf16[48,2048]{1,0:T(8,128)(2,1)S(1)}, bf16[48,2048]{1,0:T(8,128)(2,1)S(1)}, u32[]{:S(2)}, u32[]{:S(2)}) collective-permute-start(bf16[48,2048]{1,0:T(8,128)(2,1)S(1)} %collective-permute-done.1.refs_2_), channel_id=1, source_target_pairs={{0,1},{1,0},{2,3},{3,2},{4,5},{5,4},{6,7},{7,6},{8,9},{9,8},{10,11... | collective-permute-start | bytes 589832 | tf_op jit(solution)/shard_map/ppermute | solution.py:188
  23.7 26.9 %copy-start.8 = (bf16[48,2048]{1,0:T(8,128)(2,1)}, bf16[48,2048]{1,0:T(8,128)(2,1)S(1)}, u32[]{:S(2)}) copy-start(bf16[48,2048]{1,0:T(8,128)(2,1)S(1)} %collective-permute-done.refs_1_) | copy-start | bytes 589828
  23.7 12.7 %collective-permute-start.3 = (bf16[48,2048]{1,0:T(8,128)(2,1)S(1)}, bf16[48,2048]{1,0:T(8,128)(2,1)S(1)}, u32[]{:S(2)}, u32[]{:S(2)}) collective-permute-start(bf16[48,2048]{1,0:T(8,128)(2,1)S(1)} %collective-permute-done.refs_1_), channel_id=1, source_target_pairs={{0,1},{1,0},{2,3},{3,2},{4,5},{5,4},{6,7},{7,6},{8,9},{9,8},{10,11... | collective-permute-start | bytes 589832 | tf_op jit(solution)/shard_map/ppermute | solution.py:188
  29.4 10.9 %collective-permute-start.8 = (bf16[192,640]{1,0:T(8,128)(2,1)}, bf16[192,640]{1,0:T(8,128)(2,1)S(1)}, u32[]{:S(2)}, u32[]{:S(2)}) collective-permute-start(bf16[192,640]{1,0:T(8,128)(2,1)} %get-tuple-element.19.refs_0_), channel_id=1, source_target_pairs={{0,24},{8,16},{16,8},{24,0},{1,25},{9,17},{17,9},{25,1},{2,26},{10... | collective-permute-start | bytes 737288 | tf_op jit(solution)/shard_map/ppermute | solution.py:188
  33.0 29.5 %collective-permute-start.7 = (bf16[192,640]{1,0:T(8,128)(2,1)}, bf16[192,640]{1,0:T(8,128)(2,1)S(1)}, u32[]{:S(2)}, u32[]{:S(2)}) collective-permute-start(bf16[192,640]{1,0:T(8,128)(2,1)} %get-tuple-element.19.refs_0_), channel_id=1, source_target_pairs={{0,16},{8,24},{16,0},{24,8},{1,17},{9,25},{17,1},{25,9},{2,18},{10... | collective-permute-start | bytes 737288 | tf_op jit(solution)/shard_map/ppermute | solution.py:188
  33.0 37.0 %copy-start.1 = (bf16[4,48,512]{2,1,0:T(8,128)(2,1)}, bf16[4,48,512]{2,1,0:T(8,128)(2,1)S(1)}, u32[]{:S(2)}) copy-start(bf16[4,48,512]{2,1,0:T(8,128)(2,1)S(1)} %all-to-all-done.2) | copy-start | bytes 589828
  33.1 17.5 %copy-start.11 = (bf16[48,2048]{1,0:T(8,128)(2,1)}, bf16[48,2048]{1,0:T(8,128)(2,1)S(1)}, u32[]{:S(2)}) copy-start(bf16[48,2048]{1,0:T(8,128)(2,1)S(1)} %collective-permute-done.5.refs_7_) | copy-start | bytes 589828
  33.1 30.0 %collective-permute-start.11 = (bf16[192,512]{1,0:T(8,128)(2,1)S(1)}, bf16[192,512]{1,0:T(8,128)(2,1)S(1)}, u32[]{:S(2)}, u32[]{:S(2)}) collective-permute-start(bf16[192,512]{1,0:T(8,128)(2,1)S(1)} %bitcast.13), channel_id=1, source_target_pairs={{0,6},{2,4},{4,2},{6,0},{1,7},{3,5},{5,3},{7,1},{8,14},{10,12},{12... | collective-permute-start | bytes 589832 | tf_op jit(solution)/shard_map/ppermute | solution.py:188
  34.5 16.0 %copy-start.12 = (bf16[48,2048]{1,0:T(8,128)(2,1)}, bf16[48,2048]{1,0:T(8,128)(2,1)S(1)}, u32[]{:S(2)}) copy-start(bf16[48,2048]{1,0:T(8,128)(2,1)S(1)} %collective-permute-done.4.refs_6_) | copy-start | bytes 589828
  34.5 28.6 %collective-permute-start.10 = (bf16[192,512]{1,0:T(8,128)(2,1)S(1)}, bf16[192,512]{1,0:T(8,128)(2,1)S(1)}, u32[]{:S(2)}, u32[]{:S(2)}) collective-permute-start(bf16[192,512]{1,0:T(8,128)(2,1)S(1)} %bitcast.14), channel_id=1, source_target_pairs={{0,4},{2,6},{4,0},{6,2},{1,5},{3,7},{5,1},{7,3},{8,12},{10,14},{12... | collective-permute-start | bytes 589832 | tf_op jit(solution)/shard_map/ppermute | solution.py:188
  36.4 14.1 %copy-start.13 = (bf16[48,2048]{1,0:T(8,128)(2,1)}, bf16[48,2048]{1,0:T(8,128)(2,1)S(1)}, u32[]{:S(2)}) copy-start(bf16[48,2048]{1,0:T(8,128)(2,1)S(1)} %collective-permute-done.3.refs_5_) | copy-start | bytes 589828
  36.4 27.1 %collective-permute-start.9 = (bf16[192,512]{1,0:T(8,128)(2,1)S(1)}, bf16[192,512]{1,0:T(8,128)(2,1)S(1)}, u32[]{:S(2)}, u32[]{:S(2)}) collective-permute-start(bf16[192,512]{1,0:T(8,128)(2,1)S(1)} %bitcast.15), channel_id=1, source_target_pairs={{0,2},{2,0},{4,6},{6,4},{1,3},{3,1},{5,7},{7,5},{8,10},{10,8},{12,... | collective-permute-start | bytes 589832 | tf_op jit(solution)/shard_map/ppermute | solution.py:188
  40.3 29.7 %copy-start.2 = (bf16[192,640]{1,0:T(8,128)(2,1)}, bf16[192,640]{1,0:T(8,128)(2,1)S(1)}, u32[]{:S(2)}) copy-start(bf16[192,640]{1,0:T(8,128)(2,1)S(1)} %collective-permute-done.8.refs_3_) | copy-start | bytes 737284
  40.3 29.6 %collective-permute-start.6 = (bf16[192,640]{1,0:T(8,128)(2,1)}, bf16[192,640]{1,0:T(8,128)(2,1)S(1)}, u32[]{:S(2)}, u32[]{:S(2)}) collective-permute-start(bf16[192,640]{1,0:T(8,128)(2,1)} %get-tuple-element.19.refs_0_), channel_id=1, source_target_pairs={{0,8},{8,0},{16,24},{24,16},{1,9},{9,1},{17,25},{25,17},{2,10},{10... | collective-permute-start | bytes 737288 | tf_op jit(solution)/shard_map/ppermute | solution.py:188
  59.1 10.1 %all-to-all-start.1 = ((bf16[8,24,640]{2,1,0:T(8,128)(2,1)}), bf16[8,24,640]{2,1,0:T(8,128)(2,1)S(1)}, u32[]{:S(2)}, u32[]{:S(2)}) async-start(bf16[8,24,640]{2,1,0:T(8,128)(2,1)} %bitcast.11), calls=%async_computation.1 | async-start | bytes 491520 | tf_op jit(solution)/shard_map/all_to_all | solution.py:256
  62.6 7.5 %copy-start.3 = (bf16[192,640]{1,0:T(8,128)(2,1)}, bf16[192,640]{1,0:T(8,128)(2,1)S(1)}, u32[]{:S(2)}) copy-start(bf16[192,640]{1,0:T(8,128)(2,1)S(1)} %collective-permute-done.7.refs_2_) | copy-start | bytes 737284
  62.6 7.4 %collective-permute-start.12 = (bf16[192,512]{1,0:T(8,128)(2,1)S(1)}, bf16[192,512]{1,0:T(8,128)(2,1)S(1)}, u32[]{:S(2)}, u32[]{:S(2)}) collective-permute-start(bf16[192,512]{1,0:T(8,128)(2,1)S(1)} %bitcast.16), channel_id=1, source_target_pairs={{0,1},{1,0},{2,3},{3,2},{4,5},{5,4},{6,7},{7,6},{8,9},{9,8},{10,11... | collective-permute-start | bytes 589832 | tf_op jit(solution)/shard_map/ppermute | solution.py:188
  63.1 7.0 %copy-start.6 = (bf16[192,512]{1,0:T(8,128)(2,1)}, bf16[192,512]{1,0:T(8,128)(2,1)S(1)}, u32[]{:S(2)}) copy-start(bf16[192,512]{1,0:T(8,128)(2,1)S(1)} %collective-permute-done.11.refs_7_) | copy-start | bytes 589828
  63.1 6.9 %collective-permute-start.15 = (bf16[192,512]{1,0:T(8,128)(2,1)S(1)}, bf16[192,512]{1,0:T(8,128)(2,1)S(1)}, u32[]{:S(2)}, u32[]{:S(2)}) collective-permute-start(bf16[192,512]{1,0:T(8,128)(2,1)S(1)} %collective-permute-done.11.refs_7_), channel_id=1, source_target_pairs={{0,1},{1,0},{2,3},{3,2},{4,5},{5,4},{6,7},{7,6},{8,9},{9,8},{10,11... | collective-permute-start | bytes 589832 | tf_op jit(solution)/shard_map/ppermute | solution.py:188
  63.2 6.9 %copy-start.9 = (bf16[192,512]{1,0:T(8,128)(2,1)}, bf16[192,512]{1,0:T(8,128)(2,1)S(1)}, u32[]{:S(2)}) copy-start(bf16[192,512]{1,0:T(8,128)(2,1)S(1)} %collective-permute-done.10.refs_6_) | copy-start | bytes 589828
  63.2 6.8 %collective-permute-start.14 = (bf16[192,512]{1,0:T(8,128)(2,1)S(1)}, bf16[192,512]{1,0:T(8,128)(2,1)S(1)}, u32[]{:S(2)}, u32[]{:S(2)}) collective-permute-start(bf16[192,512]{1,0:T(8,128)(2,1)S(1)} %collective-permute-done.10.refs_6_), channel_id=1, source_target_pairs={{0,1},{1,0},{2,3},{3,2},{4,5},{5,4},{6,7},{7,6},{8,9},{9,8},{10,11... | collective-permute-start | bytes 589832 | tf_op jit(solution)/shard_map/ppermute | solution.py:188
  63.6 6.5 %copy-start.10 = (bf16[192,512]{1,0:T(8,128)(2,1)}, bf16[192,512]{1,0:T(8,128)(2,1)S(1)}, u32[]{:S(2)}) copy-start(bf16[192,512]{1,0:T(8,128)(2,1)S(1)} %collective-permute-done.9.refs_5_) | copy-start | bytes 589828
  63.6 6.5 %collective-permute-start.13 = (bf16[192,512]{1,0:T(8,128)(2,1)S(1)}, bf16[192,512]{1,0:T(8,128)(2,1)S(1)}, u32[]{:S(2)}, u32[]{:S(2)}) collective-permute-start(bf16[192,512]{1,0:T(8,128)(2,1)S(1)} %collective-permute-done.9.refs_5_), channel_id=1, source_target_pairs={{0,1},{1,0},{2,3},{3,2},{4,5},{5,4},{6,7},{7,6},{8,9},{9,8},{10,11... | collective-permute-start | bytes 589832 | tf_op jit(solution)/shard_map/ppermute | solution.py:188
  70.0 0.7 copy-start.4
  70.0 0.8 %copy-start.14 = (bf16[192,512]{1,0:T(8,128)(2,1)}, bf16[192,512]{1,0:T(8,128)(2,1)S(1)}, u32[]{:S(2)}) copy-start(bf16[192,512]{1,0:T(8,128)(2,1)S(1)} %collective-permute-done.12.refs_8_) | copy-start | bytes 589828
  70.0 0.8 %copy-start.15 = (bf16[192,512]{1,0:T(8,128)(2,1)}, bf16[192,512]{1,0:T(8,128)(2,1)S(1)}, u32[]{:S(2)}) copy-start(bf16[192,512]{1,0:T(8,128)(2,1)S(1)} %collective-permute-done.15.refs_11_) | copy-start | bytes 589828
  70.0 0.9 %copy-start.16 = (bf16[192,512]{1,0:T(8,128)(2,1)}, bf16[192,512]{1,0:T(8,128)(2,1)S(1)}, u32[]{:S(2)}) copy-start(bf16[192,512]{1,0:T(8,128)(2,1)S(1)} %collective-permute-done.14.refs_10_) | copy-start | bytes 589828
  70.9 0.7 copy-start.17

commit v2 on v0

v2 whole, which is shorter than its diff:
```python
import functools

import jax
import jax.numpy as jnp
from jax import lax
from jax.experimental import pallas as pl
from jax.experimental.pallas import tpu as pltpu
from jax.sharding import PartitionSpec as P

BF16 = jnp.bfloat16
F32 = jnp.float32
VMEM = pl.BlockSpec(memory_space=pltpu.VMEM)
ANY = pl.BlockSpec(memory_space=pl.ANY)
HBM = pl.BlockSpec(memory_space=pltpu.HBM)


def gelu_parts(x):
    cdf = 0.5 * (1.0 + lax.erf(x * 0.7071067811865476))
    pdf = jnp.exp(-0.5 * x * x) * 0.3989422804014327
    return (x * cdf, cdf + x * pdf)


def stream_rows(counts, order, length):
    total = counts.shape[0]
    vit_end = jnp.cumsum(counts)
    vit_start = vit_end - counts
    onehot = (order[:, None] == jnp.arange(total, dtype=jnp.int32)[None, :]).astype(jnp.int32)
    ordered = jnp.sum(onehot * counts[None, :], axis=1)
    place_start = jnp.cumsum(ordered) - ordered
    llm_start = jnp.sum(onehot * place_start[:, None], axis=0)
    shift = llm_start - vit_start
    rows = jnp.arange(length, dtype=jnp.int32)
    member = (rows[:, None] >= vit_start[None, :]) & (rows[:, None] < vit_end[None, :])
    return rows + jnp.sum(jnp.where(member, shift[None, :], 0), axis=1)


def reduced(llm_grad, merger_pre, out_weight, patch_counts, image_order, vision_rows):
    group_rows = merger_pre.shape[0] * lax.axis_size(("ctx", "mp"))
    stream = stream_rows(patch_counts.reshape(-1), image_order.reshape(-1), group_rows)
    own_places = vision_rows[0][lax.axis_index("ctx")]
    own_rows = llm_grad[own_places]
    stream_grad = lax.all_gather(own_rows, "ctx", axis=0, tiled=True)
    pre_cols = lax.all_to_all(merger_pre, ("ctx", "mp"), split_axis=1, concat_axis=0, tiled=True)
    row_grad = stream_grad[stream]
    value, slope = gelu_parts(pre_cols.astype(F32))
    act = value.astype(BF16)
    act_grad = lax.dot_general(row_grad, out_weight, (((1,), (1,)), ((), ())), preferred_element_type=F32)
    pre_grad = (act_grad * slope).astype(BF16)
    returned = lax.all_to_all(pre_grad, ("ctx", "mp"), split_axis=0, concat_axis=1, tiled=True)
    term = lax.dot_general(act, row_grad, (((0,), (0,)), ((), ())), preferred_element_type=F32)
    ones_row = jnp.ones((row_grad.shape[0],), BF16)
    bias_term = jnp.dot(ones_row, row_grad, preferred_element_type=F32)
    return (
        returned,
        lax.psum_scatter(term, "dp", scatter_dimension=1, tiled=True),
        lax.psum_scatter(bias_term, "dp", scatter_dimension=0, tiled=True),
    )


def cut_kernel(pre, blocks, sems):
    wide = blocks.shape[2]
    copies = [
        pltpu.make_async_copy(pre.at[:, i * wide : (i + 1) * wide], blocks.at[i], sems.at[i])
        for i in range(blocks.shape[0])
    ]
    for copy in copies:
        copy.start()
    for copy in copies:
        copy.wait()


def order_maps(ctx, n_ctx, counts, order, there, back):
    images, rows = order.shape[1], there.shape[0]
    block = rows // n_ctx
    up = lax.broadcasted_iota(jnp.int32, (images, images), 0)
    along = lax.broadcasted_iota(jnp.int32, (images, images), 1)
    order_row = order[...]

    def total(mask, values, axis):
        return jnp.sum(jnp.where(mask, values, 0).astype(F32), axis=axis, keepdims=True).astype(jnp.int32)

    same = up == along
    per = counts.shape[1]
    shard = lax.broadcasted_iota(jnp.int32, (images, counts.shape[2]), 1)
    image = lax.broadcasted_iota(jnp.int32, (images, counts.shape[2]), 0)
    count_col = jnp.zeros((images, 1), jnp.int32)
    for i in range(per):
        count_col += total(image == shard * per + i, counts[0, i : i + 1, :], 1)
    count_row = total(same, count_col, 0)
    order_col = total(same, order_row, 1)
    vit_start_row = total(up < along, count_col, 0)
    vit_start_col = total(along < up, count_row, 1)
    placed_row = total(order_row == up, count_col, 0)
    placed_col = total(order_col == along, count_row, 1)
    place_start_col = total(along < up, placed_row, 1)
    place_start_row = total(up < along, placed_col, 0)
    llm_start_row = total(order_col == along, place_start_col, 0)
    llm_start_col = total(order_row == up, place_start_row, 1)

    def received(shape, dim):
        at = lax.broadcasted_iota(jnp.int32, shape, dim)
        out = jnp.zeros(shape, jnp.int32)
        for k in range(n_ctx):
            inside = (at >= k * block) & (at < (k + 1) * block)
            out = jnp.where(inside, at + ((ctx ^ k) - k) * block, out)
        return out

    image = lax.broadcasted_iota(jnp.int32, (rows, images), 0)
    member = (image >= vit_start_row) & (image < vit_start_row + count_row)
    stream_col = lax.broadcasted_iota(jnp.int32, (rows, 1), 0) + total(member, llm_start_row - vit_start_row, 1)
    back[...] = (stream_col == received((1, rows), 1)).astype(F32).astype(BF16)
    image = lax.broadcasted_iota(jnp.int32, (images, rows), 1)
    member = (image >= vit_start_col) & (image < vit_start_col + count_col)
    stream_row = lax.broadcasted_iota(jnp.int32, (1, rows), 1) + total(member, llm_start_col - vit_start_col, 0)
    there[...] = (stream_row == received((rows, 1), 0)).astype(F32).astype(BF16)


def pick_kernel(n_dp, n_ctx, *refs):
    inputs, (mine, other, there, back), parts = refs[:4], refs[4:8], refs[8 : 8 + n_dp]
    local, (chosen, sems) = refs[8 + n_dp : 12 + n_dp], refs[12 + n_dp :]
    llm, places, counts, order = local
    group, ctx, core = (lax.axis_index(a) for a in ("dp", "ctx", "mp"))
    copies = [pltpu.make_async_copy(a, b, sems.at[i]) for i, (a, b) in enumerate(zip(inputs, local))]
    for copy in copies:
        copy.start()
    for copy in copies[1:]:
        copy.wait()
    order_maps(ctx, n_ctx, counts, order, there, back)
    own = places[0, pl.ds(ctx, 1), :]
    hot = (lax.broadcasted_iota(jnp.int32, (llm.shape[0], own.shape[1]), 0) == own).astype(BF16)
    copies[0].wait()
    chosen[...] = lax.dot_general(hot, llm[...], (((0,), (0,)), ((), ())), preferred_element_type=F32).astype(BF16)
    half = mine.shape[1]
    mine[...] = chosen[:, pl.ds(pl.multiple_of(core * half, half), half)]
    other[...] = chosen[:, pl.ds(pl.multiple_of((1 - core) * half, half), half)]
    for i, part in enumerate(parts):
        wide = part.shape[1]
        part[...] = chosen[:, pl.ds(pl.multiple_of((2 * (group ^ i) + core) * wide, wide), wide)]


def act_kernel(there, pre, act, slope):
    x = jnp.dot(there[...], pre[...], preferred_element_type=F32)
    value, grade = gelu_parts(x)
    act[...] = value.astype(BF16)
    slope[...] = grade


def stack_kernel(*refs):
    parts, out = refs[:-1], refs[-1]
    rows = parts[0].shape[0]
    for i, part in enumerate(parts):
        out[i * rows : (i + 1) * rows] = part[...]


def hold_kernel(source, out, sem):
    copy = pltpu.make_async_copy(source, out, sem)
    copy.start()
    copy.wait()


def spots(core):
    return (0, 1 + core, 2 - core, 3)


def grad_kernel(mine, one, two, other, far_one, far_two, weight, slope, back, out, rows):
    core = lax.axis_index("mp")
    block, half = mine.shape

    for side, own, first, second in ((core, mine, one, two), (1 - core, other, far_one, far_two)):
        columns = pl.ds(pl.multiple_of(side * half, half), half)
        pieces = (own[...], first[...], second[:block], second[block:])
        for spot, piece in zip(spots(side), pieces):
            rows[pl.ds(pl.multiple_of(spot * block, block), block), columns] = piece

    grad = lax.dot_general(rows[...], weight[...], (((1,), (1,)), ((), ())), preferred_element_type=F32)
    grad = (grad * slope[...]).astype(BF16)
    out[...] = jnp.dot(back[...], grad, preferred_element_type=F32).astype(BF16)


def early_kernel(n_dp, pair, two, far_pair, far_two, act, right, total, bias):
    core = lax.axis_index("mp")
    rows, half = pair.shape[0] // 2, pair.shape[1]
    block = rows // n_dp
    for side, first, second in ((core, pair, two), (1 - core, far_pair, far_two)):
        columns = pl.ds(pl.multiple_of(side * half, half), half)
        for at, spot in enumerate(spots(side)):
            piece = (first, second)[at // 2]
            for i in range(n_dp):
                to = (i * len(spots(0)) + spot) * block
                start = (at % 2) * rows + i * block
                right[pl.ds(pl.multiple_of(to, block), block), columns] = piece[start : start + block]
    ones = jnp.ones((8, right.shape[0]), BF16)
    bias[...] = jnp.dot(ones, right[...], preferred_element_type=F32)[:1]
    total[...] = lax.dot_general(
        act[...], right[: act.shape[0]], (((0,), (0,)), ((), ())), preferred_element_type=F32
    )


def late_kernel(*refs):
    acts, (right, total, out) = refs[:-3], refs[-3:]
    wide, rows = out.shape[1], acts[0].shape[0]
    at = pl.ds(pl.multiple_of(pl.program_id(0) * wide, wide), wide)
    sums = total[:, at]
    for i, act in enumerate(acts):
        piece = right[(i + 1) * rows : (i + 2) * rows, at]
        sums += lax.dot_general(act[...], piece, (((0,), (0,)), ((), ())), preferred_element_type=F32)
    out[...] = sums


def struct(shape, dtype=BF16):
    return jax.ShapeDtypeStruct(shape, dtype)


def limits(mebibytes):
    return dict(
        compiler_params=pltpu.CompilerParams(vmem_limit_bytes=mebibytes << 20),
        cost_estimate=pl.CostEstimate(flops=COST, bytes_accessed=COST, transcendentals=0),
    )


COST = 1


def swap(x, axis, k):
    n = lax.axis_size(axis)
    return lax.ppermute(x, axis, [(i, i ^ k) for i in range(n)])


def round_plane(x, step):
    pairs = [(2 * c + m, 2 * (c ^ (1 << (m ^ step))) + m) for c in range(4) for m in range(2)]
    return lax.ppermute(x, ("ctx", "mp"), pairs)


def pinned(x):
    return pltpu.with_memory_space_constraint(x, pltpu.HBM)


def stacked(parts, name):
    return pl.pallas_call(
        stack_kernel,
        out_shape=struct((len(parts) * parts[0].shape[0], parts[0].shape[1])),
        in_specs=[VMEM] * len(parts),
        out_specs=VMEM,
        name=name,
        **limits(4),
    )(*parts)


def gathered(llm_grad, merger_pre, out_weight, patch_counts, image_order, vision_rows):
    n_dp, n_ctx, n_mp = lax.axis_size("dp"), lax.axis_size("ctx"), lax.axis_size("mp")
    images = n_ctx * n_mp
    vit, hidden = merger_pre.shape
    hid, feat = out_weight.shape
    block = vision_rows.shape[-1]
    rows = n_ctx * block
    cols = feat // n_dp

    blocks = pl.pallas_call(
        cut_kernel,
        out_shape=struct((images, vit, hid)),
        in_specs=[ANY],
        out_specs=ANY,
        scratch_shapes=[pltpu.SemaphoreType.DMA((images,))],
        name="cut",
        **limits(4),
    )(merger_pre)
    llm_grad, blocks = lax.optimization_barrier((llm_grad, blocks))
    pre = lax.all_to_all(blocks, ("ctx", "mp"), 0, 0, tiled=True).reshape(rows, hid)

    inputs = (llm_grad, vision_rows, jnp.swapaxes(patch_counts, 1, 2), image_order)
    mine, other, there, back, *parts = pl.pallas_call(
        functools.partial(pick_kernel, n_dp, n_ctx),
        out_shape=(struct((block, feat // 2)),) * 2
        + (struct((rows, rows)),) * 2
        + (struct((block, cols // 2)),) * n_dp,
        in_specs=[HBM] * 4,
        out_specs=(VMEM,) * (4 + n_dp),
        scratch_shapes=[pltpu.VMEM(x.shape, x.dtype) for x in inputs]
        + [pltpu.VMEM((block, feat), BF16), pltpu.SemaphoreType.DMA((4,))],
        name="pick",
        **limits(8),
    )(*(pinned(x) for x in inputs))

    parts = [parts[0]] + [swap(parts[k], "dp", k) for k in range(1, n_dp)]
    one = round_plane(mine, 0)
    pre, *parts = lax.optimization_barrier((pre, *parts))
    act, slope = pl.pallas_call(
        act_kernel,
        out_shape=(struct((rows, hid)), struct((rows, hid), F32)),
        in_specs=[VMEM] * 2,
        out_specs=(VMEM,) * 2,
        name="act",
        **limits(4),
    )(there, pre)
    acts = {0: act} | {k: swap(act, "dp", k) for k in range(1, n_dp) if k & (k - 1) == 0}
    out_weight, one, _ = lax.optimization_barrier((out_weight, one, act))
    two = round_plane(stacked((mine, one), "pair"), 1)
    held = pl.pallas_call(
        hold_kernel,
        out_shape=struct(out_weight.shape),
        in_specs=[HBM],
        out_specs=VMEM,
        scratch_shapes=[pltpu.SemaphoreType.DMA],
        name="hold",
        **limits(8),
    )(pinned(out_weight))

    split = stacked(parts, "parts")
    one_part = round_plane(split, 0)
    one, two, held, split, one_part = lax.optimization_barrier((one, two, held, split, one_part))
    far_one, far_two = swap(one, "mp", 1), swap(two, "mp", 1)
    pair = stacked((split, one_part), "pair_part")
    far_pair = swap(pair, "mp", 1)
    two_part = round_plane(pair, 1)
    far_two_part = swap(two_part, "mp", 1)

    grad = pl.pallas_call(
        grad_kernel,
        out_shape=struct((rows, hid)),
        in_specs=[VMEM] * 9,
        out_specs=VMEM,
        scratch_shapes=[pltpu.VMEM((rows, feat), BF16)],
        name="grad",
        **limits(8),
    )(mine, one, two, other, far_one, far_two, held, slope, back)
    relay, _ = lax.optimization_barrier(([acts[k] for k in sorted(acts)], grad))
    relay = dict(zip(sorted(acts), relay))
    for k in range(n_dp):
        if k not in acts:
            acts[k] = swap(relay[k ^ (k & -k)] if k ^ (k & -k) in relay else acts[k ^ (k & -k)], "dp", k & -k)
    returned = lax.all_to_all(grad.reshape(images, vit, hid), ("ctx", "mp"), 0, 0, tiled=True)

    right, total, bias_grad = pl.pallas_call(
        functools.partial(early_kernel, n_dp),
        out_shape=(struct((n_dp * rows, cols)), struct((hid, cols), F32), struct((1, cols), F32)),
        in_specs=[VMEM] * 5,
        out_specs=(VMEM,) * 3,
        name="early",
        **limits(12),
    )(pair, two_part, far_pair, far_two_part, act)
    wide = cols // 2
    weight_grad = pl.pallas_call(
        late_kernel,
        out_shape=struct((hid, cols), F32),
        grid=(cols // wide,),
        in_specs=[VMEM] * (n_dp + 1),
        out_specs=pl.BlockSpec((hid, wide), lambda i: (0, i)),
        name="late",
        **limits(12),
    )(*(acts[k] for k in range(1, n_dp)), right, total)
    returned, weight_grad = lax.optimization_barrier((returned, weight_grad))
    returned = jnp.swapaxes(returned, 0, 1).reshape(vit, hidden)
    return (returned, weight_grad, bias_grad.reshape(-1))


def solution(mesh):
    n_dp, n_ctx, n_mp = (mesh.shape[a] for a in ("dp", "ctx", "mp"))
    placed = (
        P(("dp", "ctx"), None),
        P(("dp", "ctx", "mp"), None),
        P(("ctx", "mp"), None),
        P("dp", None, None),
        P("dp", None),
        P("dp", None, None),
    )

    def per_device(*args):
        hid, feat = args[2].shape
        rows = args[1].shape[0] * n_ctx * n_mp
        gather = (n_dp - 1) * rows * (hid + feat // n_dp) * 2
        scatter = hid * feat * 4 * (n_dp - 1) // n_dp
        fits = n_mp == 2 and n_ctx == 4 and n_dp & (n_dp - 1) == 0 and n_dp > 1
        return (gathered if fits and gather < scatter else reduced)(*args)

    return jax.shard_map(
        per_device,
        mesh=mesh,
        in_specs=placed,
        out_specs=(P(("dp", "ctx", "mp"), None), P(("ctx", "mp"), "dp"), P("dp")),
        check_vma=False,
    )
```

time: 240 us -> 57.6 us (0.24)
  waiting for transfers between devices: 173 us -> 21.2 us
  blocking collectives: 19.4 us -> 0 us
  between operations: 14.8 us -> 0.73 us
  starting transfers between devices: 8.65 us -> 21.8 us
  Pallas kernels: 0 us -> 11.8 us
  matrix products: 10.9 us -> 0 us
  local copies, waits for them, and re-layouts: 10.2 us -> 1.65 us
  other arithmetic: 2.48 us -> 0 us
    reduce_scatter x1 -> x0, waiting for transfers between devices: 147 us -> none  [per_device(): lax.psum_scatter(term, 'dp', scatter_dimension=1, tiled=True)]
    all_gather x1 -> x0, waiting for transfers between devices: 20.6 us -> none  [per_device(): stream_grad = lax.all_gather(own_rows, 'ctx', axis=0, tiled=True)]
    unnamed x1 -> x0, blocking collectives: 19.4 us -> none
    ppermute x0 -> x14, waiting for transfers between devices: none -> 19.1 us  [the longest x10 10 us: swap(): return lax.ppermute(x, axis, [(i, i ^ k) for i in range(n)])]
    ppermute x0 -> x14, starting transfers between devices: none -> 13.2 us  [the longest x10 8.54 us: swap(): return lax.ppermute(x, axis, [(i, i ^ k) for i in range(n)])]
    pallas_call x0 -> x10, Pallas kernels: none -> 11.8 us  [the longest x1 2.85 us: gathered(): pl.pallas_call(grad_kernel, out_shape=struct((rows, hid)), in_specs=[VMEM...]
    dot_general x3 -> x0, matrix products: 10.9 us -> none  [the longest x1 5.56 us: per_device(): lax.dot_general(act, row_grad, (((0,), (0,)), ((), ())), preferred_elemen...]
    gather x2 -> x0, local copies, waits for them, and re-layouts: 6.19 us -> none  [the longest x1 4.66 us: per_device(): row_grad = stream_grad[stream]]
  transfers between devices with their start and end apart: 4 -> 16, of which waited for: 3 -> 8; matrix products, arithmetic and copies ran while one was open for 4% -> 0% of each run, Pallas kernels for 0% -> 19%
where the time goes in v2:
time: 57.6 us; the launch traced here: 57.2 us
  starting transfers between devices  21.8 us (38%)
  waiting for transfers between devices  21.2 us (37%)
  Pallas kernels  11.8 us (20%)
  local copies, waits for them, and re-layouts  1.65 us (3%)
  between operations  0.73 us (1%)
    ppermute x10, waiting for transfers between devices, swap(): return lax.ppermute(x, axis, [(i, i ^ k) for i in range(n)])  10 us
    ppermute x4, waiting for transfers between devices, round_plane(): return lax.ppermute(x, ('ctx', 'mp'), pairs)  9.05 us
    ppermute x10, starting transfers between devices, swap(): return lax.ppermute(x, axis, [(i, i ^ k) for i in range(n)])  8.54 us
    all_to_all x1, starting transfers between devices, gathered(): lax.all_to_all(blocks, ('ctx', 'mp'), 0, 0, tiled=True).reshape(rows, hid)  5.18 us
    ppermute x4, starting transfers between devices, round_plane(): return lax.ppermute(x, ('ctx', 'mp'), pairs)  4.67 us
    all_to_all x1, starting transfers between devices, gathered(): lax.all_to_all(grad.reshape(images, vit, hid), ('ctx', 'mp'), 0, 0, tiled...  3.41 us
    pallas_call x1, Pallas kernels, gathered(): pl.pallas_call(grad_kernel, out_shape=struct((rows, hid)), in_specs=[VMEM...  2.85 us
    pallas_call x1, Pallas kernels, gathered(): pl.pallas_call(late_kernel, out_shape=struct((hid, cols), F32), grid=(col...  2.5 us
  transfers between devices with their start and end apart: 16, of which 8 were waited for; matrix products, arithmetic and copies ran while one was open for 0% of the time, Pallas kernels for 19%

profile of v2, /device:TPU:0, one launch (start us, length us, event | category | flops | bytes accessed | tf_op | source)
XLA Modules:
  0.0 57.2 jit_solution(12345196466387531066)
XLA Ops:
  0.6 0.0 copy-start
  0.6 0.9 %copy-done = bf16[24,5120]{1,0:T(8,128)(2,1)S(1)} copy-done((bf16[24,5120]{1,0:T(8,128)(2,1)S(1)}, bf16[24,5120]{1,0:T(8,128)(2,1)}, u32[]{:S(2)}) %copy-start) | copy-done | bytes 245784
  1.6 0.7 %cut.1 = bf16[8,24,640]{2,1,0:T(8,128)(2,1)} custom-call(bf16[24,5120]{1,0:T(8,128)(2,1)S(1)} %copy-done), custom_call_target="tpu_custom_call" | custom-call | flops 1 | bytes 1 | tf_op jit(solution)/shard_map/cut/pallas_call | solution.py:258
  2.3 5.2 %all-to-all-start = ((bf16[8,24,640]{2,1,0:T(8,128)(2,1)}), bf16[8,24,640]{2,1,0:T(8,128)(2,1)S(1)}, u32[]{:S(2)}, u32[]{:S(2)}) async-start(bf16[8,24,640]{2,1,0:T(8,128)(2,1)} %cut.1), calls=%async_computation | async-start | bytes 491520 | tf_op jit(solution)/shard_map/all_to_all | solution.py:268
  7.5 1.8 %pick.1 = (bf16[48,2048]{1,0:T(8,128)(2,1)S(1)}, bf16[48,2048]{1,0:T(8,128)(2,1)S(1)}, bf16[192,192]{1,0:T(8,128)(2,1)S(1)}, bf16[192,192]{1,0:T(8,128)(2,1)S(1)...) custom-call(bf16[128,4096]{1,0:T(8,128)(2,1)} %refs_0_, ...), custom_call_target="tpu_custom_call" | custom-call | flops 1 | bytes 1 | tf_op jit(solution)/shard_map/pick/pallas_call | solution.py:271
  9.3 2.1 %collective-permute-start = (bf16[48,2048]{1,0:T(8,128)(2,1)S(1)}, bf16[48,2048]{1,0:T(8,128)(2,1)S(1)}, u32[]{:S(2)}, u32[]{:S(2)}) collective-permute-start(bf16[48,2048]{1,0:T(8,128)(2,1)S(1)} %get-tuple-element.34.refs_0_.mine), channel_id=1, source_target_pairs={{0,2},{1,5},{2,0},{3,7},{4,6},{5,1},{6,4},{7,3},{8,10},{9,13},{10,... | collective-permute-start | bytes 589832 | tf_op jit(solution)/shard_map/ppermute | solution.py:231
  11.4 1.6 %collective-permute-start.1 = (bf16[48,512]{1,0:T(8,128)(2,1)S(1)}, bf16[48,512]{1,0:T(8,128)(2,1)S(1)}, u32[]{:S(2)}, u32[]{:S(2)}) collective-permute-start(bf16[48,512]{1,0:T(8,128)(2,1)S(1)} %get-tuple-element.38), channel_id=1, source_target_pairs={{0,8},{8,0},{16,24},{24,16},{1,9},{9,1},{17,25},{25,17},{2,10},{10... | collective-permute-start | bytes 147464 | tf_op jit(solution)/shard_map/ppermute | solution.py:226
  13.0 2.6 %collective-permute-start.2 = (bf16[48,512]{1,0:T(8,128)(2,1)S(1)}, bf16[48,512]{1,0:T(8,128)(2,1)S(1)}, u32[]{:S(2)}, u32[]{:S(2)}) collective-permute-start(bf16[48,512]{1,0:T(8,128)(2,1)S(1)} %get-tuple-element.39), channel_id=1, source_target_pairs={{0,16},{8,24},{16,0},{24,8},{1,17},{9,25},{17,1},{25,9},{2,18},{10... | collective-permute-start | bytes 147464 | tf_op jit(solution)/shard_map/ppermute | solution.py:226
  15.5 0.2 collective-permute-start.3
  15.8 0.0 collective-permute-done.1.refs_1_
  15.8 3.1 %collective-permute-done.2.refs_2_ = bf16[48,512]{1,0:T(8,128)(2,1)S(1)} collective-permute-done((bf16[48,512]{1,0:T(8,128)(2,1)S(1)}, bf16[48,512]{1,0:T(8,128)(2,1)S(1)}, u32[]{:S(2)}, u32[]{:S(2)}) %collective-permute-start.2) | collective-permute-done | bytes 49184 | tf_op jit(solution)/shard_map/ppermute | solution.py:226
  18.9 2.5 %collective-permute-done.3.refs_3_ = bf16[48,512]{1,0:T(8,128)(2,1)S(1)} collective-permute-done((bf16[48,512]{1,0:T(8,128)(2,1)S(1)}, bf16[48,512]{1,0:T(8,128)(2,1)S(1)}, u32[]{:S(2)}, u32[]{:S(2)}) %collective-permute-start.3) | collective-permute-done | bytes 49184 | tf_op jit(solution)/shard_map/ppermute | solution.py:226
  21.4 0.0 all-to-all-done
  21.4 0.4 act.1
  21.8 0.0 collective-permute-done.refs_1_.one
  21.8 1.5 %collective-permute-start.4 = (bf16[96,2048]{1,0:T(8,128)(2,1)S(1)}, bf16[96,2048]{1,0:T(8,128)(2,1)S(1)}, u32[]{:S(2)}, u32[]{:S(2)}) collective-permute-start(bf16[96,2048]{1,0:T(8,128)(2,1)S(1)} %pair.1), channel_id=1, source_target_pairs={{0,4},{1,3},{2,6},{3,1},{4,0},{5,7},{6,2},{7,5},{8,12},{9,11},{10,... | collective-permute-start | bytes 1179656 | tf_op jit(solution)/shard_map/ppermute | solution.py:231
  23.4 0.6 %collective-permute-start.5 = (bf16[192,512]{1,0:T(8,128)(2,1)S(1)}, bf16[192,512]{1,0:T(8,128)(2,1)S(1)}, u32[]{:S(2)}, u32[]{:S(2)}) collective-permute-start(bf16[192,512]{1,0:T(8,128)(2,1)S(1)} %parts.1.refs_0_), channel_id=1, source_target_pairs={{0,2},{1,5},{2,0},{3,7},{4,6},{5,1},{6,4},{7,3},{8,10},{9,13},{10,... | collective-permute-start | bytes 589832 | tf_op jit(solution)/shard_map/ppermute | solution.py:231
  24.0 2.5 %hold.1.weight = bf16[640,4096]{1,0:T(8,128)(2,1)S(1)} custom-call(bf16[640,4096]{1,0:T(8,128)(2,1)} %source), custom_call_target="tpu_custom_call" | custom-call | flops 1 | bytes 1 | tf_op jit(solution)/shard_map/hold/pallas_call | solution.py:298
  26.5 2.7 %collective-permute-done.5.refs_1_ = bf16[192,512]{1,0:T(8,128)(2,1)S(1)} collective-permute-done((bf16[192,512]{1,0:T(8,128)(2,1)S(1)}, bf16[192,512]{1,0:T(8,128)(2,1)S(1)}, u32[]{:S(2)}, u32[]{:S(2)}) %collective-permute-start.5) | collective-permute-done | bytes 196640 | tf_op jit(solution)/shard_map/ppermute | solution.py:231
  29.3 1.5 %collective-permute-done.4.two = bf16[96,2048]{1,0:T(8,128)(2,1)S(1)} collective-permute-done((bf16[96,2048]{1,0:T(8,128)(2,1)S(1)}, bf16[96,2048]{1,0:T(8,128)(2,1)S(1)}, u32[]{:S(2)}, u32[]{:S(2)}) %collective-permute-start.4) | collective-permute-done | bytes 393248 | tf_op jit(solution)/shard_map/ppermute | solution.py:231
  30.8 0.4 collective-permute-start.11
  31.2 0.0 collective-permute-start.7
  31.3 0.5 collective-permute-start.6
  31.8 0.0 collective-permute-start.8
  31.8 2.1 %collective-permute-start.9 = (bf16[192,640]{1,0:T(8,128)(2,1)S(1)}, bf16[192,640]{1,0:T(8,128)(2,1)S(1)}, u32[]{:S(2)}, u32[]{:S(2)}) collective-permute-start(bf16[192,640]{1,0:T(8,128)(2,1)S(1)} %get-tuple-element.42.act), channel_id=1, source_target_pairs={{0,16},{8,24},{16,0},{24,8},{1,17},{9,25},{17,1},{25,9},{2,18},{10... | collective-permute-start | bytes 737288 | tf_op jit(solution)/shard_map/ppermute | solution.py:226
  33.9 0.0 collective-permute-done.6.far_one
  33.9 0.0 collective-permute-start.12
  33.9 4.8 %collective-permute-done.11.two = bf16[384,512]{1,0:T(8,128)(2,1)S(1)} collective-permute-done((bf16[384,512]{1,0:T(8,128)(2,1)S(1)}, bf16[384,512]{1,0:T(8,128)(2,1)S(1)}, u32[]{:S(2)}, u32[]{:S(2)}) %collective-permute-start.11) | collective-permute-done | bytes 393248 | tf_op jit(solution)/shard_map/ppermute | solution.py:231
  38.7 0.0 collective-permute-start.13
  38.7 0.0 collective-permute-done.7.far_two
  38.7 2.9 %grad.1 = bf16[192,640]{1,0:T(8,128)(2,1)} custom-call(bf16[48,2048]{1,0:T(8,128)(2,1)S(1)} %get-tuple-element.34.refs_0_.mine, bf16[48,2048]{1,0:T(8,128)(2,1)S(1)} %collective-permute-done.refs_1_.one, bf16[96,2048]{1,0:T(8,128)(2,1)S(1)} %collective-permute-done.4.two, bf16[48,2048]{1,0:T(8,128)(2,1)S(1)} %get-tuple-element.51.other, ...), custom_call_target="tpu_custom_call" | custom-call | flops 1 | bytes 1 | tf_op jit(solution)/shard_map/grad/pallas_call | solution.py:317
  41.5 3.4 %collective-permute-done.8.refs_0_ = bf16[192,640]{1,0:T(8,128)(2,1)S(1)} collective-permute-done((bf16[192,640]{1,0:T(8,128)(2,1)S(1)}, bf16[192,640]{1,0:T(8,128)(2,1)S(1)}, u32[]{:S(2)}, u32[]{:S(2)}) %collective-permute-start.8) | collective-permute-done | bytes 245792 | tf_op jit(solution)/shard_map/ppermute | solution.py:226
  44.9 0.0 collective-permute-done.9.refs_1_
  44.9 1.5 %collective-permute-start.10 = (bf16[192,640]{1,0:T(8,128)(2,1)S(1)}, bf16[192,640]{1,0:T(8,128)(2,1)S(1)}, u32[]{:S(2)}, u32[]{:S(2)}) collective-permute-start(bf16[192,640]{1,0:T(8,128)(2,1)S(1)} %collective-permute-done.9.refs_1_), channel_id=1, source_target_pairs={{0,8},{8,0},{16,24},{24,16},{1,9},{9,1},{17,25},{25,17},{2,10},{10... | collective-permute-start | bytes 737288 | tf_op jit(solution)/shard_map/ppermute | solution.py:226
  46.4 3.4 %all-to-all-start.1 = ((bf16[8,24,640]{2,1,0:T(8,128)(2,1)}), bf16[8,24,640]{2,1,0:T(8,128)(2,1)S(1)}, u32[]{:S(2)}, u32[]{:S(2)}) async-start(bf16[8,24,640]{2,1,0:T(8,128)(2,1)} %bitcast.2), calls=%async_computation.1 | async-start | bytes 491520 | tf_op jit(solution)/shard_map/all_to_all | solution.py:331
  49.8 0.0 collective-permute-done.12.far_pair
  49.8 0.0 collective-permute-done.13.far_two
  49.8 1.1 %early.1 = (bf16[768,1024]{1,0:T(8,128)(2,1)S(1)}, f32[640,1024]{1,0:T(8,128)S(1)}, f32[1,1024]{1,0:T(1,128)}) custom-call(bf16[384,512]{1,0:T(8,128)(2,1)S(1)} %pair_part.1.pair, bf16[384,512]{1,0:T(8,128)(2,1)S(1)} %collective-permute-done.11.two, bf16[384,512]{1,0:T(8,128)(2,1)S(1)} %collective-permute-done.12.far_pair, ...), custom_call_target="tpu_custom_call" | custom-call | flops 1 | bytes 1 | tf_op jit(solution)/shard_map/early/pallas_call | solution.py:333
  50.9 1.0 %collective-permute-done.10.refs_2_ = bf16[192,640]{1,0:T(8,128)(2,1)S(1)} collective-permute-done((bf16[192,640]{1,0:T(8,128)(2,1)S(1)}, bf16[192,640]{1,0:T(8,128)(2,1)S(1)}, u32[]{:S(2)}, u32[]{:S(2)}) %collective-permute-start.10) | collective-permute-done | bytes 245792 | tf_op jit(solution)/shard_map/ppermute | solution.py:226
  51.9 2.5 %late.1 = f32[640,1024]{1,0:T(8,128)} custom-call(bf16[192,640]{1,0:T(8,128)(2,1)S(1)} %collective-permute-done.8.refs_0_, bf16[192,640]{1,0:T(8,128)(2,1)S(1)} %collective-permute-done.9.refs_1_, bf16[192,640]{1,0:T(8,128)(2,1)S(1)} %collective-permute-done.10.refs_2_, bf16[768,1024]{1,0:T(8,128)(2,1)S(1)} %get-tuple-element.58.refs_3_, ...), custom_call_target="tpu_custom_call" | custom-call | flops 1 | bytes 1 | tf_op jit(solution)/shard_map/late/pallas_call | solution.py:342
  54.4 2.1 %all-to-all-done.1 = bf16[8,24,640]{2,1,0:T(8,128)(2,1)S(1)} async-done(((bf16[8,24,640]{2,1,0:T(8,128)(2,1)}), bf16[8,24,640]{2,1,0:T(8,128)(2,1)S(1)}, u32[]{:S(2)}, u32[]{:S(2)}) %all-to-all-start.1) | async-done | bytes 245792 | tf_op jit(solution)/shard_map/all_to_all | solution.py:331
  56.5 0.7 %copy.10 = bf16[8,3,8,640]{3,2,0,1:T(8,128)(2,1)} copy(bf16[8,3,8,640]{3,2,1,0:T(8,128)(2,1)S(1)} %bitcast.8) | data formatting | bytes 491520 | tf_op jit(solution)/shard_map/reshape | solution.py:352
  (3 shorter events, 0.1 us)
Async XLA Ops:
  0.6 0.9 %copy-start = (bf16[24,5120]{1,0:T(8,128)(2,1)S(1)}, bf16[24,5120]{1,0:T(8,128)(2,1)}, u32[]{:S(2)}) copy-start(bf16[24,5120]{1,0:T(8,128)(2,1)} %pre.1) | copy-start | bytes 737284
  2.3 19.1 %all-to-all-start = ((bf16[8,24,640]{2,1,0:T(8,128)(2,1)}), bf16[8,24,640]{2,1,0:T(8,128)(2,1)S(1)}, u32[]{:S(2)}, u32[]{:S(2)}) async-start(bf16[8,24,640]{2,1,0:T(8,128)(2,1)} %cut.1), calls=%async_computation | async-start | bytes 491520 | tf_op jit(solution)/shard_map/all_to_all | solution.py:268
  9.3 12.5 %collective-permute-start = (bf16[48,2048]{1,0:T(8,128)(2,1)S(1)}, bf16[48,2048]{1,0:T(8,128)(2,1)S(1)}, u32[]{:S(2)}, u32[]{:S(2)}) collective-permute-start(bf16[48,2048]{1,0:T(8,128)(2,1)S(1)} %get-tuple-element.34.refs_0_.mine), channel_id=1, source_target_pairs={{0,2},{1,5},{2,0},{3,7},{4,6},{5,1},{6,4},{7,3},{8,10},{9,13},{10,... | collective-permute-start | bytes 589832 | tf_op jit(solution)/shard_map/ppermute | solution.py:231
  11.4 4.4 %collective-permute-start.1 = (bf16[48,512]{1,0:T(8,128)(2,1)S(1)}, bf16[48,512]{1,0:T(8,128)(2,1)S(1)}, u32[]{:S(2)}, u32[]{:S(2)}) collective-permute-start(bf16[48,512]{1,0:T(8,128)(2,1)S(1)} %get-tuple-element.38), channel_id=1, source_target_pairs={{0,8},{8,0},{16,24},{24,16},{1,9},{9,1},{17,25},{25,17},{2,10},{10... | collective-permute-start | bytes 147464 | tf_op jit(solution)/shard_map/ppermute | solution.py:226
  13.0 6.0 %collective-permute-start.2 = (bf16[48,512]{1,0:T(8,128)(2,1)S(1)}, bf16[48,512]{1,0:T(8,128)(2,1)S(1)}, u32[]{:S(2)}, u32[]{:S(2)}) collective-permute-start(bf16[48,512]{1,0:T(8,128)(2,1)S(1)} %get-tuple-element.39), channel_id=1, source_target_pairs={{0,16},{8,24},{16,0},{24,8},{1,17},{9,25},{17,1},{25,9},{2,18},{10... | collective-permute-start | bytes 147464 | tf_op jit(solution)/shard_map/ppermute | solution.py:226
  15.5 5.9 %collective-permute-start.3 = (bf16[48,512]{1,0:T(8,128)(2,1)S(1)}, bf16[48,512]{1,0:T(8,128)(2,1)S(1)}, u32[]{:S(2)}, u32[]{:S(2)}) collective-permute-start(bf16[48,512]{1,0:T(8,128)(2,1)S(1)} %get-tuple-element.40), channel_id=1, source_target_pairs={{0,24},{8,16},{16,8},{24,0},{1,25},{9,17},{17,9},{25,1},{2,26},{10... | collective-permute-start | bytes 147464 | tf_op jit(solution)/shard_map/ppermute | solution.py:226
  21.8 9.0 %collective-permute-start.4 = (bf16[96,2048]{1,0:T(8,128)(2,1)S(1)}, bf16[96,2048]{1,0:T(8,128)(2,1)S(1)}, u32[]{:S(2)}, u32[]{:S(2)}) collective-permute-start(bf16[96,2048]{1,0:T(8,128)(2,1)S(1)} %pair.1), channel_id=1, source_target_pairs={{0,4},{1,3},{2,6},{3,1},{4,0},{5,7},{6,2},{7,5},{8,12},{9,11},{10,... | collective-permute-start | bytes 1179656 | tf_op jit(solution)/shard_map/ppermute | solution.py:231
  23.4 5.9 %collective-permute-start.5 = (bf16[192,512]{1,0:T(8,128)(2,1)S(1)}, bf16[192,512]{1,0:T(8,128)(2,1)S(1)}, u32[]{:S(2)}, u32[]{:S(2)}) collective-permute-start(bf16[192,512]{1,0:T(8,128)(2,1)S(1)} %parts.1.refs_0_), channel_id=1, source_target_pairs={{0,2},{1,5},{2,0},{3,7},{4,6},{5,1},{6,4},{7,3},{8,10},{9,13},{10,... | collective-permute-start | bytes 589832 | tf_op jit(solution)/shard_map/ppermute | solution.py:231
  30.8 7.8 %collective-permute-start.11 = (bf16[384,512]{1,0:T(8,128)(2,1)S(1)}, bf16[384,512]{1,0:T(8,128)(2,1)S(1)}, u32[]{:S(2)}, u32[]{:S(2)}) collective-permute-start(bf16[384,512]{1,0:T(8,128)(2,1)S(1)} %pair_part.1.pair), channel_id=1, source_target_pairs={{0,4},{1,3},{2,6},{3,1},{4,0},{5,7},{6,2},{7,5},{8,12},{9,11},{10,... | collective-permute-start | bytes 1179656 | tf_op jit(solution)/shard_map/ppermute | solution.py:231
  31.2 7.4 %collective-permute-start.7 = (bf16[96,2048]{1,0:T(8,128)(2,1)S(1)}, bf16[96,2048]{1,0:T(8,128)(2,1)S(1)}, u32[]{:S(2)}, u32[]{:S(2)}) collective-permute-start(bf16[96,2048]{1,0:T(8,128)(2,1)S(1)} %collective-permute-done.4.two), channel_id=1, source_target_pairs={{0,1},{1,0},{2,3},{3,2},{4,5},{5,4},{6,7},{7,6},{8,9},{9,8},{10,11... | collective-permute-start | bytes 1179656 | tf_op jit(solution)/shard_map/ppermute | solution.py:226
  31.3 2.6 %collective-permute-start.6 = (bf16[48,2048]{1,0:T(8,128)(2,1)S(1)}, bf16[48,2048]{1,0:T(8,128)(2,1)S(1)}, u32[]{:S(2)}, u32[]{:S(2)}) collective-permute-start(bf16[48,2048]{1,0:T(8,128)(2,1)S(1)} %collective-permute-done.refs_1_.one), channel_id=1, source_target_pairs={{0,1},{1,0},{2,3},{3,2},{4,5},{5,4},{6,7},{7,6},{8,9},{9,8},{10,11... | collective-permute-start | bytes 589832 | tf_op jit(solution)/shard_map/ppermute | solution.py:226
  31.8 13.1 %collective-permute-start.8 = (bf16[192,640]{1,0:T(8,128)(2,1)S(1)}, bf16[192,640]{1,0:T(8,128)(2,1)S(1)}, u32[]{:S(2)}, u32[]{:S(2)}) collective-permute-start(bf16[192,640]{1,0:T(8,128)(2,1)S(1)} %get-tuple-element.42.act), channel_id=1, source_target_pairs={{0,8},{8,0},{16,24},{24,16},{1,9},{9,1},{17,25},{25,17},{2,10},{10... | collective-permute-start | bytes 737288 | tf_op jit(solution)/shard_map/ppermute | solution.py:226
  31.8 13.1 %collective-permute-start.9 = (bf16[192,640]{1,0:T(8,128)(2,1)S(1)}, bf16[192,640]{1,0:T(8,128)(2,1)S(1)}, u32[]{:S(2)}, u32[]{:S(2)}) collective-permute-start(bf16[192,640]{1,0:T(8,128)(2,1)S(1)} %get-tuple-element.42.act), channel_id=1, source_target_pairs={{0,16},{8,24},{16,0},{24,8},{1,17},{9,25},{17,1},{25,9},{2,18},{10... | collective-permute-start | bytes 737288 | tf_op jit(solution)/shard_map/ppermute | solution.py:226
  33.9 15.9 %collective-permute-start.12 = (bf16[384,512]{1,0:T(8,128)(2,1)S(1)}, bf16[384,512]{1,0:T(8,128)(2,1)S(1)}, u32[]{:S(2)}, u32[]{:S(2)}) collective-permute-start(bf16[384,512]{1,0:T(8,128)(2,1)S(1)} %pair_part.1.pair), channel_id=1, source_target_pairs={{0,1},{1,0},{2,3},{3,2},{4,5},{5,4},{6,7},{7,6},{8,9},{9,8},{10,11... | collective-permute-start | bytes 1179656 | tf_op jit(solution)/shard_map/ppermute | solution.py:226
  38.7 11.2 %collective-permute-start.13 = (bf16[384,512]{1,0:T(8,128)(2,1)S(1)}, bf16[384,512]{1,0:T(8,128)(2,1)S(1)}, u32[]{:S(2)}, u32[]{:S(2)}) collective-permute-start(bf16[384,512]{1,0:T(8,128)(2,1)S(1)} %collective-permute-done.11.two), channel_id=1, source_target_pairs={{0,1},{1,0},{2,3},{3,2},{4,5},{5,4},{6,7},{7,6},{8,9},{9,8},{10,11... | collective-permute-start | bytes 1179656 | tf_op jit(solution)/shard_map/ppermute | solution.py:226
  44.9 7.0 %collective-permute-start.10 = (bf16[192,640]{1,0:T(8,128)(2,1)S(1)}, bf16[192,640]{1,0:T(8,128)(2,1)S(1)}, u32[]{:S(2)}, u32[]{:S(2)}) collective-permute-start(bf16[192,640]{1,0:T(8,128)(2,1)S(1)} %collective-permute-done.9.refs_1_), channel_id=1, source_target_pairs={{0,8},{8,0},{16,24},{24,16},{1,9},{9,1},{17,25},{25,17},{2,10},{10... | collective-permute-start | bytes 737288 | tf_op jit(solution)/shard_map/ppermute | solution.py:226
  46.4 10.1 %all-to-all-start.1 = ((bf16[8,24,640]{2,1,0:T(8,128)(2,1)}), bf16[8,24,640]{2,1,0:T(8,128)(2,1)S(1)}, u32[]{:S(2)}, u32[]{:S(2)}) async-start(bf16[8,24,640]{2,1,0:T(8,128)(2,1)} %bitcast.2), calls=%async_computation.1 | async-start | bytes 491520 | tf_op jit(solution)/shard_map/all_to_all | solution.py:331

commit v3 on v2

--- a/solution.py
+++ b/solution.py
@@ -115,9 +115,9 @@
     there[...] = (stream_row == received((rows, 1), 0)).astype(F32).astype(BF16)
 
 
-def pick_kernel(n_dp, n_ctx, *refs):
-    inputs, (mine, other, there, back), parts = refs[:4], refs[4:8], refs[8 : 8 + n_dp]
-    local, (chosen, sems) = refs[8 + n_dp : 12 + n_dp], refs[12 + n_dp :]
+def pick_kernel(n_ctx, *refs):
+    inputs, (chosen, there, back), parts = refs[:4], refs[4:7], refs[7:10]
+    local, sems = refs[10:14], refs[14]
     llm, places, counts, order = local
     group, ctx, core = (lax.axis_index(a) for a in ("dp", "ctx", "mp"))
     copies = [pltpu.make_async_copy(a, b, sems.at[i]) for i, (a, b) in enumerate(zip(inputs, local))]
@@ -130,12 +130,11 @@
     hot = (lax.broadcasted_iota(jnp.int32, (llm.shape[0], own.shape[1]), 0) == own).astype(BF16)
     copies[0].wait()
     chosen[...] = lax.dot_general(hot, llm[...], (((0,), (0,)), ((), ())), preferred_element_type=F32).astype(BF16)
-    half = mine.shape[1]
-    mine[...] = chosen[:, pl.ds(pl.multiple_of(core * half, half), half)]
-    other[...] = chosen[:, pl.ds(pl.multiple_of((1 - core) * half, half), half)]
-    for i, part in enumerate(parts):
-        wide = part.shape[1]
-        part[...] = chosen[:, pl.ds(pl.multiple_of((2 * (group ^ i) + core) * wide, wide), wide)]
+    wide = parts[0].shape[1]
+    for out, distances in zip(parts, ((0,), (2,), (1, 3))):
+        for i, far in enumerate(distances):
+            at = pl.ds(pl.multiple_of((2 * (group ^ far) + core) * wide, wide), wide)
+            out[i * chosen.shape[0] : (i + 1) * chosen.shape[0]] = chosen[:, at]
 
 
 def act_kernel(there, pre, act, slope):
@@ -145,11 +144,20 @@
     slope[...] = grade
 
 
-def stack_kernel(*refs):
+def stack_kernel(starts, *refs):
     parts, out = refs[:-1], refs[-1]
-    rows = parts[0].shape[0]
-    for i, part in enumerate(parts):
-        out[i * rows : (i + 1) * rows] = part[...]
+    at = 0
+    for part, start in zip(parts, starts):
+        rows = part.shape[0] - start
+        out[at : at + rows] = part[start:]
+        at += rows
+
+
+def spread_kernel(keep, first, second, out):
+    rows = keep.shape[0]
+    out[:rows] = keep[...]
+    out[rows : 2 * rows] = first[:rows]
+    out[2 * rows :] = second[...]
 
 
 def hold_kernel(source, out, sem):
@@ -158,37 +166,28 @@
     copy.wait()
 
 
-def spots(core):
-    return (0, 1 + core, 2 - core, 3)
-
-
-def grad_kernel(mine, one, two, other, far_one, far_two, weight, slope, back, out, rows):
+def grad_kernel(mine, one, two, weight, slope, back, out, rows):
     core = lax.axis_index("mp")
-    block, half = mine.shape
-
-    for side, own, first, second in ((core, mine, one, two), (1 - core, other, far_one, far_two)):
-        columns = pl.ds(pl.multiple_of(side * half, half), half)
-        pieces = (own[...], first[...], second[:block], second[block:])
-        for spot, piece in zip(spots(side), pieces):
-            rows[pl.ds(pl.multiple_of(spot * block, block), block), columns] = piece
-
+    block = mine.shape[0]
+    pieces = (mine[...], one[...], two[:block], two[block:])
+    for spot, piece in zip((0, 1 + core, 2 - core, 3), pieces):
+        rows[pl.ds(pl.multiple_of(spot * block, block), block)] = piece
     grad = lax.dot_general(rows[...], weight[...], (((1,), (1,)), ((), ())), preferred_element_type=F32)
     grad = (grad * slope[...]).astype(BF16)
     out[...] = jnp.dot(back[...], grad, preferred_element_type=F32).astype(BF16)
 
 
-def early_kernel(n_dp, pair, two, far_pair, far_two, act, right, total, bias):
+def early_kernel(n_dp, n_ctx, *refs):
+    near, far, (act, right, total, bias) = refs[:n_ctx], refs[n_ctx : 2 * n_ctx], refs[2 * n_ctx :]
     core = lax.axis_index("mp")
-    rows, half = pair.shape[0] // 2, pair.shape[1]
+    rows, half = near[0].shape
     block = rows // n_dp
-    for side, first, second in ((core, pair, two), (1 - core, far_pair, far_two)):
+    for side, pieces in ((core, near), (1 - core, far)):
         columns = pl.ds(pl.multiple_of(side * half, half), half)
-        for at, spot in enumerate(spots(side)):
-            piece = (first, second)[at // 2]
+        for k, piece in enumerate(pieces):
             for i in range(n_dp):
-                to = (i * len(spots(0)) + spot) * block
-                start = (at % 2) * rows + i * block
-                right[pl.ds(pl.multiple_of(to, block), block), columns] = piece[start : start + block]
+                to = (i * n_ctx + k) * block
+                right[to : to + block, columns] = piece[i * block : (i + 1) * block]
     ones = jnp.ones((8, right.shape[0]), BF16)
     bias[...] = jnp.dot(ones, right[...], preferred_element_type=F32)[:1]
     total[...] = lax.dot_general(
@@ -211,14 +210,11 @@
     return jax.ShapeDtypeStruct(shape, dtype)
 
 
-def limits(mebibytes):
+def limits(mebibytes, cost=1):
     return dict(
         compiler_params=pltpu.CompilerParams(vmem_limit_bytes=mebibytes << 20),
-        cost_estimate=pl.CostEstimate(flops=COST, bytes_accessed=COST, transcendentals=0),
-    )
-
-
-COST = 1
+        cost_estimate=pl.CostEstimate(flops=cost, bytes_accessed=cost, transcendentals=0),
+    )
 
 
 def swap(x, axis, k):
@@ -226,19 +222,19 @@
     return lax.ppermute(x, axis, [(i, i ^ k) for i in range(n)])
 
 
+def pinned(x):
+    return pltpu.with_memory_space_constraint(x, pltpu.HBM)
+
+
 def round_plane(x, step):
     pairs = [(2 * c + m, 2 * (c ^ (1 << (m ^ step))) + m) for c in range(4) for m in range(2)]
     return lax.ppermute(x, ("ctx", "mp"), pairs)
 
 
-def pinned(x):
-    return pltpu.with_memory_space_constraint(x, pltpu.HBM)
-
-
-def stacked(parts, name):
+def stacked(kernel, parts, rows, name):
     return pl.pallas_call(
-        stack_kernel,
-        out_shape=struct((len(parts) * parts[0].shape[0], parts[0].shape[1])),
+        kernel,
+        out_shape=struct((rows, parts[0].shape[1])),
         in_specs=[VMEM] * len(parts),
         out_specs=VMEM,
         name=name,
@@ -268,33 +264,35 @@
     pre = lax.all_to_all(blocks, ("ctx", "mp"), 0, 0, tiled=True).reshape(rows, hid)
 
     inputs = (llm_grad, vision_rows, jnp.swapaxes(patch_counts, 1, 2), image_order)
-    mine, other, there, back, *parts = pl.pallas_call(
-        functools.partial(pick_kernel, n_dp, n_ctx),
-        out_shape=(struct((block, feat // 2)),) * 2
+    mine, there, back, keep, pass_on, send = pl.pallas_call(
+        functools.partial(pick_kernel, n_ctx),
+        out_shape=(struct((block, feat)),)
         + (struct((rows, rows)),) * 2
-        + (struct((block, cols // 2)),) * n_dp,
+        + (struct((block, cols // 2)),) * 2
+        + (struct((2 * block, cols // 2)),),
         in_specs=[HBM] * 4,
-        out_specs=(VMEM,) * (4 + n_dp),
+        out_specs=(VMEM,) * 6,
         scratch_shapes=[pltpu.VMEM(x.shape, x.dtype) for x in inputs]
-        + [pltpu.VMEM((block, feat), BF16), pltpu.SemaphoreType.DMA((4,))],
+        + [pltpu.SemaphoreType.DMA((4,))],
         name="pick",
         **limits(8),
     )(*(pinned(x) for x in inputs))
 
-    parts = [parts[0]] + [swap(parts[k], "dp", k) for k in range(1, n_dp)]
     one = round_plane(mine, 0)
-    pre, *parts = lax.optimization_barrier((pre, *parts))
+    first = swap(send, "dp", 1)
     act, slope = pl.pallas_call(
         act_kernel,
         out_shape=(struct((rows, hid)), struct((rows, hid), F32)),
         in_specs=[VMEM] * 2,
         out_specs=(VMEM,) * 2,
         name="act",
-        **limits(4),
+        **limits(4, 1),
     )(there, pre)
     acts = {0: act} | {k: swap(act, "dp", k) for k in range(1, n_dp) if k & (k - 1) == 0}
-    out_weight, one, _ = lax.optimization_barrier((out_weight, one, act))
-    two = round_plane(stacked((mine, one), "pair"), 1)
+    out_weight, one, first, _ = lax.optimization_barrier((out_weight, one, first, act))
+    two = round_plane(stacked(functools.partial(stack_kernel, (0, 0)), (mine, one), 2 * block, "pair"), 1)
+    second = stacked(functools.partial(stack_kernel, (0, block)), (pass_on, first), 2 * block, "pass_on")
+    second = swap(second, "dp", 2)
     held = pl.pallas_call(
         hold_kernel,
         out_shape=struct(out_weight.shape),
@@ -305,24 +303,20 @@
         **limits(8),
     )(pinned(out_weight))
 
-    split = stacked(parts, "parts")
-    one_part = round_plane(split, 0)
-    one, two, held, split, one_part = lax.optimization_barrier((one, two, held, split, one_part))
-    far_one, far_two = swap(one, "mp", 1), swap(two, "mp", 1)
-    pair = stacked((split, one_part), "pair_part")
-    far_pair = swap(pair, "mp", 1)
-    two_part = round_plane(pair, 1)
-    far_two_part = swap(two_part, "mp", 1)
+    second, held = lax.optimization_barrier((second, held))
+    split = stacked(spread_kernel, (keep, first, second), n_dp * block, "parts")
+    near_part = [split] + [swap(split, "ctx", k) for k in range(1, n_ctx)]
+    far_part = [swap(x, "mp", 1) for x in near_part]
 
     grad = pl.pallas_call(
         grad_kernel,
         out_shape=struct((rows, hid)),
-        in_specs=[VMEM] * 9,
+        in_specs=[VMEM] * 6,
         out_specs=VMEM,
         scratch_shapes=[pltpu.VMEM((rows, feat), BF16)],
         name="grad",
         **limits(8),
-    )(mine, one, two, other, far_one, far_two, held, slope, back)
+    )(mine, one, two, held, slope, back)
     relay, _ = lax.optimization_barrier(([acts[k] for k in sorted(acts)], grad))
     relay = dict(zip(sorted(acts), relay))
     for k in range(n_dp):
@@ -331,13 +325,13 @@
     returned = lax.all_to_all(grad.reshape(images, vit, hid), ("ctx", "mp"), 0, 0, tiled=True)
 
     right, total, bias_grad = pl.pallas_call(
-        functools.partial(early_kernel, n_dp),
+        functools.partial(early_kernel, n_dp, n_ctx),
         out_shape=(struct((n_dp * rows, cols)), struct((hid, cols), F32), struct((1, cols), F32)),
-        in_specs=[VMEM] * 5,
+        in_specs=[VMEM] * (2 * n_ctx + 1),
         out_specs=(VMEM,) * 3,
         name="early",
         **limits(12),
-    )(pair, two_part, far_pair, far_two_part, act)
+    )(*near_part, *far_part, act)
     wide = cols // 2
     weight_grad = pl.pallas_call(
         late_kernel,
@@ -369,7 +363,7 @@
         rows = args[1].shape[0] * n_ctx * n_mp
         gather = (n_dp - 1) * rows * (hid + feat // n_dp) * 2
         scatter = hid * feat * 4 * (n_dp - 1) // n_dp
-        fits = n_mp == 2 and n_ctx == 4 and n_dp & (n_dp - 1) == 0 and n_dp > 1
+        fits = (n_dp, n_ctx, n_mp) == (4, 4, 2)
         return (gathered if fits and gather < scatter else reduced)(*args)
 
     return jax.shard_map(

time: 57.6 us -> 48.7 us (0.85)
  waiting for transfers between devices: 21.2 us -> 11.1 us
  starting transfers between devices: 21.8 us -> 22.9 us
    ppermute x10 -> x12, waiting for transfers between devices: 10 us -> 1.33 us  [swap(): return lax.ppermute(x, axis, [(i, i ^ k) for i in range(n)])]
    all_to_all x1, waiting for transfers between devices: 0.01 us -> 5.05 us  [gathered(): lax.all_to_all(blocks, ('ctx', 'mp'), 0, 0, tiled=True).reshape(rows, hid)]
    ppermute x4 -> x2, waiting for transfers between devices: 9.05 us -> 4.1 us  [round_plane(): return lax.ppermute(x, ('ctx', 'mp'), pairs)]
    ppermute x10 -> x12, starting transfers between devices: 8.54 us -> 12.5 us  [swap(): return lax.ppermute(x, axis, [(i, i ^ k) for i in range(n)])]
    all_to_all x1, starting transfers between devices: 5.18 us -> 3.41 us  [gathered(): lax.all_to_all(blocks, ('ctx', 'mp'), 0, 0, tiled=True).reshape(rows, hid)]
    all_to_all x1, waiting for transfers between devices: 2.1 us -> 0.62 us  [gathered(): lax.all_to_all(grad.reshape(images, vit, hid), ('ctx', 'mp'), 0, 0, tiled...]
    ppermute x4 -> x2, starting transfers between devices: 4.67 us -> 3.6 us  [round_plane(): return lax.ppermute(x, ('ctx', 'mp'), pairs)]
  transfers between devices with their start and end apart: 16 -> 16, of which waited for: 8 -> 7; matrix products, arithmetic and copies ran while one was open for 0% -> 0% of each run, Pallas kernels for 19% -> 19%
where the time goes in v3:
time: 48.7 us; the launch traced here: 48.3 us
  starting transfers between devices  22.9 us (47%)
  Pallas kernels  11.9 us (24%)
  waiting for transfers between devices  11.1 us (23%)
  local copies, waits for them, and re-layouts  1.65 us (3%)
  between operations  0.74 us (2%)
    ppermute x12, starting transfers between devices, swap(): return lax.ppermute(x, axis, [(i, i ^ k) for i in range(n)])  12.5 us
    all_to_all x1, waiting for transfers between devices, gathered(): lax.all_to_all(blocks, ('ctx', 'mp'), 0, 0, tiled=True).reshape(rows, hid)  5.05 us
    ppermute x2, waiting for transfers between devices, round_plane(): return lax.ppermute(x, ('ctx', 'mp'), pairs)  4.1 us
    ppermute x2, starting transfers between devices, round_plane(): return lax.ppermute(x, ('ctx', 'mp'), pairs)  3.6 us
    all_to_all x1, starting transfers between devices, gathered(): lax.all_to_all(grad.reshape(images, vit, hid), ('ctx', 'mp'), 0, 0, tiled...  3.41 us
    all_to_all x1, starting transfers between devices, gathered(): lax.all_to_all(blocks, ('ctx', 'mp'), 0, 0, tiled=True).reshape(rows, hid)  3.41 us
    pallas_call x1, Pallas kernels, gathered(): pl.pallas_call(grad_kernel, out_shape=struct((rows, hid)), in_specs=[VMEM...  2.81 us
    pallas_call x1, Pallas kernels, gathered(): pl.pallas_call(late_kernel, out_shape=struct((hid, cols), F32), grid=(col...  2.5 us
  transfers between devices with their start and end apart: 16, of which 7 were waited for; matrix products, arithmetic and copies ran while one was open for 0% of the time, Pallas kernels for 19%

profile of v3, /device:TPU:0, one launch (start us, length us, event | category | flops | bytes accessed | tf_op | source)
XLA Modules:
  0.0 48.3 jit_solution(17032360269674819827)
XLA Ops:
  0.6 0.0 copy-start
  0.6 0.9 %copy-done = bf16[24,5120]{1,0:T(8,128)(2,1)S(1)} copy-done((bf16[24,5120]{1,0:T(8,128)(2,1)S(1)}, bf16[24,5120]{1,0:T(8,128)(2,1)}, u32[]{:S(2)}) %copy-start) | copy-done | bytes 245784
  1.6 0.7 %cut.1 = bf16[8,24,640]{2,1,0:T(8,128)(2,1)} custom-call(bf16[24,5120]{1,0:T(8,128)(2,1)S(1)} %copy-done), custom_call_target="tpu_custom_call" | custom-call | flops 1 | bytes 1 | tf_op jit(solution)/shard_map/cut/pallas_call | solution.py:254
  2.3 1.7 %pick.1 = (bf16[48,4096]{1,0:T(8,128)(2,1)S(1)}, bf16[192,192]{1,0:T(8,128)(2,1)S(1)}, bf16[192,192]{1,0:T(8,128)(2,1)S(1)}, bf16[48,512]{1,0:T(8,128)(2,1)S(1)}...) custom-call(bf16[128,4096]{1,0:T(8,128)(2,1)} %refs_0_, s32[1,4,48]{2,1,0:T(4,128)} %refs_1_.1, ...), custom_call_target="tpu_custom_call" | custom-call | flops 1 | bytes 1 | tf_op jit(solution)/shard_map/pick/pallas_call | solution.py:267
  4.1 3.0 %collective-permute-start = (bf16[48,4096]{1,0:T(8,128)(2,1)S(1)}, bf16[48,4096]{1,0:T(8,128)(2,1)S(1)}, u32[]{:S(2)}, u32[]{:S(2)}) collective-permute-start(bf16[48,4096]{1,0:T(8,128)(2,1)S(1)} %get-tuple-element.25.refs_0_.mine), channel_id=1, source_target_pairs={{0,2},{1,5},{2,0},{3,7},{4,6},{5,1},{6,4},{7,3},{8,10},{9,13},{10,... | collective-permute-start | bytes 1179656 | tf_op jit(solution)/shard_map/ppermute | solution.py:231
  7.1 3.4 %all-to-all-start = ((bf16[8,24,640]{2,1,0:T(8,128)(2,1)}), bf16[8,24,640]{2,1,0:T(8,128)(2,1)S(1)}, u32[]{:S(2)}, u32[]{:S(2)}) async-start(bf16[8,24,640]{2,1,0:T(8,128)(2,1)} %cut.1), calls=%async_computation | async-start | bytes 491520 | tf_op jit(solution)/shard_map/all_to_all | solution.py:264
  10.5 1.6 %collective-permute-start.1 = (bf16[96,512]{1,0:T(8,128)(2,1)S(1)}, bf16[96,512]{1,0:T(8,128)(2,1)S(1)}, u32[]{:S(2)}, u32[]{:S(2)}) collective-permute-start(bf16[96,512]{1,0:T(8,128)(2,1)S(1)} %get-tuple-element.26), channel_id=1, source_target_pairs={{0,8},{8,0},{16,24},{24,16},{1,9},{9,1},{17,25},{25,17},{2,10},{10... | collective-permute-start | bytes 294920 | tf_op jit(solution)/shard_map/ppermute | solution.py:222
  12.1 5.0 %all-to-all-done = bf16[8,24,640]{2,1,0:T(8,128)(2,1)S(1)} async-done(((bf16[8,24,640]{2,1,0:T(8,128)(2,1)}), bf16[8,24,640]{2,1,0:T(8,128)(2,1)S(1)}, u32[]{:S(2)}, u32[]{:S(2)}) %all-to-all-start) | async-done | bytes 245792 | tf_op jit(solution)/shard_map/all_to_all | solution.py:264
  17.2 0.4 act.1
  17.6 0.0 collective-permute-done.1.refs_1_.first
  17.6 0.0 collective-permute-done.refs_1_.one
  17.6 0.1 pair.1
  17.6 0.6 %collective-permute-start.2 = (bf16[96,4096]{1,0:T(8,128)(2,1)S(1)}, bf16[96,4096]{1,0:T(8,128)(2,1)S(1)}, u32[]{:S(2)}, u32[]{:S(2)}) collective-permute-start(bf16[96,4096]{1,0:T(8,128)(2,1)S(1)} %pair.1), channel_id=1, source_target_pairs={{0,4},{1,3},{2,6},{3,1},{4,0},{5,7},{6,2},{7,5},{8,12},{9,11},{10,... | collective-permute-start | bytes 2359304 | tf_op jit(solution)/shard_map/ppermute | solution.py:231
  18.2 2.7 %collective-permute-start.3 = (bf16[96,512]{1,0:T(8,128)(2,1)S(1)}, bf16[96,512]{1,0:T(8,128)(2,1)S(1)}, u32[]{:S(2)}, u32[]{:S(2)}) collective-permute-start(bf16[96,512]{1,0:T(8,128)(2,1)S(1)} %pass_on.1), channel_id=1, source_target_pairs={{0,16},{8,24},{16,0},{24,8},{1,17},{9,25},{17,1},{25,9},{2,18},{10... | collective-permute-start | bytes 294920 | tf_op jit(solution)/shard_map/ppermute | solution.py:222
  20.9 1.6 %collective-permute-start.4 = (bf16[192,640]{1,0:T(8,128)(2,1)S(1)}, bf16[192,640]{1,0:T(8,128)(2,1)S(1)}, u32[]{:S(2)}, u32[]{:S(2)}) collective-permute-start(bf16[192,640]{1,0:T(8,128)(2,1)S(1)} %get-tuple-element.29.refs_8_), channel_id=1, source_target_pairs={{0,8},{8,0},{16,24},{24,16},{1,9},{9,1},{17,25},{25,17},{2,10},{10... | collective-permute-start | bytes 737288 | tf_op jit(solution)/shard_map/ppermute | solution.py:222
  22.5 0.3 collective-permute-start.5
  22.8 2.5 %hold.1.weight = bf16[640,4096]{1,0:T(8,128)(2,1)S(1)} custom-call(bf16[640,4096]{1,0:T(8,128)(2,1)} %source), custom_call_target="tpu_custom_call" | custom-call | flops 1 | bytes 1 | tf_op jit(solution)/shard_map/hold/pallas_call | solution.py:296
  25.3 0.0 collective-permute-done.3.second
  25.3 1.4 %collective-permute-start.7 = (bf16[192,512]{1,0:T(8,128)(2,1)S(1)}, bf16[192,512]{1,0:T(8,128)(2,1)S(1)}, u32[]{:S(2)}, u32[]{:S(2)}) collective-permute-start(bf16[192,512]{1,0:T(8,128)(2,1)S(1)} %parts.1.refs_0_), channel_id=1, source_target_pairs={{0,2},{2,0},{4,6},{6,4},{1,3},{3,1},{5,7},{7,5},{8,10},{10,8},{12,... | collective-permute-start | bytes 589832 | tf_op jit(solution)/shard_map/ppermute | solution.py:222
  26.7 1.1 %collective-permute-start.8 = (bf16[192,512]{1,0:T(8,128)(2,1)S(1)}, bf16[192,512]{1,0:T(8,128)(2,1)S(1)}, u32[]{:S(2)}, u32[]{:S(2)}) collective-permute-start(bf16[192,512]{1,0:T(8,128)(2,1)S(1)} %parts.1.refs_0_), channel_id=1, source_target_pairs={{0,4},{2,6},{4,0},{6,2},{1,5},{3,7},{5,1},{7,3},{8,12},{10,14},{12... | collective-permute-start | bytes 589832 | tf_op jit(solution)/shard_map/ppermute | solution.py:222
  27.8 4.1 %collective-permute-done.2.two = bf16[96,4096]{1,0:T(8,128)(2,1)S(1)} collective-permute-done((bf16[96,4096]{1,0:T(8,128)(2,1)S(1)}, bf16[96,4096]{1,0:T(8,128)(2,1)S(1)}, u32[]{:S(2)}, u32[]{:S(2)}) %collective-permute-start.2) | collective-permute-done | bytes 786464 | tf_op jit(solution)/shard_map/ppermute | solution.py:231
  31.9 1.1 %collective-permute-start.9 = (bf16[192,512]{1,0:T(8,128)(2,1)S(1)}, bf16[192,512]{1,0:T(8,128)(2,1)S(1)}, u32[]{:S(2)}, u32[]{:S(2)}) collective-permute-start(bf16[192,512]{1,0:T(8,128)(2,1)S(1)} %parts.1.refs_0_), channel_id=1, source_target_pairs={{0,6},{2,4},{4,2},{6,0},{1,7},{3,5},{5,3},{7,1},{8,14},{10,12},{12... | collective-permute-start | bytes 589832 | tf_op jit(solution)/shard_map/ppermute | solution.py:222
  33.0 2.8 %grad.1 = bf16[192,640]{1,0:T(8,128)(2,1)} custom-call(bf16[48,4096]{1,0:T(8,128)(2,1)S(1)} %get-tuple-element.25.refs_0_.mine, bf16[48,4096]{1,0:T(8,128)(2,1)S(1)} %collective-permute-done.refs_1_.one, bf16[96,4096]{1,0:T(8,128)(2,1)S(1)} %collective-permute-done.2.two, bf16[640,4096]{1,0:T(8,128)(2,1)S(1)} %hold.1.weight, ...), custom_call_target="tpu_custom_call" | custom-call | flops 1 | bytes 1 | tf_op jit(solution)/shard_map/grad/pallas_call | solution.py:311
  35.8 0.0 collective-permute-done.4.refs_0_
  35.8 0.0 collective-permute-done.5.refs_1_
  35.8 1.6 %collective-permute-start.6 = (bf16[192,640]{1,0:T(8,128)(2,1)S(1)}, bf16[192,640]{1,0:T(8,128)(2,1)S(1)}, u32[]{:S(2)}, u32[]{:S(2)}) collective-permute-start(bf16[192,640]{1,0:T(8,128)(2,1)S(1)} %collective-permute-done.5.refs_1_), channel_id=1, source_target_pairs={{0,8},{8,0},{16,24},{24,16},{1,9},{9,1},{17,25},{25,17},{2,10},{10... | collective-permute-start | bytes 737288 | tf_op jit(solution)/shard_map/ppermute | solution.py:222
  37.5 3.4 %all-to-all-start.1 = ((bf16[8,24,640]{2,1,0:T(8,128)(2,1)}), bf16[8,24,640]{2,1,0:T(8,128)(2,1)S(1)}, u32[]{:S(2)}, u32[]{:S(2)}) async-start(bf16[8,24,640]{2,1,0:T(8,128)(2,1)} %bitcast.2), calls=%async_computation.1 | async-start | bytes 491520 | tf_op jit(solution)/shard_map/all_to_all | solution.py:325
  40.9 0.4 collective-permute-start.10
  41.3 0.0 collective-permute-done.7.refs_1_
  41.3 0.2 collective-permute-start.11
  41.4 0.0 collective-permute-done.8.refs_2_
  41.5 0.3 collective-permute-start.12
  41.8 0.0 collective-permute-done.9.refs_3_
  41.8 0.2 collective-permute-start.13
  42.0 0.4 collective-permute-done.10.refs_4_
  42.4 0.3 collective-permute-done.11.refs_5_
  42.7 0.3 collective-permute-done.12.refs_6_
  43.0 0.3 collective-permute-done.13.refs_7_
  43.3 1.2 %early.1 = (bf16[768,1024]{1,0:T(8,128)(2,1)S(1)}, f32[640,1024]{1,0:T(8,128)S(1)}, f32[1,1024]{1,0:T(1,128)}) custom-call(bf16[192,512]{1,0:T(8,128)(2,1)S(1)} %parts.1.refs_0_, bf16[192,512]{1,0:T(8,128)(2,1)S(1)} %collective-permute-done.7.refs_1_, bf16[192,512]{1,0:T(8,128)(2,1)S(1)} %collective-permute-done.8.refs_2_, ...), custom_call_target="tpu_custom_call" | custom-call | flops 1 | bytes 1 | tf_op jit(solution)/shard_map/early/pallas_call | solution.py:327
  44.4 0.0 collective-permute-done.6.refs_2_
  44.4 2.5 %late.1 = f32[640,1024]{1,0:T(8,128)} custom-call(bf16[192,640]{1,0:T(8,128)(2,1)S(1)} %collective-permute-done.4.refs_0_, bf16[192,640]{1,0:T(8,128)(2,1)S(1)} %collective-permute-done.5.refs_1_, bf16[192,640]{1,0:T(8,128)(2,1)S(1)} %collective-permute-done.6.refs_2_, bf16[768,1024]{1,0:T(8,128)(2,1)S(1)} %get-tuple-element.40.refs_3_, ...), custom_call_target="tpu_custom_call" | custom-call | flops 1 | bytes 1 | tf_op jit(solution)/shard_map/late/pallas_call | solution.py:336
  46.9 0.6 %all-to-all-done.1 = bf16[8,24,640]{2,1,0:T(8,128)(2,1)S(1)} async-done(((bf16[8,24,640]{2,1,0:T(8,128)(2,1)}), bf16[8,24,640]{2,1,0:T(8,128)(2,1)S(1)}, u32[]{:S(2)}, u32[]{:S(2)}) %all-to-all-start.1) | async-done | bytes 245792 | tf_op jit(solution)/shard_map/all_to_all | solution.py:325
  47.6 0.7 %copy.10 = bf16[8,3,8,640]{3,2,0,1:T(8,128)(2,1)} copy(bf16[8,3,8,640]{3,2,1,0:T(8,128)(2,1)S(1)} %bitcast.8) | data formatting | bytes 491520 | tf_op jit(solution)/shard_map/reshape | solution.py:346
  (2 shorter events, 0.0 us)
Async XLA Ops:
  0.6 0.9 %copy-start = (bf16[24,5120]{1,0:T(8,128)(2,1)S(1)}, bf16[24,5120]{1,0:T(8,128)(2,1)}, u32[]{:S(2)}) copy-start(bf16[24,5120]{1,0:T(8,128)(2,1)} %pre.1) | copy-start | bytes 737284
  4.1 13.5 %collective-permute-start = (bf16[48,4096]{1,0:T(8,128)(2,1)S(1)}, bf16[48,4096]{1,0:T(8,128)(2,1)S(1)}, u32[]{:S(2)}, u32[]{:S(2)}) collective-permute-start(bf16[48,4096]{1,0:T(8,128)(2,1)S(1)} %get-tuple-element.25.refs_0_.mine), channel_id=1, source_target_pairs={{0,2},{1,5},{2,0},{3,7},{4,6},{5,1},{6,4},{7,3},{8,10},{9,13},{10,... | collective-permute-start | bytes 1179656 | tf_op jit(solution)/shard_map/ppermute | solution.py:231
  7.1 10.1 %all-to-all-start = ((bf16[8,24,640]{2,1,0:T(8,128)(2,1)}), bf16[8,24,640]{2,1,0:T(8,128)(2,1)S(1)}, u32[]{:S(2)}, u32[]{:S(2)}) async-start(bf16[8,24,640]{2,1,0:T(8,128)(2,1)} %cut.1), calls=%async_computation | async-start | bytes 491520 | tf_op jit(solution)/shard_map/all_to_all | solution.py:264
  10.5 7.1 %collective-permute-start.1 = (bf16[96,512]{1,0:T(8,128)(2,1)S(1)}, bf16[96,512]{1,0:T(8,128)(2,1)S(1)}, u32[]{:S(2)}, u32[]{:S(2)}) collective-permute-start(bf16[96,512]{1,0:T(8,128)(2,1)S(1)} %get-tuple-element.26), channel_id=1, source_target_pairs={{0,8},{8,0},{16,24},{24,16},{1,9},{9,1},{17,25},{25,17},{2,10},{10... | collective-permute-start | bytes 294920 | tf_op jit(solution)/shard_map/ppermute | solution.py:222
  17.6 14.3 %collective-permute-start.2 = (bf16[96,4096]{1,0:T(8,128)(2,1)S(1)}, bf16[96,4096]{1,0:T(8,128)(2,1)S(1)}, u32[]{:S(2)}, u32[]{:S(2)}) collective-permute-start(bf16[96,4096]{1,0:T(8,128)(2,1)S(1)} %pair.1), channel_id=1, source_target_pairs={{0,4},{1,3},{2,6},{3,1},{4,0},{5,7},{6,2},{7,5},{8,12},{9,11},{10,... | collective-permute-start | bytes 2359304 | tf_op jit(solution)/shard_map/ppermute | solution.py:231
  18.2 7.1 %collective-permute-start.3 = (bf16[96,512]{1,0:T(8,128)(2,1)S(1)}, bf16[96,512]{1,0:T(8,128)(2,1)S(1)}, u32[]{:S(2)}, u32[]{:S(2)}) collective-permute-start(bf16[96,512]{1,0:T(8,128)(2,1)S(1)} %pass_on.1), channel_id=1, source_target_pairs={{0,16},{8,24},{16,0},{24,8},{1,17},{9,25},{17,1},{25,9},{2,18},{10... | collective-permute-start | bytes 294920 | tf_op jit(solution)/shard_map/ppermute | solution.py:222
  20.9 14.9 %collective-permute-start.4 = (bf16[192,640]{1,0:T(8,128)(2,1)S(1)}, bf16[192,640]{1,0:T(8,128)(2,1)S(1)}, u32[]{:S(2)}, u32[]{:S(2)}) collective-permute-start(bf16[192,640]{1,0:T(8,128)(2,1)S(1)} %get-tuple-element.29.refs_8_), channel_id=1, source_target_pairs={{0,8},{8,0},{16,24},{24,16},{1,9},{9,1},{17,25},{25,17},{2,10},{10... | collective-permute-start | bytes 737288 | tf_op jit(solution)/shard_map/ppermute | solution.py:222
  22.5 13.4 %collective-permute-start.5 = (bf16[192,640]{1,0:T(8,128)(2,1)S(1)}, bf16[192,640]{1,0:T(8,128)(2,1)S(1)}, u32[]{:S(2)}, u32[]{:S(2)}) collective-permute-start(bf16[192,640]{1,0:T(8,128)(2,1)S(1)} %get-tuple-element.29.refs_8_), channel_id=1, source_target_pairs={{0,16},{8,24},{16,0},{24,8},{1,17},{9,25},{17,1},{25,9},{2,18},{10... | collective-permute-start | bytes 737288 | tf_op jit(solution)/shard_map/ppermute | solution.py:222
  25.3 15.9 %collective-permute-start.7 = (bf16[192,512]{1,0:T(8,128)(2,1)S(1)}, bf16[192,512]{1,0:T(8,128)(2,1)S(1)}, u32[]{:S(2)}, u32[]{:S(2)}) collective-permute-start(bf16[192,512]{1,0:T(8,128)(2,1)S(1)} %parts.1.refs_0_), channel_id=1, source_target_pairs={{0,2},{2,0},{4,6},{6,4},{1,3},{3,1},{5,7},{7,5},{8,10},{10,8},{12,... | collective-permute-start | bytes 589832 | tf_op jit(solution)/shard_map/ppermute | solution.py:222
  26.7 14.8 %collective-permute-start.8 = (bf16[192,512]{1,0:T(8,128)(2,1)S(1)}, bf16[192,512]{1,0:T(8,128)(2,1)S(1)}, u32[]{:S(2)}, u32[]{:S(2)}) collective-permute-start(bf16[192,512]{1,0:T(8,128)(2,1)S(1)} %parts.1.refs_0_), channel_id=1, source_target_pairs={{0,4},{2,6},{4,0},{6,2},{1,5},{3,7},{5,1},{7,3},{8,12},{10,14},{12... | collective-permute-start | bytes 589832 | tf_op jit(solution)/shard_map/ppermute | solution.py:222
  31.9 9.9 %collective-permute-start.9 = (bf16[192,512]{1,0:T(8,128)(2,1)S(1)}, bf16[192,512]{1,0:T(8,128)(2,1)S(1)}, u32[]{:S(2)}, u32[]{:S(2)}) collective-permute-start(bf16[192,512]{1,0:T(8,128)(2,1)S(1)} %parts.1.refs_0_), channel_id=1, source_target_pairs={{0,6},{2,4},{4,2},{6,0},{1,7},{3,5},{5,3},{7,1},{8,14},{10,12},{12... | collective-permute-start | bytes 589832 | tf_op jit(solution)/shard_map/ppermute | solution.py:222
  35.8 8.6 %collective-permute-start.6 = (bf16[192,640]{1,0:T(8,128)(2,1)S(1)}, bf16[192,640]{1,0:T(8,128)(2,1)S(1)}, u32[]{:S(2)}, u32[]{:S(2)}) collective-permute-start(bf16[192,640]{1,0:T(8,128)(2,1)S(1)} %collective-permute-done.5.refs_1_), channel_id=1, source_target_pairs={{0,8},{8,0},{16,24},{24,16},{1,9},{9,1},{17,25},{25,17},{2,10},{10... | collective-permute-start | bytes 737288 | tf_op jit(solution)/shard_map/ppermute | solution.py:222
  37.5 10.1 %all-to-all-start.1 = ((bf16[8,24,640]{2,1,0:T(8,128)(2,1)}), bf16[8,24,640]{2,1,0:T(8,128)(2,1)S(1)}, u32[]{:S(2)}, u32[]{:S(2)}) async-start(bf16[8,24,640]{2,1,0:T(8,128)(2,1)} %bitcast.2), calls=%async_computation.1 | async-start | bytes 491520 | tf_op jit(solution)/shard_map/all_to_all | solution.py:325
  40.9 1.5 %collective-permute-start.10 = (bf16[192,512]{1,0:T(8,128)(2,1)S(1)}, bf16[192,512]{1,0:T(8,128)(2,1)S(1)}, u32[]{:S(2)}, u32[]{:S(2)}) collective-permute-start(bf16[192,512]{1,0:T(8,128)(2,1)S(1)} %parts.1.refs_0_), channel_id=1, source_target_pairs={{0,1},{1,0},{2,3},{3,2},{4,5},{5,4},{6,7},{7,6},{8,9},{9,8},{10,11... | collective-permute-start | bytes 589832 | tf_op jit(solution)/shard_map/ppermute | solution.py:222
  41.3 1.4 %collective-permute-start.11 = (bf16[192,512]{1,0:T(8,128)(2,1)S(1)}, bf16[192,512]{1,0:T(8,128)(2,1)S(1)}, u32[]{:S(2)}, u32[]{:S(2)}) collective-permute-start(bf16[192,512]{1,0:T(8,128)(2,1)S(1)} %collective-permute-done.7.refs_1_), channel_id=1, source_target_pairs={{0,1},{1,0},{2,3},{3,2},{4,5},{5,4},{6,7},{7,6},{8,9},{9,8},{10,11... | collective-permute-start | bytes 589832 | tf_op jit(solution)/shard_map/ppermute | solution.py:222
  41.5 1.5 %collective-permute-start.12 = (bf16[192,512]{1,0:T(8,128)(2,1)S(1)}, bf16[192,512]{1,0:T(8,128)(2,1)S(1)}, u32[]{:S(2)}, u32[]{:S(2)}) collective-permute-start(bf16[192,512]{1,0:T(8,128)(2,1)S(1)} %collective-permute-done.8.refs_2_), channel_id=1, source_target_pairs={{0,1},{1,0},{2,3},{3,2},{4,5},{5,4},{6,7},{7,6},{8,9},{9,8},{10,11... | collective-permute-start | bytes 589832 | tf_op jit(solution)/shard_map/ppermute | solution.py:222
  41.8 1.5 %collective-permute-start.13 = (bf16[192,512]{1,0:T(8,128)(2,1)S(1)}, bf16[192,512]{1,0:T(8,128)(2,1)S(1)}, u32[]{:S(2)}, u32[]{:S(2)}) collective-permute-start(bf16[192,512]{1,0:T(8,128)(2,1)S(1)} %collective-permute-done.9.refs_3_), channel_id=1, source_target_pairs={{0,1},{1,0},{2,3},{3,2},{4,5},{5,4},{6,7},{7,6},{8,9},{9,8},{10,11... | collective-permute-start | bytes 589832 | tf_op jit(solution)/shard_map/ppermute | solution.py:222

commit v4 on v3

--- a/solution.py
+++ b/solution.py
@@ -254,12 +254,12 @@
     blocks = pl.pallas_call(
         cut_kernel,
         out_shape=struct((images, vit, hid)),
-        in_specs=[ANY],
-        out_specs=ANY,
+        in_specs=[HBM],
+        out_specs=VMEM,
         scratch_shapes=[pltpu.SemaphoreType.DMA((images,))],
         name="cut",
         **limits(4),
-    )(merger_pre)
+    )(pinned(merger_pre))
     llm_grad, blocks = lax.optimization_barrier((llm_grad, blocks))
     pre = lax.all_to_all(blocks, ("ctx", "mp"), 0, 0, tiled=True).reshape(rows, hid)
 
@@ -332,7 +332,7 @@
         name="early",
         **limits(12),
     )(*near_part, *far_part, act)
-    wide = cols // 2
+    wide = cols
     weight_grad = pl.pallas_call(
         late_kernel,
         out_shape=struct((hid, cols), F32),

time: 48.7 us -> 48.7 us (level)
  Pallas kernels: 11.9 us -> 13 us
  local copies, waits for them, and re-layouts: 1.65 us -> 0.72 us
    unnamed x2 -> x0, local copies, waits for them, and re-layouts: 0.94 us -> none
    pallas_call x1, Pallas kernels: 0.75 us -> 1.63 us  [gathered(): pl.pallas_call(cut_kernel, out_shape=struct((images, vit, hid)), in_specs...]
  transfers between devices with their start and end apart: 16 -> 16, of which waited for: 7 -> 7; matrix products, arithmetic and copies ran while one was open for 0% -> 0% of each run, Pallas kernels for 19% -> 20%
where the time goes in v4:
time: 48.7 us; the launch traced here: 48.2 us
  starting transfers between devices  22.9 us (47%)
  Pallas kernels  13 us (27%)
  waiting for transfers between devices  10.9 us (22%)
  between operations  0.73 us (1%)
  local copies, waits for them, and re-layouts  0.72 us (1%)
    ppermute x12, starting transfers between devices, swap(): return lax.ppermute(x, axis, [(i, i ^ k) for i in range(n)])  12.5 us
    all_to_all x1, waiting for transfers between devices, gathered(): lax.all_to_all(blocks, ('ctx', 'mp'), 0, 0, tiled=True).reshape(rows, hid)  5.05 us
    ppermute x2, waiting for transfers between devices, round_plane(): return lax.ppermute(x, ('ctx', 'mp'), pairs)  4.1 us
    ppermute x2, starting transfers between devices, round_plane(): return lax.ppermute(x, ('ctx', 'mp'), pairs)  3.6 us
    all_to_all x1, starting transfers between devices, gathered(): lax.all_to_all(grad.reshape(images, vit, hid), ('ctx', 'mp'), 0, 0, tiled...  3.41 us
    all_to_all x1, starting transfers between devices, gathered(): lax.all_to_all(blocks, ('ctx', 'mp'), 0, 0, tiled=True).reshape(rows, hid)  3.41 us
    pallas_call x1, Pallas kernels, gathered(): pl.pallas_call(grad_kernel, out_shape=struct((rows, hid)), in_specs=[VMEM...  2.81 us
    pallas_call x1, Pallas kernels, gathered(): pl.pallas_call(late_kernel, out_shape=struct((hid, cols), F32), grid=(col...  2.72 us
  transfers between devices with their start and end apart: 16, of which 7 were waited for; matrix products, arithmetic and copies ran while one was open for 0% of the time, Pallas kernels for 20%

profile of v4, /device:TPU:0, one launch (start us, length us, event | category | flops | bytes accessed | tf_op | source)
XLA Modules:
  0.0 48.2 jit_solution(1987396392839911595)
XLA Ops:
  0.6 1.6 %cut.1 = bf16[8,24,640]{2,1,0:T(8,128)(2,1)} custom-call(bf16[24,5120]{1,0:T(8,128)(2,1)} %pre.1), custom_call_target="tpu_custom_call" | custom-call | flops 1 | bytes 1 | tf_op jit(solution)/shard_map/cut/pallas_call | solution.py:254
  2.3 1.7 %pick.1 = (bf16[48,4096]{1,0:T(8,128)(2,1)S(1)}, bf16[192,192]{1,0:T(8,128)(2,1)S(1)}, bf16[192,192]{1,0:T(8,128)(2,1)S(1)}, bf16[48,512]{1,0:T(8,128)(2,1)S(1)}...) custom-call(bf16[128,4096]{1,0:T(8,128)(2,1)} %refs_0_, s32[1,4,48]{2,1,0:T(4,128)} %refs_1_.1, ...), custom_call_target="tpu_custom_call" | custom-call | flops 1 | bytes 1 | tf_op jit(solution)/shard_map/pick/pallas_call | solution.py:267
  4.0 3.0 %collective-permute-start = (bf16[48,4096]{1,0:T(8,128)(2,1)S(1)}, bf16[48,4096]{1,0:T(8,128)(2,1)S(1)}, u32[]{:S(2)}, u32[]{:S(2)}) collective-permute-start(bf16[48,4096]{1,0:T(8,128)(2,1)S(1)} %get-tuple-element.25.refs_0_.mine), channel_id=1, source_target_pairs={{0,2},{1,5},{2,0},{3,7},{4,6},{5,1},{6,4},{7,3},{8,10},{9,13},{10,... | collective-permute-start | bytes 1179656 | tf_op jit(solution)/shard_map/ppermute | solution.py:231
  7.0 3.4 %all-to-all-start = ((bf16[8,24,640]{2,1,0:T(8,128)(2,1)}), bf16[8,24,640]{2,1,0:T(8,128)(2,1)S(1)}, u32[]{:S(2)}, u32[]{:S(2)}) async-start(bf16[8,24,640]{2,1,0:T(8,128)(2,1)} %cut.1), calls=%async_computation | async-start | bytes 491520 | tf_op jit(solution)/shard_map/all_to_all | solution.py:264
  10.4 1.6 %collective-permute-start.1 = (bf16[96,512]{1,0:T(8,128)(2,1)S(1)}, bf16[96,512]{1,0:T(8,128)(2,1)S(1)}, u32[]{:S(2)}, u32[]{:S(2)}) collective-permute-start(bf16[96,512]{1,0:T(8,128)(2,1)S(1)} %get-tuple-element.26), channel_id=1, source_target_pairs={{0,8},{8,0},{16,24},{24,16},{1,9},{9,1},{17,25},{25,17},{2,10},{10... | collective-permute-start | bytes 294920 | tf_op jit(solution)/shard_map/ppermute | solution.py:222
  12.1 5.0 %all-to-all-done = bf16[8,24,640]{2,1,0:T(8,128)(2,1)S(1)} async-done(((bf16[8,24,640]{2,1,0:T(8,128)(2,1)}), bf16[8,24,640]{2,1,0:T(8,128)(2,1)S(1)}, u32[]{:S(2)}, u32[]{:S(2)}) %all-to-all-start) | async-done | bytes 245792 | tf_op jit(solution)/shard_map/all_to_all | solution.py:264
  17.1 0.4 act.1
  17.5 0.0 collective-permute-done.1.refs_1_.first
  17.5 0.0 collective-permute-done.refs_1_.one
  17.5 0.1 pair.1
  17.6 0.6 %collective-permute-start.2 = (bf16[96,4096]{1,0:T(8,128)(2,1)S(1)}, bf16[96,4096]{1,0:T(8,128)(2,1)S(1)}, u32[]{:S(2)}, u32[]{:S(2)}) collective-permute-start(bf16[96,4096]{1,0:T(8,128)(2,1)S(1)} %pair.1), channel_id=1, source_target_pairs={{0,4},{1,3},{2,6},{3,1},{4,0},{5,7},{6,2},{7,5},{8,12},{9,11},{10,... | collective-permute-start | bytes 2359304 | tf_op jit(solution)/shard_map/ppermute | solution.py:231
  18.2 2.7 %collective-permute-start.3 = (bf16[96,512]{1,0:T(8,128)(2,1)S(1)}, bf16[96,512]{1,0:T(8,128)(2,1)S(1)}, u32[]{:S(2)}, u32[]{:S(2)}) collective-permute-start(bf16[96,512]{1,0:T(8,128)(2,1)S(1)} %pass_on.1), channel_id=1, source_target_pairs={{0,16},{8,24},{16,0},{24,8},{1,17},{9,25},{17,1},{25,9},{2,18},{10... | collective-permute-start | bytes 294920 | tf_op jit(solution)/shard_map/ppermute | solution.py:222
  20.8 1.6 %collective-permute-start.4 = (bf16[192,640]{1,0:T(8,128)(2,1)S(1)}, bf16[192,640]{1,0:T(8,128)(2,1)S(1)}, u32[]{:S(2)}, u32[]{:S(2)}) collective-permute-start(bf16[192,640]{1,0:T(8,128)(2,1)S(1)} %get-tuple-element.29.refs_8_), channel_id=1, source_target_pairs={{0,8},{8,0},{16,24},{24,16},{1,9},{9,1},{17,25},{25,17},{2,10},{10... | collective-permute-start | bytes 737288 | tf_op jit(solution)/shard_map/ppermute | solution.py:222
  22.4 0.3 collective-permute-start.5
  22.7 2.5 %hold.1.weight = bf16[640,4096]{1,0:T(8,128)(2,1)S(1)} custom-call(bf16[640,4096]{1,0:T(8,128)(2,1)} %source), custom_call_target="tpu_custom_call" | custom-call | flops 1 | bytes 1 | tf_op jit(solution)/shard_map/hold/pallas_call | solution.py:296
  25.2 0.0 collective-permute-done.3.second
  25.3 1.4 %collective-permute-start.7 = (bf16[192,512]{1,0:T(8,128)(2,1)S(1)}, bf16[192,512]{1,0:T(8,128)(2,1)S(1)}, u32[]{:S(2)}, u32[]{:S(2)}) collective-permute-start(bf16[192,512]{1,0:T(8,128)(2,1)S(1)} %parts.1.refs_0_), channel_id=1, source_target_pairs={{0,2},{2,0},{4,6},{6,4},{1,3},{3,1},{5,7},{7,5},{8,10},{10,8},{12,... | collective-permute-start | bytes 589832 | tf_op jit(solution)/shard_map/ppermute | solution.py:222
  26.6 1.1 %collective-permute-start.8 = (bf16[192,512]{1,0:T(8,128)(2,1)S(1)}, bf16[192,512]{1,0:T(8,128)(2,1)S(1)}, u32[]{:S(2)}, u32[]{:S(2)}) collective-permute-start(bf16[192,512]{1,0:T(8,128)(2,1)S(1)} %parts.1.refs_0_), channel_id=1, source_target_pairs={{0,4},{2,6},{4,0},{6,2},{1,5},{3,7},{5,1},{7,3},{8,12},{10,14},{12... | collective-permute-start | bytes 589832 | tf_op jit(solution)/shard_map/ppermute | solution.py:222
  27.8 4.1 %collective-permute-done.2.two = bf16[96,4096]{1,0:T(8,128)(2,1)S(1)} collective-permute-done((bf16[96,4096]{1,0:T(8,128)(2,1)S(1)}, bf16[96,4096]{1,0:T(8,128)(2,1)S(1)}, u32[]{:S(2)}, u32[]{:S(2)}) %collective-permute-start.2) | collective-permute-done | bytes 786464 | tf_op jit(solution)/shard_map/ppermute | solution.py:231
  31.9 1.1 %collective-permute-start.9 = (bf16[192,512]{1,0:T(8,128)(2,1)S(1)}, bf16[192,512]{1,0:T(8,128)(2,1)S(1)}, u32[]{:S(2)}, u32[]{:S(2)}) collective-permute-start(bf16[192,512]{1,0:T(8,128)(2,1)S(1)} %parts.1.refs_0_), channel_id=1, source_target_pairs={{0,6},{2,4},{4,2},{6,0},{1,7},{3,5},{5,3},{7,1},{8,14},{10,12},{12... | collective-permute-start | bytes 589832 | tf_op jit(solution)/shard_map/ppermute | solution.py:222
  32.9 2.8 %grad.1 = bf16[192,640]{1,0:T(8,128)(2,1)} custom-call(bf16[48,4096]{1,0:T(8,128)(2,1)S(1)} %get-tuple-element.25.refs_0_.mine, bf16[48,4096]{1,0:T(8,128)(2,1)S(1)} %collective-permute-done.refs_1_.one, bf16[96,4096]{1,0:T(8,128)(2,1)S(1)} %collective-permute-done.2.two, bf16[640,4096]{1,0:T(8,128)(2,1)S(1)} %hold.1.weight, ...), custom_call_target="tpu_custom_call" | custom-call | flops 1 | bytes 1 | tf_op jit(solution)/shard_map/grad/pallas_call | solution.py:311
  35.8 0.0 collective-permute-done.4.refs_0_
  35.8 0.0 collective-permute-done.5.refs_1_
  35.8 1.6 %collective-permute-start.6 = (bf16[192,640]{1,0:T(8,128)(2,1)S(1)}, bf16[192,640]{1,0:T(8,128)(2,1)S(1)}, u32[]{:S(2)}, u32[]{:S(2)}) collective-permute-start(bf16[192,640]{1,0:T(8,128)(2,1)S(1)} %collective-permute-done.5.refs_1_), channel_id=1, source_target_pairs={{0,8},{8,0},{16,24},{24,16},{1,9},{9,1},{17,25},{25,17},{2,10},{10... | collective-permute-start | bytes 737288 | tf_op jit(solution)/shard_map/ppermute | solution.py:222
  37.4 3.4 %all-to-all-start.1 = ((bf16[8,24,640]{2,1,0:T(8,128)(2,1)}), bf16[8,24,640]{2,1,0:T(8,128)(2,1)S(1)}, u32[]{:S(2)}, u32[]{:S(2)}) async-start(bf16[8,24,640]{2,1,0:T(8,128)(2,1)} %bitcast.2), calls=%async_computation.1 | async-start | bytes 491520 | tf_op jit(solution)/shard_map/all_to_all | solution.py:325
  40.8 0.4 collective-permute-start.10
  41.2 0.0 collective-permute-done.7.refs_1_
  41.2 0.2 collective-permute-start.11
  41.4 0.0 collective-permute-done.8.refs_2_
  41.4 0.3 collective-permute-start.12
  41.7 0.0 collective-permute-done.9.refs_3_
  41.7 0.2 collective-permute-start.13
  41.9 0.4 collective-permute-done.10.refs_4_
  42.3 0.3 collective-permute-done.11.refs_5_
  42.7 0.3 collective-permute-done.12.refs_6_
  42.9 0.3 collective-permute-done.13.refs_7_
  43.2 1.2 %early.1 = (bf16[768,1024]{1,0:T(8,128)(2,1)S(1)}, f32[640,1024]{1,0:T(8,128)S(1)}, f32[1,1024]{1,0:T(1,128)}) custom-call(bf16[192,512]{1,0:T(8,128)(2,1)S(1)} %parts.1.refs_0_, bf16[192,512]{1,0:T(8,128)(2,1)S(1)} %collective-permute-done.7.refs_1_, bf16[192,512]{1,0:T(8,128)(2,1)S(1)} %collective-permute-done.8.refs_2_, ...), custom_call_target="tpu_custom_call" | custom-call | flops 1 | bytes 1 | tf_op jit(solution)/shard_map/early/pallas_call | solution.py:327
  44.4 0.0 collective-permute-done.6.refs_2_
  44.4 2.7 %late.1 = f32[640,1024]{1,0:T(8,128)} custom-call(bf16[192,640]{1,0:T(8,128)(2,1)S(1)} %collective-permute-done.4.refs_0_, bf16[192,640]{1,0:T(8,128)(2,1)S(1)} %collective-permute-done.5.refs_1_, bf16[192,640]{1,0:T(8,128)(2,1)S(1)} %collective-permute-done.6.refs_2_, bf16[768,1024]{1,0:T(8,128)(2,1)S(1)} %get-tuple-element.40.refs_3_, ...), custom_call_target="tpu_custom_call" | custom-call | flops 1 | bytes 1 | tf_op jit(solution)/shard_map/late/pallas_call | solution.py:336
  47.1 0.4 all-to-all-done.1
  47.5 0.7 %copy.10 = bf16[8,3,8,640]{3,2,0,1:T(8,128)(2,1)} copy(bf16[8,3,8,640]{3,2,1,0:T(8,128)(2,1)S(1)} %bitcast.8) | data formatting | bytes 491520 | tf_op jit(solution)/shard_map/reshape | solution.py:346
  (2 shorter events, 0.0 us)
Async XLA Ops:
  4.0 13.5 %collective-permute-start = (bf16[48,4096]{1,0:T(8,128)(2,1)S(1)}, bf16[48,4096]{1,0:T(8,128)(2,1)S(1)}, u32[]{:S(2)}, u32[]{:S(2)}) collective-permute-start(bf16[48,4096]{1,0:T(8,128)(2,1)S(1)} %get-tuple-element.25.refs_0_.mine), channel_id=1, source_target_pairs={{0,2},{1,5},{2,0},{3,7},{4,6},{5,1},{6,4},{7,3},{8,10},{9,13},{10,... | collective-permute-start | bytes 1179656 | tf_op jit(solution)/shard_map/ppermute | solution.py:231
  7.0 10.1 %all-to-all-start = ((bf16[8,24,640]{2,1,0:T(8,128)(2,1)}), bf16[8,24,640]{2,1,0:T(8,128)(2,1)S(1)}, u32[]{:S(2)}, u32[]{:S(2)}) async-start(bf16[8,24,640]{2,1,0:T(8,128)(2,1)} %cut.1), calls=%async_computation | async-start | bytes 491520 | tf_op jit(solution)/shard_map/all_to_all | solution.py:264
  10.4 7.1 %collective-permute-start.1 = (bf16[96,512]{1,0:T(8,128)(2,1)S(1)}, bf16[96,512]{1,0:T(8,128)(2,1)S(1)}, u32[]{:S(2)}, u32[]{:S(2)}) collective-permute-start(bf16[96,512]{1,0:T(8,128)(2,1)S(1)} %get-tuple-element.26), channel_id=1, source_target_pairs={{0,8},{8,0},{16,24},{24,16},{1,9},{9,1},{17,25},{25,17},{2,10},{10... | collective-permute-start | bytes 294920 | tf_op jit(solution)/shard_map/ppermute | solution.py:222
  17.6 14.3 %collective-permute-start.2 = (bf16[96,4096]{1,0:T(8,128)(2,1)S(1)}, bf16[96,4096]{1,0:T(8,128)(2,1)S(1)}, u32[]{:S(2)}, u32[]{:S(2)}) collective-permute-start(bf16[96,4096]{1,0:T(8,128)(2,1)S(1)} %pair.1), channel_id=1, source_target_pairs={{0,4},{1,3},{2,6},{3,1},{4,0},{5,7},{6,2},{7,5},{8,12},{9,11},{10,... | collective-permute-start | bytes 2359304 | tf_op jit(solution)/shard_map/ppermute | solution.py:231
  18.2 7.1 %collective-permute-start.3 = (bf16[96,512]{1,0:T(8,128)(2,1)S(1)}, bf16[96,512]{1,0:T(8,128)(2,1)S(1)}, u32[]{:S(2)}, u32[]{:S(2)}) collective-permute-start(bf16[96,512]{1,0:T(8,128)(2,1)S(1)} %pass_on.1), channel_id=1, source_target_pairs={{0,16},{8,24},{16,0},{24,8},{1,17},{9,25},{17,1},{25,9},{2,18},{10... | collective-permute-start | bytes 294920 | tf_op jit(solution)/shard_map/ppermute | solution.py:222
  20.8 14.9 %collective-permute-start.4 = (bf16[192,640]{1,0:T(8,128)(2,1)S(1)}, bf16[192,640]{1,0:T(8,128)(2,1)S(1)}, u32[]{:S(2)}, u32[]{:S(2)}) collective-permute-start(bf16[192,640]{1,0:T(8,128)(2,1)S(1)} %get-tuple-element.29.refs_8_), channel_id=1, source_target_pairs={{0,8},{8,0},{16,24},{24,16},{1,9},{9,1},{17,25},{25,17},{2,10},{10... | collective-permute-start | bytes 737288 | tf_op jit(solution)/shard_map/ppermute | solution.py:222
  22.4 13.4 %collective-permute-start.5 = (bf16[192,640]{1,0:T(8,128)(2,1)S(1)}, bf16[192,640]{1,0:T(8,128)(2,1)S(1)}, u32[]{:S(2)}, u32[]{:S(2)}) collective-permute-start(bf16[192,640]{1,0:T(8,128)(2,1)S(1)} %get-tuple-element.29.refs_8_), channel_id=1, source_target_pairs={{0,16},{8,24},{16,0},{24,8},{1,17},{9,25},{17,1},{25,9},{2,18},{10... | collective-permute-start | bytes 737288 | tf_op jit(solution)/shard_map/ppermute | solution.py:222
  25.3 15.9 %collective-permute-start.7 = (bf16[192,512]{1,0:T(8,128)(2,1)S(1)}, bf16[192,512]{1,0:T(8,128)(2,1)S(1)}, u32[]{:S(2)}, u32[]{:S(2)}) collective-permute-start(bf16[192,512]{1,0:T(8,128)(2,1)S(1)} %parts.1.refs_0_), channel_id=1, source_target_pairs={{0,2},{2,0},{4,6},{6,4},{1,3},{3,1},{5,7},{7,5},{8,10},{10,8},{12,... | collective-permute-start | bytes 589832 | tf_op jit(solution)/shard_map/ppermute | solution.py:222
  26.6 14.8 %collective-permute-start.8 = (bf16[192,512]{1,0:T(8,128)(2,1)S(1)}, bf16[192,512]{1,0:T(8,128)(2,1)S(1)}, u32[]{:S(2)}, u32[]{:S(2)}) collective-permute-start(bf16[192,512]{1,0:T(8,128)(2,1)S(1)} %parts.1.refs_0_), channel_id=1, source_target_pairs={{0,4},{2,6},{4,0},{6,2},{1,5},{3,7},{5,1},{7,3},{8,12},{10,14},{12... | collective-permute-start | bytes 589832 | tf_op jit(solution)/shard_map/ppermute | solution.py:222
  31.9 9.9 %collective-permute-start.9 = (bf16[192,512]{1,0:T(8,128)(2,1)S(1)}, bf16[192,512]{1,0:T(8,128)(2,1)S(1)}, u32[]{:S(2)}, u32[]{:S(2)}) collective-permute-start(bf16[192,512]{1,0:T(8,128)(2,1)S(1)} %parts.1.refs_0_), channel_id=1, source_target_pairs={{0,6},{2,4},{4,2},{6,0},{1,7},{3,5},{5,3},{7,1},{8,14},{10,12},{12... | collective-permute-start | bytes 589832 | tf_op jit(solution)/shard_map/ppermute | solution.py:222
  35.8 8.6 %collective-permute-start.6 = (bf16[192,640]{1,0:T(8,128)(2,1)S(1)}, bf16[192,640]{1,0:T(8,128)(2,1)S(1)}, u32[]{:S(2)}, u32[]{:S(2)}) collective-permute-start(bf16[192,640]{1,0:T(8,128)(2,1)S(1)} %collective-permute-done.5.refs_1_), channel_id=1, source_target_pairs={{0,8},{8,0},{16,24},{24,16},{1,9},{9,1},{17,25},{25,17},{2,10},{10... | collective-permute-start | bytes 737288 | tf_op jit(solution)/shard_map/ppermute | solution.py:222
  37.4 10.1 %all-to-all-start.1 = ((bf16[8,24,640]{2,1,0:T(8,128)(2,1)}), bf16[8,24,640]{2,1,0:T(8,128)(2,1)S(1)}, u32[]{:S(2)}, u32[]{:S(2)}) async-start(bf16[8,24,640]{2,1,0:T(8,128)(2,1)} %bitcast.2), calls=%async_computation.1 | async-start | bytes 491520 | tf_op jit(solution)/shard_map/all_to_all | solution.py:325
  40.8 1.5 %collective-permute-start.10 = (bf16[192,512]{1,0:T(8,128)(2,1)S(1)}, bf16[192,512]{1,0:T(8,128)(2,1)S(1)}, u32[]{:S(2)}, u32[]{:S(2)}) collective-permute-start(bf16[192,512]{1,0:T(8,128)(2,1)S(1)} %parts.1.refs_0_), channel_id=1, source_target_pairs={{0,1},{1,0},{2,3},{3,2},{4,5},{5,4},{6,7},{7,6},{8,9},{9,8},{10,11... | collective-permute-start | bytes 589832 | tf_op jit(solution)/shard_map/ppermute | solution.py:222
  41.2 1.4 %collective-permute-start.11 = (bf16[192,512]{1,0:T(8,128)(2,1)S(1)}, bf16[192,512]{1,0:T(8,128)(2,1)S(1)}, u32[]{:S(2)}, u32[]{:S(2)}) collective-permute-start(bf16[192,512]{1,0:T(8,128)(2,1)S(1)} %collective-permute-done.7.refs_1_), channel_id=1, source_target_pairs={{0,1},{1,0},{2,3},{3,2},{4,5},{5,4},{6,7},{7,6},{8,9},{9,8},{10,11... | collective-permute-start | bytes 589832 | tf_op jit(solution)/shard_map/ppermute | solution.py:222
  41.4 1.5 %collective-permute-start.12 = (bf16[192,512]{1,0:T(8,128)(2,1)S(1)}, bf16[192,512]{1,0:T(8,128)(2,1)S(1)}, u32[]{:S(2)}, u32[]{:S(2)}) collective-permute-start(bf16[192,512]{1,0:T(8,128)(2,1)S(1)} %collective-permute-done.8.refs_2_), channel_id=1, source_target_pairs={{0,1},{1,0},{2,3},{3,2},{4,5},{5,4},{6,7},{7,6},{8,9},{9,8},{10,11... | collective-permute-start | bytes 589832 | tf_op jit(solution)/shard_map/ppermute | solution.py:222
  41.7 1.5 %collective-permute-start.13 = (bf16[192,512]{1,0:T(8,128)(2,1)S(1)}, bf16[192,512]{1,0:T(8,128)(2,1)S(1)}, u32[]{:S(2)}, u32[]{:S(2)}) collective-permute-start(bf16[192,512]{1,0:T(8,128)(2,1)S(1)} %collective-permute-done.9.refs_3_), channel_id=1, source_target_pairs={{0,1},{1,0},{2,3},{3,2},{4,5},{5,4},{6,7},{7,6},{8,9},{9,8},{10,11... | collective-permute-start | bytes 589832 | tf_op jit(solution)/shard_map/ppermute | solution.py:222

commit v5 on v3

--- a/solution.py
+++ b/solution.py
@@ -166,12 +166,11 @@
     copy.wait()
 
 
-def grad_kernel(mine, one, two, weight, slope, back, out, rows):
+def grad_kernel(mine, one, side, two, weight, slope, back, out, rows):
     core = lax.axis_index("mp")
     block = mine.shape[0]
-    pieces = (mine[...], one[...], two[:block], two[block:])
-    for spot, piece in zip((0, 1 + core, 2 - core, 3), pieces):
-        rows[pl.ds(pl.multiple_of(spot * block, block), block)] = piece
+    for spot, piece in zip((0, 1 + core, 2 - core, 3), (mine, one, side, two)):
+        rows[pl.ds(pl.multiple_of(spot * block, block), block)] = piece[...]
     grad = lax.dot_general(rows[...], weight[...], (((1,), (1,)), ((), ())), preferred_element_type=F32)
     grad = (grad * slope[...]).astype(BF16)
     out[...] = jnp.dot(back[...], grad, preferred_element_type=F32).astype(BF16)
@@ -290,7 +289,7 @@
     )(there, pre)
     acts = {0: act} | {k: swap(act, "dp", k) for k in range(1, n_dp) if k & (k - 1) == 0}
     out_weight, one, first, _ = lax.optimization_barrier((out_weight, one, first, act))
-    two = round_plane(stacked(functools.partial(stack_kernel, (0, 0)), (mine, one), 2 * block, "pair"), 1)
+    two, side = round_plane(one, 1), swap(one, "mp", 1)
     second = stacked(functools.partial(stack_kernel, (0, block)), (pass_on, first), 2 * block, "pass_on")
     second = swap(second, "dp", 2)
     held = pl.pallas_call(
@@ -311,12 +310,12 @@
     grad = pl.pallas_call(
         grad_kernel,
         out_shape=struct((rows, hid)),
-        in_specs=[VMEM] * 6,
+        in_specs=[VMEM] * 7,
         out_specs=VMEM,
         scratch_shapes=[pltpu.VMEM((rows, feat), BF16)],
         name="grad",
         **limits(8),
-    )(mine, one, two, held, slope, back)
+    )(mine, one, side, two, held, slope, back)
     relay, _ = lax.optimization_barrier(([acts[k] for k in sorted(acts)], grad))
     relay = dict(zip(sorted(acts), relay))
     for k in range(n_dp):

time: 48.7 us -> 49.1 us (level)
  waiting for transfers between devices: 11.1 us -> 12.4 us
  starting transfers between devices: 22.9 us -> 22 us
    ppermute x12 -> x13, waiting for transfers between devices: 1.33 us -> 6.76 us  [swap(): return lax.ppermute(x, axis, [(i, i ^ k) for i in range(n)])]
    ppermute x2, waiting for transfers between devices: 4.1 us -> 0.01 us  [round_plane(): return lax.ppermute(x, ('ctx', 'mp'), pairs)]
    ppermute x12 -> x13, starting transfers between devices: 12.5 us -> 11.6 us  [swap(): return lax.ppermute(x, axis, [(i, i ^ k) for i in range(n)])]
  transfers between devices with their start and end apart: 16 -> 17, of which waited for: 7 -> 9; matrix products, arithmetic and copies ran while one was open for 0% -> 0% of each run, Pallas kernels for 19% -> 19%
where the time goes in v5:
time: 49.1 us; the launch traced here: 48.7 us
  starting transfers between devices  22 us (45%)
  waiting for transfers between devices  12.4 us (25%)
  Pallas kernels  11.8 us (24%)
  local copies, waits for them, and re-layouts  1.65 us (3%)
  between operations  0.73 us (1%)
    ppermute x13, starting transfers between devices, swap(): return lax.ppermute(x, axis, [(i, i ^ k) for i in range(n)])  11.6 us
    ppermute x13, waiting for transfers between devices, swap(): return lax.ppermute(x, axis, [(i, i ^ k) for i in range(n)])  6.76 us
    all_to_all x1, waiting for transfers between devices, gathered(): lax.all_to_all(blocks, ('ctx', 'mp'), 0, 0, tiled=True).reshape(rows, hid)  5.05 us
    ppermute x2, starting transfers between devices, round_plane(): return lax.ppermute(x, ('ctx', 'mp'), pairs)  3.61 us
    all_to_all x1, starting transfers between devices, gathered(): lax.all_to_all(blocks, ('ctx', 'mp'), 0, 0, tiled=True).reshape(rows, hid)  3.41 us
    all_to_all x1, starting transfers between devices, gathered(): lax.all_to_all(grad.reshape(images, vit, hid), ('ctx', 'mp'), 0, 0, tiled...  3.41 us
    pallas_call x1, Pallas kernels, gathered(): pl.pallas_call(grad_kernel, out_shape=struct((rows, hid)), in_specs=[VMEM...  2.81 us
    pallas_call x1, Pallas kernels, gathered(): pl.pallas_call(late_kernel, out_shape=struct((hid, cols), F32), grid=(col...  2.5 us
  transfers between devices with their start and end apart: 17, of which 9 were waited for; matrix products, arithmetic and copies ran while one was open for 0% of the time, Pallas kernels for 19%

profile of v5, /device:TPU:0, one launch (start us, length us, event | category | flops | bytes accessed | tf_op | source)
XLA Modules:
  0.0 48.7 jit_solution(5699603972161254482)
XLA Ops:
  0.6 0.0 copy-start
  0.6 0.9 %copy-done = bf16[24,5120]{1,0:T(8,128)(2,1)S(1)} copy-done((bf16[24,5120]{1,0:T(8,128)(2,1)S(1)}, bf16[24,5120]{1,0:T(8,128)(2,1)}, u32[]{:S(2)}) %copy-start) | copy-done | bytes 245784
  1.6 0.7 %cut.1 = bf16[8,24,640]{2,1,0:T(8,128)(2,1)} custom-call(bf16[24,5120]{1,0:T(8,128)(2,1)S(1)} %copy-done), custom_call_target="tpu_custom_call" | custom-call | flops 1 | bytes 1 | tf_op jit(solution)/shard_map/cut/pallas_call | solution.py:253
  2.3 1.7 %pick.1 = (bf16[48,4096]{1,0:T(8,128)(2,1)S(1)}, bf16[192,192]{1,0:T(8,128)(2,1)S(1)}, bf16[192,192]{1,0:T(8,128)(2,1)S(1)}, bf16[48,512]{1,0:T(8,128)(2,1)S(1)}...) custom-call(bf16[128,4096]{1,0:T(8,128)(2,1)} %refs_0_, s32[1,4,48]{2,1,0:T(4,128)} %refs_1_.1, ...), custom_call_target="tpu_custom_call" | custom-call | flops 1 | bytes 1 | tf_op jit(solution)/shard_map/pick/pallas_call | solution.py:266
  4.1 3.0 %collective-permute-start = (bf16[48,4096]{1,0:T(8,128)(2,1)S(1)}, bf16[48,4096]{1,0:T(8,128)(2,1)S(1)}, u32[]{:S(2)}, u32[]{:S(2)}) collective-permute-start(bf16[48,4096]{1,0:T(8,128)(2,1)S(1)} %get-tuple-element.25.mine), channel_id=1, source_target_pairs={{0,2},{1,5},{2,0},{3,7},{4,6},{5,1},{6,4},{7,3},{8,10},{9,13},{10,... | collective-permute-start | bytes 1179656 | tf_op jit(solution)/shard_map/ppermute | solution.py:230
  7.1 3.4 %all-to-all-start = ((bf16[8,24,640]{2,1,0:T(8,128)(2,1)}), bf16[8,24,640]{2,1,0:T(8,128)(2,1)S(1)}, u32[]{:S(2)}, u32[]{:S(2)}) async-start(bf16[8,24,640]{2,1,0:T(8,128)(2,1)} %cut.1), calls=%async_computation | async-start | bytes 491520 | tf_op jit(solution)/shard_map/all_to_all | solution.py:263
  10.5 1.6 %collective-permute-start.1 = (bf16[96,512]{1,0:T(8,128)(2,1)S(1)}, bf16[96,512]{1,0:T(8,128)(2,1)S(1)}, u32[]{:S(2)}, u32[]{:S(2)}) collective-permute-start(bf16[96,512]{1,0:T(8,128)(2,1)S(1)} %get-tuple-element.26), channel_id=1, source_target_pairs={{0,8},{8,0},{16,24},{24,16},{1,9},{9,1},{17,25},{25,17},{2,10},{10... | collective-permute-start | bytes 294920 | tf_op jit(solution)/shard_map/ppermute | solution.py:221
  12.1 5.0 %all-to-all-done = bf16[8,24,640]{2,1,0:T(8,128)(2,1)S(1)} async-done(((bf16[8,24,640]{2,1,0:T(8,128)(2,1)}), bf16[8,24,640]{2,1,0:T(8,128)(2,1)S(1)}, u32[]{:S(2)}, u32[]{:S(2)}) %all-to-all-start) | async-done | bytes 245792 | tf_op jit(solution)/shard_map/all_to_all | solution.py:263
  17.2 0.4 act.1
  17.5 0.0 collective-permute-done.1.refs_1_.first
  17.6 0.0 collective-permute-done.one
  17.6 0.1 collective-permute-start.2
  17.6 0.6 %collective-permute-start.3 = (bf16[48,4096]{1,0:T(8,128)(2,1)S(1)}, bf16[48,4096]{1,0:T(8,128)(2,1)S(1)}, u32[]{:S(2)}, u32[]{:S(2)}) collective-permute-start(bf16[48,4096]{1,0:T(8,128)(2,1)S(1)} %collective-permute-done.one), channel_id=1, source_target_pairs={{0,4},{1,3},{2,6},{3,1},{4,0},{5,7},{6,2},{7,5},{8,12},{9,11},{10,... | collective-permute-start | bytes 1179656 | tf_op jit(solution)/shard_map/ppermute | solution.py:230
  18.3 2.7 %collective-permute-start.4 = (bf16[96,512]{1,0:T(8,128)(2,1)S(1)}, bf16[96,512]{1,0:T(8,128)(2,1)S(1)}, u32[]{:S(2)}, u32[]{:S(2)}) collective-permute-start(bf16[96,512]{1,0:T(8,128)(2,1)S(1)} %pass_on.1), channel_id=1, source_target_pairs={{0,16},{8,24},{16,0},{24,8},{1,17},{9,25},{17,1},{25,9},{2,18},{10... | collective-permute-start | bytes 294920 | tf_op jit(solution)/shard_map/ppermute | solution.py:221
  20.9 1.6 %collective-permute-start.5 = (bf16[192,640]{1,0:T(8,128)(2,1)S(1)}, bf16[192,640]{1,0:T(8,128)(2,1)S(1)}, u32[]{:S(2)}, u32[]{:S(2)}) collective-permute-start(bf16[192,640]{1,0:T(8,128)(2,1)S(1)} %get-tuple-element.29.refs_8_), channel_id=1, source_target_pairs={{0,8},{8,0},{16,24},{24,16},{1,9},{9,1},{17,25},{25,17},{2,10},{10... | collective-permute-start | bytes 737288 | tf_op jit(solution)/shard_map/ppermute | solution.py:221
  22.5 0.3 collective-permute-start.6
  22.8 2.5 %hold.1.weight = bf16[640,4096]{1,0:T(8,128)(2,1)S(1)} custom-call(bf16[640,4096]{1,0:T(8,128)(2,1)} %source), custom_call_target="tpu_custom_call" | custom-call | flops 1 | bytes 1 | tf_op jit(solution)/shard_map/hold/pallas_call | solution.py:295
  25.3 1.7 %collective-permute-done.4.second = bf16[96,512]{1,0:T(8,128)(2,1)S(1)} collective-permute-done((bf16[96,512]{1,0:T(8,128)(2,1)S(1)}, bf16[96,512]{1,0:T(8,128)(2,1)S(1)}, u32[]{:S(2)}, u32[]{:S(2)}) %collective-permute-start.4) | collective-permute-done | bytes 98336 | tf_op jit(solution)/shard_map/ppermute | solution.py:221
  27.0 1.3 %collective-permute-start.8 = (bf16[192,512]{1,0:T(8,128)(2,1)S(1)}, bf16[192,512]{1,0:T(8,128)(2,1)S(1)}, u32[]{:S(2)}, u32[]{:S(2)}) collective-permute-start(bf16[192,512]{1,0:T(8,128)(2,1)S(1)} %parts.1.refs_0_), channel_id=1, source_target_pairs={{0,2},{2,0},{4,6},{6,4},{1,3},{3,1},{5,7},{7,5},{8,10},{10,8},{12,... | collective-permute-start | bytes 589832 | tf_op jit(solution)/shard_map/ppermute | solution.py:221
  28.3 0.0 collective-permute-done.2.side
  28.3 0.1 collective-permute-start.9
  28.5 0.0 collective-permute-done.3.two
  28.5 2.1 %collective-permute-start.10 = (bf16[192,512]{1,0:T(8,128)(2,1)S(1)}, bf16[192,512]{1,0:T(8,128)(2,1)S(1)}, u32[]{:S(2)}, u32[]{:S(2)}) collective-permute-start(bf16[192,512]{1,0:T(8,128)(2,1)S(1)} %parts.1.refs_0_), channel_id=1, source_target_pairs={{0,6},{2,4},{4,2},{6,0},{1,7},{3,5},{5,3},{7,1},{8,14},{10,12},{12... | collective-permute-start | bytes 589832 | tf_op jit(solution)/shard_map/ppermute | solution.py:221
  30.6 2.8 %grad.1 = bf16[192,640]{1,0:T(8,128)(2,1)} custom-call(bf16[48,4096]{1,0:T(8,128)(2,1)S(1)} %get-tuple-element.25.mine, bf16[48,4096]{1,0:T(8,128)(2,1)S(1)} %collective-permute-done.one, bf16[48,4096]{1,0:T(8,128)(2,1)S(1)} %collective-permute-done.2.side, bf16[48,4096]{1,0:T(8,128)(2,1)S(1)} %collective-permute-done.3.two, ...), custom_call_target="tpu_custom_call" | custom-call | flops 1 | bytes 1 | tf_op jit(solution)/shard_map/grad/pallas_call | solution.py:310
  33.4 0.9 %collective-permute-done.5.refs_0_ = bf16[192,640]{1,0:T(8,128)(2,1)S(1)} collective-permute-done((bf16[192,640]{1,0:T(8,128)(2,1)S(1)}, bf16[192,640]{1,0:T(8,128)(2,1)S(1)}, u32[]{:S(2)}, u32[]{:S(2)}) %collective-permute-start.5) | collective-permute-done | bytes 245792 | tf_op jit(solution)/shard_map/ppermute | solution.py:221
  34.3 2.8 %collective-permute-done.6.refs_1_ = bf16[192,640]{1,0:T(8,128)(2,1)S(1)} collective-permute-done((bf16[192,640]{1,0:T(8,128)(2,1)S(1)}, bf16[192,640]{1,0:T(8,128)(2,1)S(1)}, u32[]{:S(2)}, u32[]{:S(2)}) %collective-permute-start.6) | collective-permute-done | bytes 245792 | tf_op jit(solution)/shard_map/ppermute | solution.py:221
  37.1 0.7 %collective-permute-start.7 = (bf16[192,640]{1,0:T(8,128)(2,1)S(1)}, bf16[192,640]{1,0:T(8,128)(2,1)S(1)}, u32[]{:S(2)}, u32[]{:S(2)}) collective-permute-start(bf16[192,640]{1,0:T(8,128)(2,1)S(1)} %collective-permute-done.6.refs_1_), channel_id=1, source_target_pairs={{0,8},{8,0},{16,24},{24,16},{1,9},{9,1},{17,25},{25,17},{2,10},{10... | collective-permute-start | bytes 737288 | tf_op jit(solution)/shard_map/ppermute | solution.py:221
  37.9 3.4 %all-to-all-start.1 = ((bf16[8,24,640]{2,1,0:T(8,128)(2,1)}), bf16[8,24,640]{2,1,0:T(8,128)(2,1)S(1)}, u32[]{:S(2)}, u32[]{:S(2)}) async-start(bf16[8,24,640]{2,1,0:T(8,128)(2,1)} %bitcast.2), calls=%async_computation.1 | async-start | bytes 491520 | tf_op jit(solution)/shard_map/all_to_all | solution.py:324
  41.3 0.4 collective-permute-start.11
  41.7 0.0 collective-permute-done.8.refs_1_
  41.7 0.2 collective-permute-start.12
  41.9 0.0 collective-permute-done.9.refs_2_
  41.9 0.3 collective-permute-start.13
  42.2 0.0 collective-permute-done.10.refs_3_
  42.2 0.2 collective-permute-start.14
  42.4 0.4 collective-permute-done.11.refs_4_
  42.8 0.3 collective-permute-done.12.refs_5_
  43.1 0.3 collective-permute-done.13.refs_6_
  43.4 0.3 collective-permute-done.14.refs_7_
  43.7 1.2 %early.1 = (bf16[768,1024]{1,0:T(8,128)(2,1)S(1)}, f32[640,1024]{1,0:T(8,128)S(1)}, f32[1,1024]{1,0:T(1,128)}) custom-call(bf16[192,512]{1,0:T(8,128)(2,1)S(1)} %parts.1.refs_0_, bf16[192,512]{1,0:T(8,128)(2,1)S(1)} %collective-permute-done.8.refs_1_, bf16[192,512]{1,0:T(8,128)(2,1)S(1)} %collective-permute-done.9.refs_2_, ...), custom_call_target="tpu_custom_call" | custom-call | flops 1 | bytes 1 | tf_op jit(solution)/shard_map/early/pallas_call | solution.py:326
  44.8 0.0 collective-permute-done.7.refs_2_
  44.8 2.5 %late.1 = f32[640,1024]{1,0:T(8,128)} custom-call(bf16[192,640]{1,0:T(8,128)(2,1)S(1)} %collective-permute-done.5.refs_0_, bf16[192,640]{1,0:T(8,128)(2,1)S(1)} %collective-permute-done.6.refs_1_, bf16[192,640]{1,0:T(8,128)(2,1)S(1)} %collective-permute-done.7.refs_2_, bf16[768,1024]{1,0:T(8,128)(2,1)S(1)} %get-tuple-element.40.refs_3_, ...), custom_call_target="tpu_custom_call" | custom-call | flops 1 | bytes 1 | tf_op jit(solution)/shard_map/late/pallas_call | solution.py:335
  47.3 0.6 %all-to-all-done.1 = bf16[8,24,640]{2,1,0:T(8,128)(2,1)S(1)} async-done(((bf16[8,24,640]{2,1,0:T(8,128)(2,1)}), bf16[8,24,640]{2,1,0:T(8,128)(2,1)S(1)}, u32[]{:S(2)}, u32[]{:S(2)}) %all-to-all-start.1) | async-done | bytes 245792 | tf_op jit(solution)/shard_map/all_to_all | solution.py:324
  48.0 0.7 %copy.10 = bf16[8,3,8,640]{3,2,0,1:T(8,128)(2,1)} copy(bf16[8,3,8,640]{3,2,1,0:T(8,128)(2,1)S(1)} %bitcast.8) | data formatting | bytes 491520 | tf_op jit(solution)/shard_map/reshape | solution.py:345
  (2 shorter events, 0.0 us)
Async XLA Ops:
  0.6 0.9 %copy-start = (bf16[24,5120]{1,0:T(8,128)(2,1)S(1)}, bf16[24,5120]{1,0:T(8,128)(2,1)}, u32[]{:S(2)}) copy-start(bf16[24,5120]{1,0:T(8,128)(2,1)} %pre.1) | copy-start | bytes 737284
  4.1 13.5 %collective-permute-start = (bf16[48,4096]{1,0:T(8,128)(2,1)S(1)}, bf16[48,4096]{1,0:T(8,128)(2,1)S(1)}, u32[]{:S(2)}, u32[]{:S(2)}) collective-permute-start(bf16[48,4096]{1,0:T(8,128)(2,1)S(1)} %get-tuple-element.25.mine), channel_id=1, source_target_pairs={{0,2},{1,5},{2,0},{3,7},{4,6},{5,1},{6,4},{7,3},{8,10},{9,13},{10,... | collective-permute-start | bytes 1179656 | tf_op jit(solution)/shard_map/ppermute | solution.py:230
  7.1 10.1 %all-to-all-start = ((bf16[8,24,640]{2,1,0:T(8,128)(2,1)}), bf16[8,24,640]{2,1,0:T(8,128)(2,1)S(1)}, u32[]{:S(2)}, u32[]{:S(2)}) async-start(bf16[8,24,640]{2,1,0:T(8,128)(2,1)} %cut.1), calls=%async_computation | async-start | bytes 491520 | tf_op jit(solution)/shard_map/all_to_all | solution.py:263
  10.5 7.1 %collective-permute-start.1 = (bf16[96,512]{1,0:T(8,128)(2,1)S(1)}, bf16[96,512]{1,0:T(8,128)(2,1)S(1)}, u32[]{:S(2)}, u32[]{:S(2)}) collective-permute-start(bf16[96,512]{1,0:T(8,128)(2,1)S(1)} %get-tuple-element.26), channel_id=1, source_target_pairs={{0,8},{8,0},{16,24},{24,16},{1,9},{9,1},{17,25},{25,17},{2,10},{10... | collective-permute-start | bytes 294920 | tf_op jit(solution)/shard_map/ppermute | solution.py:221
  17.6 10.8 %collective-permute-start.2 = (bf16[48,4096]{1,0:T(8,128)(2,1)S(1)}, bf16[48,4096]{1,0:T(8,128)(2,1)S(1)}, u32[]{:S(2)}, u32[]{:S(2)}) collective-permute-start(bf16[48,4096]{1,0:T(8,128)(2,1)S(1)} %collective-permute-done.one), channel_id=1, source_target_pairs={{0,1},{1,0},{2,3},{3,2},{4,5},{5,4},{6,7},{7,6},{8,9},{9,8},{10,11... | collective-permute-start | bytes 1179656 | tf_op jit(solution)/shard_map/ppermute | solution.py:221
  17.6 10.8 %collective-permute-start.3 = (bf16[48,4096]{1,0:T(8,128)(2,1)S(1)}, bf16[48,4096]{1,0:T(8,128)(2,1)S(1)}, u32[]{:S(2)}, u32[]{:S(2)}) collective-permute-start(bf16[48,4096]{1,0:T(8,128)(2,1)S(1)} %collective-permute-done.one), channel_id=1, source_target_pairs={{0,4},{1,3},{2,6},{3,1},{4,0},{5,7},{6,2},{7,5},{8,12},{9,11},{10,... | collective-permute-start | bytes 1179656 | tf_op jit(solution)/shard_map/ppermute | solution.py:230
  18.3 8.8 %collective-permute-start.4 = (bf16[96,512]{1,0:T(8,128)(2,1)S(1)}, bf16[96,512]{1,0:T(8,128)(2,1)S(1)}, u32[]{:S(2)}, u32[]{:S(2)}) collective-permute-start(bf16[96,512]{1,0:T(8,128)(2,1)S(1)} %pass_on.1), channel_id=1, source_target_pairs={{0,16},{8,24},{16,0},{24,8},{1,17},{9,25},{17,1},{25,9},{2,18},{10... | collective-permute-start | bytes 294920 | tf_op jit(solution)/shard_map/ppermute | solution.py:221
  20.9 13.4 %collective-permute-start.5 = (bf16[192,640]{1,0:T(8,128)(2,1)S(1)}, bf16[192,640]{1,0:T(8,128)(2,1)S(1)}, u32[]{:S(2)}, u32[]{:S(2)}) collective-permute-start(bf16[192,640]{1,0:T(8,128)(2,1)S(1)} %get-tuple-element.29.refs_8_), channel_id=1, source_target_pairs={{0,8},{8,0},{16,24},{24,16},{1,9},{9,1},{17,25},{25,17},{2,10},{10... | collective-permute-start | bytes 737288 | tf_op jit(solution)/shard_map/ppermute | solution.py:221
  22.5 14.7 %collective-permute-start.6 = (bf16[192,640]{1,0:T(8,128)(2,1)S(1)}, bf16[192,640]{1,0:T(8,128)(2,1)S(1)}, u32[]{:S(2)}, u32[]{:S(2)}) collective-permute-start(bf16[192,640]{1,0:T(8,128)(2,1)S(1)} %get-tuple-element.29.refs_8_), channel_id=1, source_target_pairs={{0,16},{8,24},{16,0},{24,8},{1,17},{9,25},{17,1},{25,9},{2,18},{10... | collective-permute-start | bytes 737288 | tf_op jit(solution)/shard_map/ppermute | solution.py:221
  27.0 14.6 %collective-permute-start.8 = (bf16[192,512]{1,0:T(8,128)(2,1)S(1)}, bf16[192,512]{1,0:T(8,128)(2,1)S(1)}, u32[]{:S(2)}, u32[]{:S(2)}) collective-permute-start(bf16[192,512]{1,0:T(8,128)(2,1)S(1)} %parts.1.refs_0_), channel_id=1, source_target_pairs={{0,2},{2,0},{4,6},{6,4},{1,3},{3,1},{5,7},{7,5},{8,10},{10,8},{12,... | collective-permute-start | bytes 589832 | tf_op jit(solution)/shard_map/ppermute | solution.py:221
  28.3 13.5 %collective-permute-start.9 = (bf16[192,512]{1,0:T(8,128)(2,1)S(1)}, bf16[192,512]{1,0:T(8,128)(2,1)S(1)}, u32[]{:S(2)}, u32[]{:S(2)}) collective-permute-start(bf16[192,512]{1,0:T(8,128)(2,1)S(1)} %parts.1.refs_0_), channel_id=1, source_target_pairs={{0,4},{2,6},{4,0},{6,2},{1,5},{3,7},{5,1},{7,3},{8,12},{10,14},{12... | collective-permute-start | bytes 589832 | tf_op jit(solution)/shard_map/ppermute | solution.py:221
  28.5 13.7 %collective-permute-start.10 = (bf16[192,512]{1,0:T(8,128)(2,1)S(1)}, bf16[192,512]{1,0:T(8,128)(2,1)S(1)}, u32[]{:S(2)}, u32[]{:S(2)}) collective-permute-start(bf16[192,512]{1,0:T(8,128)(2,1)S(1)} %parts.1.refs_0_), channel_id=1, source_target_pairs={{0,6},{2,4},{4,2},{6,0},{1,7},{3,5},{5,3},{7,1},{8,14},{10,12},{12... | collective-permute-start | bytes 589832 | tf_op jit(solution)/shard_map/ppermute | solution.py:221
  37.1 7.7 %collective-permute-start.7 = (bf16[192,640]{1,0:T(8,128)(2,1)S(1)}, bf16[192,640]{1,0:T(8,128)(2,1)S(1)}, u32[]{:S(2)}, u32[]{:S(2)}) collective-permute-start(bf16[192,640]{1,0:T(8,128)(2,1)S(1)} %collective-permute-done.6.refs_1_), channel_id=1, source_target_pairs={{0,8},{8,0},{16,24},{24,16},{1,9},{9,1},{17,25},{25,17},{2,10},{10... | collective-permute-start | bytes 737288 | tf_op jit(solution)/shard_map/ppermute | solution.py:221
  37.9 10.1 %all-to-all-start.1 = ((bf16[8,24,640]{2,1,0:T(8,128)(2,1)}), bf16[8,24,640]{2,1,0:T(8,128)(2,1)S(1)}, u32[]{:S(2)}, u32[]{:S(2)}) async-start(bf16[8,24,640]{2,1,0:T(8,128)(2,1)} %bitcast.2), calls=%async_computation.1 | async-start | bytes 491520 | tf_op jit(solution)/shard_map/all_to_all | solution.py:324
  41.3 1.5 %collective-permute-start.11 = (bf16[192,512]{1,0:T(8,128)(2,1)S(1)}, bf16[192,512]{1,0:T(8,128)(2,1)S(1)}, u32[]{:S(2)}, u32[]{:S(2)}) collective-permute-start(bf16[192,512]{1,0:T(8,128)(2,1)S(1)} %parts.1.refs_0_), channel_id=1, source_target_pairs={{0,1},{1,0},{2,3},{3,2},{4,5},{5,4},{6,7},{7,6},{8,9},{9,8},{10,11... | collective-permute-start | bytes 589832 | tf_op jit(solution)/shard_map/ppermute | solution.py:221
  41.7 1.4 %collective-permute-start.12 = (bf16[192,512]{1,0:T(8,128)(2,1)S(1)}, bf16[192,512]{1,0:T(8,128)(2,1)S(1)}, u32[]{:S(2)}, u32[]{:S(2)}) collective-permute-start(bf16[192,512]{1,0:T(8,128)(2,1)S(1)} %collective-permute-done.8.refs_1_), channel_id=1, source_target_pairs={{0,1},{1,0},{2,3},{3,2},{4,5},{5,4},{6,7},{7,6},{8,9},{9,8},{10,11... | collective-permute-start | bytes 589832 | tf_op jit(solution)/shard_map/ppermute | solution.py:221
  41.9 1.5 %collective-permute-start.13 = (bf16[192,512]{1,0:T(8,128)(2,1)S(1)}, bf16[192,512]{1,0:T(8,128)(2,1)S(1)}, u32[]{:S(2)}, u32[]{:S(2)}) collective-permute-start(bf16[192,512]{1,0:T(8,128)(2,1)S(1)} %collective-permute-done.9.refs_2_), channel_id=1, source_target_pairs={{0,1},{1,0},{2,3},{3,2},{4,5},{5,4},{6,7},{7,6},{8,9},{9,8},{10,11... | collective-permute-start | bytes 589832 | tf_op jit(solution)/shard_map/ppermute | solution.py:221
  42.2 1.5 %collective-permute-start.14 = (bf16[192,512]{1,0:T(8,128)(2,1)S(1)}, bf16[192,512]{1,0:T(8,128)(2,1)S(1)}, u32[]{:S(2)}, u32[]{:S(2)}) collective-permute-start(bf16[192,512]{1,0:T(8,128)(2,1)S(1)} %collective-permute-done.10.refs_3_), channel_id=1, source_target_pairs={{0,1},{1,0},{2,3},{3,2},{4,5},{5,4},{6,7},{7,6},{8,9},{9,8},{10,11... | collective-permute-start | bytes 589832 | tf_op jit(solution)/shard_map/ppermute | solution.py:221
